TPU v7x, 32 devices: a whole 2x2x4 slice. The times are simulated.
32 devices in a mesh: rowpt: 8 (over y, x, core), colpt: 4 (over z).
Axes of the slice: x: 2, y: 2, z: 4, core: 2. Of those that a mesh axis runs over, the one named last changes fastest.
Arguments:
- x_pairs: float32 [4, 1024, 1024], P(None, 'rowpt', 'colpt'), may hold values from -6 to 6
- eps_val: float32 [1024], P('rowpt'), may hold values from -2 to -0.5
- eps_con: float32 [1024], P('colpt'), may hold values from 0.5 to 2
- orb_val: float32 [8192, 1024], P(('rowpt', 'colpt')), may hold values from -0.35 to 0.35
- orb_con: float32 [8192, 1024], P(('rowpt', 'colpt')), may hold values from -0.35 to 0.35
- screened_w: float32 [8192, 8192], P('rowpt', 'colpt'), may hold values from -0.0625 to 0.0625
Outputs:
- hx: float32 [4, 1024, 1024], P(None, 'rowpt', 'colpt')
All inputs are finite; a program needn't handle non-finite values.
Results may differ from a plain program's by a relative error of at most 0.00005.
Values sent between devices are 32-bit elements; how exact they have to be, the bound alone decides.
No kernel may reach another device: no remote copies, remote signals or barrier semaphores. Data moves between devices by JAX's collectives and lax.ppermute only.
A program may use at most 64 MiB of HBM per device.

v0:
```python
import jax
import jax.numpy as jnp
from jax import lax
from jax.sharding import PartitionSpec as P

NP = 8192


def reorder_points(values, outer, inner):
    width = values.shape[1]
    shaped = values.reshape(outer, inner, -1, width)
    return jnp.transpose(shaped, (1, 0, 2, 3)).reshape(-1, width)


def per_device(x_pairs, eps_val, eps_con, orb_val, orb_con, screened_w):
    nrow = lax.axis_size("rowpt")
    ncol = lax.axis_size("colpt")
    val_part = lax.all_to_all(orb_val, "rowpt", split_axis=1, concat_axis=0, tiled=True)
    val_mixed = lax.all_gather(val_part, "colpt", axis=0, tiled=True)
    val_cols = reorder_points(val_mixed, ncol, nrow)
    con_part = lax.all_to_all(orb_con, "colpt", split_axis=1, concat_axis=0, tiled=True)
    con_cols = lax.all_gather(con_part, "rowpt", axis=0, tiled=True)
    block_pts = min(NP, 2048)
    nblocks = NP // block_pts
    vecs = x_pairs.shape[0]
    val_blocks = val_cols.reshape(nblocks, block_pts, val_cols.shape[1])
    con_blocks = con_cols.reshape(nblocks, block_pts, con_cols.shape[1])

    def density_block(pieces):
        val_piece, con_piece = pieces
        through = jnp.einsum("pc,bvc->bpv", con_piece, x_pairs, precision=lax.Precision.HIGHEST)
        return jnp.sum(through * val_piece[None], axis=2)

    partial_density = lax.map(density_block, (val_blocks, con_blocks))
    partial_density = jnp.transpose(partial_density, (1, 0, 2)).reshape(vecs, NP)
    column_share = lax.psum_scatter(partial_density, "colpt", scatter_dimension=1, tiled=True)
    density = lax.psum(column_share, "rowpt")
    screened_part = jnp.einsum("bq,pq->bp", density, screened_w, precision=lax.Precision.HIGHEST)
    row_total = lax.psum(screened_part, "colpt")
    screened = lax.all_gather(row_total, "rowpt", axis=1, tiled=True)
    pot_blocks = jnp.transpose(screened.reshape(vecs, nblocks, block_pts), (1, 0, 2))

    def kernel_block(total, pieces):
        val_piece, con_piece, pot_piece = pieces
        weighted = val_piece[None] * pot_piece[:, :, None]
        step = jnp.einsum("bpv,pc->bvc", weighted, con_piece, precision=lax.Precision.HIGHEST)
        return (total + step, None)

    start = jnp.zeros(x_pairs.shape, jnp.float32)
    kernel, unused = lax.scan(kernel_block, start, (val_blocks, con_blocks, pot_blocks))
    diff = eps_con[None, None, :] - eps_val[None, :, None]
    return diff * x_pairs + kernel


def solution(mesh):
    in_specs = (
        P(None, "rowpt", "colpt"),
        P("rowpt"),
        P("colpt"),
        P(("rowpt", "colpt"), None),
        P(("rowpt", "colpt"), None),
        P("rowpt", "colpt"),
    )
    out_specs = P(None, "rowpt", "colpt")
    return jax.shard_map(
        per_device, mesh=mesh, in_specs=in_specs, out_specs=out_specs, check_vma=False
    )
```

profile of v0, /device:TPU:0, one launch (start us, length us, event | category | flops | bytes accessed | tf_op | source)
XLA Modules:
  0.0 387.7 jit_solution(4577572689245964335)
XLA Ops:
  6.5 0.0 all-gather.3.cloned.1.call-start
  6.5 1.6 copy.27
  8.1 20.3 %all_to_all.38 = f32[256,8,128]{0,2,1:T(8,128)S(1)} all-to-all(f32[256,8,128]{0,2,1:T(8,128)S(1)} %bitcast.64), channel_id=1, replica_groups=mesh['rowpt'=8,'colpt'=4] {'rowpt'}, dimensions={1} | all-to-all | bytes 2097152 | tf_op jit(solution)/shard_map/all_to_all | solution.py:18
  28.4 1.4 copy.28
  29.8 0.0 all-gather.3.cloned.1.call-update
  29.8 0.0 all-gather.5.cloned.1.call-start
  29.9 1.6 copy.30
  31.4 0.3 copy.31
  31.8 57.7 %all_to_all.39 = f32[256,4,256]{2,0,1:T(8,128)} all-to-all(f32[256,4,256]{2,0,1:T(8,128)S(1)} %copy.31), channel_id=1, replica_groups=mesh['rowpt'=8,'colpt'=4] {'colpt'}, dimensions={1} | all-to-all | bytes 2097152 | tf_op jit(solution)/shard_map/all_to_all | solution.py:21
  89.5 0.0 all-gather.5.cloned.1.call-update
  89.5 0.0 reduce-scatter.4.cloned.1.call-start
  89.5 39.9 %all-gather.3.cloned.1.call-done = f32[8192,128]{1,0:T(8,128)} async-done(((f32[2048,128]{1,0:T(8,128)}), f32[8192,128]{1,0:T(8,128)}) %all-gather.3.cloned.1.call-update) | async-done | bytes 4194320 | tf_op jit(solution)/shard_map/all_gather | solution.py:19
  129.4 4.6 %copy.29 = f32[4,8,256,128]{3,2,0,1:T(8,128)} copy(f32[4,8,256,128]{3,2,1,0:T(8,128)} %bitcast.60) | data formatting | bytes 8388608 | tf_op jit(solution)/shard_map/reshape | solution.py:11
  134.0 0.0 copy-start
  134.0 5.6 %copy.34 = f32[4,2048,128]{1,2,0:T(8,128)} copy(f32[4,2048,128]{2,1,0:T(8,128)} %bitcast.59) | data formatting | bytes 8388608
  139.6 44.1 %all-gather.5.cloned.1.call-done = f32[8192,256]{1,0:T(8,128)} async-done(((f32[1024,256]{1,0:T(8,128)}), f32[8192,256]{1,0:T(8,128)}) %all-gather.5.cloned.1.call-update) | async-done | bytes 8388624 | tf_op jit(solution)/shard_map/all_gather | solution.py:22
  183.7 0.0 copy-done
  183.7 29.0 %while.21 = (s32[]{:T(128)}, f32[4,4,2048]{2,1,0:T(4,128)S(1)}, f32[4,2048,256]{2,1,0:T(8,128)}, f32[4,128,256]{2,1,0:T(8,128)S(1)}, f32[4,2048,128]{1,2,0:T(8,128)}, /*index=5*/s32[]{:T(128)}) while((s32[]{:T(128)}, f32[4,4,2048]{2,1,0:T(4,128)S(1)}, f32[4,2048,256]{2,1,0:T(8,128)}, f32[4,128,256]{2,1,0:T(8,128)S(1)}, ...), condition=%wide.region_2.3_spmd, body=%wide.region_0.2_spmd.sunk | while | flops 3223314432 | bytes 5866061 | solution.py:34
  183.7 1.3 dynamic-slice_bitcast_fusion.6
  185.0 5.9 %multiply_reduce_fusion.2 = f32[2048,4]{0,1:T(4,128)S(1)} fusion(f32[4,128,256]{2,1,0:T(8,128)S(1)} %get-tuple-element.216, f32[2048,128]{0,1:T(8,128)S(1)} %dynamic-slice_bitcast_fusion.6, f32[4,2048,256]{2,1,0:T(8,128)} %get-tuple-element.215, s32[]{:T(128)} %get-tuple-element.207), kind=kOutput, calls=%fused_computation.clone.1 | convolution fusion | flops 3223314432 | bytes 3703296 | tf_op jit(solution)/shard_map/while/body/eval_jaxpr/pc,bvc->bpv/dot_general | solution.py:31
  191.0 1.3 dynamic-slice_bitcast_fusion.6
  192.3 5.9 %multiply_reduce_fusion.2 = f32[2048,4]{0,1:T(4,128)S(1)} fusion(f32[4,128,256]{2,1,0:T(8,128)S(1)} %get-tuple-element.216, f32[2048,128]{0,1:T(8,128)S(1)} %dynamic-slice_bitcast_fusion.6, f32[4,2048,256]{2,1,0:T(8,128)} %get-tuple-element.215, s32[]{:T(128)} %get-tuple-element.207), kind=kOutput, calls=%fused_computation.clone.1 | convolution fusion | flops 3223314432 | bytes 3703296 | tf_op jit(solution)/shard_map/while/body/eval_jaxpr/pc,bvc->bpv/dot_general | solution.py:31
  198.2 1.3 dynamic-slice_bitcast_fusion.6
  199.5 5.9 %multiply_reduce_fusion.2 = f32[2048,4]{0,1:T(4,128)S(1)} fusion(f32[4,128,256]{2,1,0:T(8,128)S(1)} %get-tuple-element.216, f32[2048,128]{0,1:T(8,128)S(1)} %dynamic-slice_bitcast_fusion.6, f32[4,2048,256]{2,1,0:T(8,128)} %get-tuple-element.215, s32[]{:T(128)} %get-tuple-element.207), kind=kOutput, calls=%fused_computation.clone.1 | convolution fusion | flops 3223314432 | bytes 3703296 | tf_op jit(solution)/shard_map/while/body/eval_jaxpr/pc,bvc->bpv/dot_general | solution.py:31
  205.5 1.3 dynamic-slice_bitcast_fusion.6
  206.8 5.9 %multiply_reduce_fusion.2 = f32[2048,4]{0,1:T(4,128)S(1)} fusion(f32[4,128,256]{2,1,0:T(8,128)S(1)} %get-tuple-element.216, f32[2048,128]{0,1:T(8,128)S(1)} %dynamic-slice_bitcast_fusion.6, f32[4,2048,256]{2,1,0:T(8,128)} %get-tuple-element.215, s32[]{:T(128)} %get-tuple-element.207), kind=kOutput, calls=%fused_computation.clone.1 | convolution fusion | flops 3223314432 | bytes 3703296 | tf_op jit(solution)/shard_map/while/body/eval_jaxpr/pc,bvc->bpv/dot_general | solution.py:31
  212.7 0.0 copy-start.1
  212.7 0.0 copy-start.2
  212.7 2.6 copy.35
  215.4 0.0 reduce-scatter.4.cloned.1.call-update
  215.4 0.0 copy-done.1
  215.4 0.0 copy-done.2
  215.4 0.1 broadcast_subtract_fusion
  215.5 76.8 %reduce-scatter.4.cloned.1.call-done = f32[2048,4]{1,0:T(8,128)} async-done(((f32[8192,4]{1,0:T(8,128)}), f32[2048,4]{1,0:T(8,128)}) %reduce-scatter.4.cloned.1.call-update) | async-done | bytes 32784
  292.3 1.6 copy.36
  293.9 24.0 %psum.14 = f32[4,2048]{1,0:T(4,128)S(1)} all-reduce(f32[4,2048]{1,0:T(4,128)S(1)} %copy.36), channel_id=1, replica_groups=mesh['rowpt'=8,'colpt'=4] {'rowpt'}, use_global_device_ids=true, to_apply=%region_4.5 | all-reduce | flops 8192 | bytes 65536 | tf_op jit(solution)/shard_map/psum | solution.py:37
  317.9 9.2 %fusion.15 = f32[4,1024]{1,0:T(4,128)S(1)} fusion(f32[4,2048]{1,0:T(4,128)S(1)} %psum.14, f32[1024,2048]{1,0:T(8,128)} %param.15), kind=kOutput, calls=%fused_computation.18 | convolution fusion | flops 100663296 | bytes 8437760 | tf_op jit(solution)/shard_map/bq,pq->bp/dot_general | solution.py:38
  327.1 18.2 %psum.15 = f32[4,1024]{1,0:T(4,128)S(1)} all-reduce(f32[4,1024]{1,0:T(4,128)S(1)} %fusion.15), channel_id=1, replica_groups=mesh['rowpt'=8,'colpt'=4] {'colpt'}, use_global_device_ids=true, to_apply=%region_5.6 | all-reduce | flops 4096 | bytes 32768 | tf_op jit(solution)/shard_map/psum | solution.py:39
  345.3 8.4 %all_gather.11 = f32[4,8192]{1,0:T(4,128)S(1)} all-gather(f32[4,1024]{1,0:T(4,128)S(1)} %psum.15), channel_id=1, replica_groups=mesh['rowpt'=8,'colpt'=4] {'rowpt'}, dimensions={1}, use_global_device_ids=true | all-gather | bytes 147456 | tf_op jit(solution)/shard_map/all_gather | solution.py:40
  353.7 26.5 %while.22 = (s32[]{:T(128)}, f32[4,128,256]{2,1,0:T(8,128)S(1)}, f32[4,2048,128]{1,2,0:T(8,128)}, f32[4,4,2048]{2,1,0:T(4,128)S(1)}, f32[4,2048,256]{2,1,0:T(8,128)}, /*index=5*/s32[]{:T(128)}, s32[]{:T(128)}) while((s32[]{:T(128)}, f32[4,128,256]{2,1,0:T(8,128)S(1)}, f32[4,2048,128]{1,2,0:T(8,128)}, f32[4,4,2048]{2,1,0:T(4,128)S(1)}, ...), condition=%wide.region_7.8_spmd.clone, body=%wide.region_6.7_spmd.clone.sunk | while | flops 3222536192 | bytes 6390367 | solution.py:50
  353.7 1.3 dynamic-slice_bitcast_fusion.8
  355.0 5.3 %fusion.28 = f32[4,128,256]{2,1,0:T(8,128)S(1)} fusion(f32[4,2048,256]{2,1,0:T(8,128)} %get-tuple-element.237, s32[]{:T(128)} %get-tuple-element.226, f32[4,2048]{1,0:T(4,128)S(1)} %dynamic-slice_bitcast_fusion.7, f32[2048,128]{0,1:T(8,128)S(1)} %dynamic-slice_bitcast_fusion.8, f32[4,128,256]{2,1,0:T(8,128)S(1)} %get-tuple-element.227, pred[]{:T(512)S(6)} %compare.3), kind=kOutput, calls=%fused_computation.12.clone.1 | convolution fusion | flops 3222536192 | bytes 4227585 | tf_op jit(solution)/shard_map/while/body/eval_jaxpr/bpv,pc->bvc/dot_general | solution.py:46
  360.3 1.3 dynamic-slice_bitcast_fusion.8
  361.7 5.3 %fusion.28 = f32[4,128,256]{2,1,0:T(8,128)S(1)} fusion(f32[4,2048,256]{2,1,0:T(8,128)} %get-tuple-element.237, s32[]{:T(128)} %get-tuple-element.226, f32[4,2048]{1,0:T(4,128)S(1)} %dynamic-slice_bitcast_fusion.7, f32[2048,128]{0,1:T(8,128)S(1)} %dynamic-slice_bitcast_fusion.8, f32[4,128,256]{2,1,0:T(8,128)S(1)} %get-tuple-element.227, pred[]{:T(512)S(6)} %compare.3), kind=kOutput, calls=%fused_computation.12.clone.1 | convolution fusion | flops 3222536192 | bytes 4227585 | tf_op jit(solution)/shard_map/while/body/eval_jaxpr/bpv,pc->bvc/dot_general | solution.py:46
  367.0 1.3 dynamic-slice_bitcast_fusion.8
  368.3 5.3 %fusion.28 = f32[4,128,256]{2,1,0:T(8,128)S(1)} fusion(f32[4,2048,256]{2,1,0:T(8,128)} %get-tuple-element.237, s32[]{:T(128)} %get-tuple-element.226, f32[4,2048]{1,0:T(4,128)S(1)} %dynamic-slice_bitcast_fusion.7, f32[2048,128]{0,1:T(8,128)S(1)} %dynamic-slice_bitcast_fusion.8, f32[4,128,256]{2,1,0:T(8,128)S(1)} %get-tuple-element.227, pred[]{:T(512)S(6)} %compare.3), kind=kOutput, calls=%fused_computation.12.clone.1 | convolution fusion | flops 3222536192 | bytes 4227585 | tf_op jit(solution)/shard_map/while/body/eval_jaxpr/bpv,pc->bvc/dot_general | solution.py:46
  373.6 1.3 dynamic-slice_bitcast_fusion.8
  375.0 5.3 %fusion.28 = f32[4,128,256]{2,1,0:T(8,128)S(1)} fusion(f32[4,2048,256]{2,1,0:T(8,128)} %get-tuple-element.237, s32[]{:T(128)} %get-tuple-element.226, f32[4,2048]{1,0:T(4,128)S(1)} %dynamic-slice_bitcast_fusion.7, f32[2048,128]{0,1:T(8,128)S(1)} %dynamic-slice_bitcast_fusion.8, f32[4,128,256]{2,1,0:T(8,128)S(1)} %get-tuple-element.227, pred[]{:T(512)S(6)} %compare.3), kind=kOutput, calls=%fused_computation.12.clone.1 | convolution fusion | flops 3222536192 | bytes 4227585 | tf_op jit(solution)/shard_map/while/body/eval_jaxpr/bpv,pc->bvc/dot_general | solution.py:46
  380.3 0.9 multiply_add_fusion
  (10 shorter events, 0.1 us)
Async XLA Ops:
  6.5 122.9 %all-gather.3.cloned.1.call-start = ((), (), s32[]{:S(2)}) async-start(), calls=%async_computation.3 | async-start | bytes 5242880 | tf_op jit(solution)/shard_map/all_gather | solution.py:19
  29.8 153.9 %all-gather.5.cloned.1.call-start = ((), (), s32[]{:S(2)}) async-start(), calls=%async_computation.4 | async-start | bytes 9437184 | tf_op jit(solution)/shard_map/all_gather | solution.py:22
  89.5 202.8 %reduce-scatter.4.cloned.1.call-start = ((), (), s32[]{:S(2)}) async-start(), calls=%async_computation.5 | async-start | bytes 5242880
  134.0 49.7 %copy-start = (f32[4,128,256]{2,1,0:T(8,128)S(1)}, f32[4,128,256]{2,1,0:T(8,128)}, u32[]{:S(2)}) copy-start(f32[4,128,256]{2,1,0:T(8,128)} %param.10) | copy-start | bytes 1572868
  212.7 2.7 copy-start.1
  212.7 2.7 copy-start.2
Sparse Core Ops, SparseCore 0:
  30.0 99.4 all-gather.2
  131.3 52.3 all-gather.4
  215.5 76.7 reduce-scatter.3
where the time goes:
time: 389 us; the launch traced here: 388 us
  waiting for transfers between devices  161 us (41%)
  blocking collectives  129 us (33%)
  matrix products  53.9 us (14%)
  local copies, waits for them, and re-layouts  29.7 us (8%)
  between operations  13.2 us (3%)
    unnamed x4, waiting for transfers between devices  76.9 us
    all_to_all x1, blocking collectives, per_device(): lax.all_to_all(orb_con, 'colpt', split_axis=1, concat_axis=0, tiled=True)  57.7 us
    all_gather x1, waiting for transfers between devices, per_device(): con_cols = lax.all_gather(con_part, 'rowpt', axis=0, tiled=True)  44.1 us
    all_gather x1, waiting for transfers between devices, per_device(): val_mixed = lax.all_gather(val_part, 'colpt', axis=0, tiled=True)  39.9 us
    psum x1, blocking collectives, per_device(): density = lax.psum(column_share, 'rowpt')  24 us
    dot_general x4, matrix products, density_block(): jnp.einsum('pc,bvc->bpv', con_piece, x_pairs, precision=lax.Precision.HIG...  23.6 us
    dot_general x4, matrix products, kernel_block(): jnp.einsum('bpv,pc->bvc', weighted, con_piece, precision=lax.Precision.HI...  21.1 us
    all_to_all x1, blocking collectives, per_device(): lax.all_to_all(orb_val, 'rowpt', split_axis=1, concat_axis=0, tiled=True)  20.3 us
  transfers between devices with their start and end apart: 3, of which 3 were waited for; matrix products, arithmetic and copies ran while one was open for 3% of the time, Pallas kernels for 0%

commit v1 on v0

v1 whole, which is shorter than its diff:
```python
import jax
import jax.numpy as jnp
from jax import lax
from jax.sharding import Mesh, PartitionSpec as P

HIGH = lax.Precision.HIGH


def swap(x, axis, size, mask):
    return lax.ppermute(x, axis, [(i, i ^ mask) for i in range(size)])


def relative(x, axis, index):
    size = x.shape[axis]
    bit = 1
    while bit < size:
        shape = x.shape[:axis] + (size // (2 * bit), 2, bit) + x.shape[axis + 1:]
        flipped = jnp.flip(x.reshape(shape), axis + 1).reshape(x.shape)
        x = jnp.where((index & bit) != 0, flipped, x)
        bit *= 2
    return x


def make(nchip, ntop):
    def rc_swap(x, mask):
        return swap(x, "rc", nchip, mask)

    def top_swap(x, mask):
        return swap(x, "top", ntop, mask)

    def pair_swap(x):
        return swap(x, "pair", 2, 1)

    def core_swap(x):
        return swap(x, "core", 2, 1)

    def gather_chips(native):
        out = {0: native}
        half = native.shape[0] // 2
        for j in range(1, nchip):
            low = j & -j
            high = 1 << (j.bit_length() - 1)
            if low == high:
                out[j] = rc_swap(native, j)
            else:
                first = rc_swap(out[j ^ high][:half], high)
                second = rc_swap(out[j ^ low][half:], low)
                out[j] = jnp.concatenate([first, second], axis=0)
        return [out[j] for j in range(nchip)]

    def per_device(x_pairs, eps_val, eps_con, orb_val, orb_con, screened_w):
        rc = lax.axis_index("rc")
        core = lax.axis_index("core")
        top = lax.axis_index("top")
        pair = lax.axis_index("pair")
        nb, nv, nc = x_pairs.shape
        pts = orb_val.shape[0]

        parts = [x_pairs] + [top_swap(x_pairs, a) for a in range(1, ntop)]
        x_own = jnp.concatenate(parts, axis=2)
        x_other = core_swap(x_own)
        x_all = jnp.where(core == 0, jnp.stack([x_own, x_other], 1), jnp.stack([x_other, x_own], 1))
        x_all = x_all.reshape(nb * 2 * nv, ntop * nc)

        con = orb_con.reshape(pts, ntop, 2, nc)
        con_mine = jnp.where(pair == 0, con[:, :, 0], con[:, :, 1])
        con_theirs = jnp.where(pair == 0, con[:, :, 1], con[:, :, 0])
        con_mine = relative(con_mine, 1, top).reshape(pts, ntop * nc)
        con_theirs = relative(con_theirs, 1, top).reshape(pts, ntop * nc)
        con_next = pair_swap(con_theirs)
        con_blocks = [gather_chips(con_mine), gather_chips(con_next)]

        val_t = orb_val.T.reshape(nchip, 2 * nv, pts)
        val_here = []
        for j in range(nchip):
            piece = lax.dynamic_index_in_dim(val_t, rc ^ j, 0, keepdims=False)
            val_here.append(piece if j == 0 else rc_swap(piece, j))
        val_next = [pair_swap(piece) for piece in val_here]
        val_blocks = [val_here, val_next]

        dens = []
        for e in range(2):
            for j in range(nchip):
                through = lax.dot_general(
                    x_all, con_blocks[e][j], (((1,), (1,)), ((), ())), precision=HIGH
                ).reshape(nb, 2 * nv, pts)
                dens.append(jnp.sum(through * val_blocks[e][j][None], axis=1))
        dens = jnp.stack(dens, 0).reshape(2, nchip, nb, pts)

        by_rc = relative(dens, 1, rc).reshape(2, ntop, 2, nb, pts)
        by_pair = [
            jnp.where(pair == 0, by_rc[:, :, 0], by_rc[:, :, 1]),
            jnp.where(pair == 0, by_rc[:, :, 1], by_rc[:, :, 0]),
        ]
        total = by_pair[0]
        for a in range(1, nchip):
            total = total + rc_swap(by_pair[0], a)
        across = by_pair[1]
        sent = swap2(across, nchip)
        for piece in sent:
            total = total + piece[::-1]
        total = relative(total, 1, top)
        cols = [total[:, 0]] + [top_swap(total[:, a], a) for a in range(1, ntop)]
        cols = jnp.stack(cols, 0)
        cols = relative(relative(cols, 0, top), 1, pair)
        other = core_swap(cols)
        both = jnp.where(core == 0, jnp.stack([cols, other], 0), jnp.stack([other, cols], 0))
        density = jnp.transpose(both.reshape(-1, nb, pts), (1, 0, 2)).reshape(nb, -1)

        part = lax.dot_general(density, screened_w, (((1,), (1,)), ((), ())), precision=HIGH)
        part = jnp.transpose(part.reshape(nb, ntop, 2, pts), (1, 2, 0, 3))
        part = relative(relative(part, 0, top), 1, pair)
        row = part[0] + swap_pt(part[0], ntop, 0, True)[::-1]
        for a in range(1, ntop):
            row = row + swap_pt(part[a], ntop, a, False) + swap_pt(part[a], ntop, a, True)[::-1]
        pot = jnp.stack([row] + [rc_swap(row, j) for j in range(1, nchip)], 1)
        pot = jnp.transpose(pot, (2, 0, 1, 3)).reshape(nb, -1)

        val_all = jnp.concatenate(val_here + val_next, axis=1)
        con_all = jnp.concatenate(con_blocks[0] + con_blocks[1], axis=0)
        weighted = (val_all[None] * pot[:, None, :]).reshape(nb, 2, nv, -1)
        mine = jnp.where(core == 0, weighted[:, 0], weighted[:, 1]).reshape(nb * nv, -1)
        yours = jnp.where(core == 0, weighted[:, 1], weighted[:, 0]).reshape(nb * nv, -1)
        kernel = None
        for a in list(range(1, ntop)) + [0]:
            con_a = con_all[:, a * nc:(a + 1) * nc]
            away = core_swap(jnp.dot(yours, con_a, precision=HIGH))
            step = jnp.dot(mine, con_a, precision=HIGH) + away
            if a:
                step = top_swap(step, a)
            kernel = step if kernel is None else kernel + step
        diff = eps_con[None, None, :] - eps_val[None, :, None]
        return diff * x_pairs + kernel.reshape(nb, nv, nc)

    def swap2(x, n):
        return [
            lax.ppermute(x, ("rc", "pair"), [(r * 2 + p, (r ^ a) * 2 + (p ^ 1)) for r in range(n) for p in range(2)])
            for a in range(n)
        ]

    def swap_pt(x, n, a, flip):
        return lax.ppermute(
            x,
            ("top", "pair"),
            [(t * 2 + p, (t ^ a) * 2 + (p ^ int(flip))) for t in range(n) for p in range(2)],
        )

    return per_device


def solution(mesh):
    nrow, ncol = mesh.shape["rowpt"], mesh.shape["colpt"]
    nchip, ntop = nrow // 2, ncol // 2
    fine = Mesh(mesh.devices.reshape(nchip, 2, ntop, 2), ("rc", "core", "top", "pair"))
    row, col = ("rc", "core"), ("top", "pair")
    in_specs = (P(None, row, col), P(row), P(col), P(row + col, None), P(row + col, None), P(row, col))
    return jax.shard_map(
        make(nchip, ntop), mesh=fine, in_specs=in_specs, out_specs=P(None, row, col), check_vma=False
    )
```

time: 389 us -> 177 us (0.46)
  blocking collectives: 129 us -> 0 us
  waiting for transfers between devices: 161 us -> 69.6 us
  starting transfers between devices: 0.09 us -> 46 us
  matrix products: 53.9 us -> 28.4 us
  between operations: 13.2 us -> 0.62 us
  other arithmetic: 0.95 us -> 7.98 us
  local copies, waits for them, and re-layouts: 29.7 us -> 24 us
    all_gather x2 -> x0, waiting for transfers between devices: 84 us -> none  [the longest x1 44.1 us: per_device(): con_cols = lax.all_gather(con_part, 'rowpt', axis=0, tiled=True)]
    all_to_all x2 -> x0, blocking collectives: 78 us -> none  [the longest x1 57.7 us: per_device(): lax.all_to_all(orb_con, 'colpt', split_axis=1, concat_axis=0, tiled=True)]
    unnamed x4 -> x0, waiting for transfers between devices: 76.9 us -> none
    ppermute x0 -> x36, waiting for transfers between devices: none -> 69.6 us  [the longest x29 63.2 us: swap(): return lax.ppermute(x, axis, [(i, i ^ mask) for i in range(size)])]
    ppermute x0 -> x36, starting transfers between devices: none -> 46 us  [the longest x29 35.4 us: swap(): return lax.ppermute(x, axis, [(i, i ^ mask) for i in range(size)])]
    psum x2 -> x0, blocking collectives: 42.3 us -> none  [the longest x1 24 us: per_device(): density = lax.psum(column_share, 'rowpt')]
    dot_general x9 -> x13, matrix products: 53.9 us -> 28.4 us  [the longest x8 11.2 us: per_device(): lax.dot_general(x_all, con_blocks[e][j], (((1,), (1,)), ((), ())), precis...]
    mul x12 -> x1, local copies, waits for them, and re-layouts: 10.4 us -> 0.03 us  [per_device(): weighted = (val_all[None] * pot[:, None, :]).reshape(nb, 2, nv, -1)]
  transfers between devices with their start and end apart: 3 -> 36, of which waited for: 3 -> 16; matrix products, arithmetic and copies ran while one was open for 3% -> 24% of each run, Pallas kernels for 0% -> 0%
where the time goes in v1:
time: 177 us; the launch traced here: 176 us
  waiting for transfers between devices  69.6 us (39%)
  starting transfers between devices  46 us (26%)
  matrix products  28.4 us (16%)
  local copies, waits for them, and re-layouts  24 us (14%)
  other arithmetic  7.98 us (5%)
    ppermute x29, waiting for transfers between devices, swap(): return lax.ppermute(x, axis, [(i, i ^ mask) for i in range(size)])  63.2 us
    ppermute x29, starting transfers between devices, swap(): return lax.ppermute(x, axis, [(i, i ^ mask) for i in range(size)])  35.4 us
    dot_general x8, matrix products, per_device(): lax.dot_general(x_all, con_blocks[e][j], (((1,), (1,)), ((), ())), precis...  11.2 us
    unnamed x41, local copies, waits for them, and re-layouts  10.5 us
    dot_general x2, matrix products, per_device(): away = core_swap(jnp.dot(yours, con_a, precision=HIGH))  6.93 us
    dot_general x2, matrix products, per_device(): step = jnp.dot(mine, con_a, precision=HIGH) + away  6.92 us
    ppermute x4, starting transfers between devices, swap2(): lax.ppermute(x, ('rc', 'pair'), [(r * 2 + p, (r ^ a) * 2 + (p ^ 1)) for r...  5.85 us
    ppermute x3, starting transfers between devices, swap_pt(): lax.ppermute(x, ('top', 'pair'), [(t * 2 + p, (t ^ a) * 2 + (p ^ int(flip...  4.72 us
  transfers between devices with their start and end apart: 36, of which 16 were waited for; matrix products, arithmetic and copies ran while one was open for 24% of the time, Pallas kernels for 0%

profile of v1, /device:TPU:0, one launch (start us, length us, event | category | flops | bytes accessed | tf_op | source)
XLA Modules:
  0.0 176.5 jit_solution(17160697661345629188)
XLA Ops:
  0.0 2.1 %reshape.242 = f32[256,2,2,256]{3,2,1,0:T(2,128)S(1)} reshape(f32[256,1024]{1,0:T(8,128)} %param.10) | data formatting | bytes 2097152 | tf_op jit(solution)/shard_map/reshape | solution.py:65
  3.5 1.4 reverse.11
  5.0 1.1 constant_dynamic-update-slice_fusion.27
  6.1 2.9 %collective-permute-start.9 = (f32[256,512]{1,0:T(8,128)}, f32[256,512]{1,0:T(8,128)S(1)}, u32[]{:S(2)}, u32[]{:S(2)}) collective-permute-start(f32[256,512]{1,0:T(8,128)} %get-tuple-element.6), channel_id=1, source_target_pairs={{0,8},{8,0},{16,24},{24,16},{1,9},{9,1},{17,25},{25,17},{2,10},{10... | collective-permute-start | bytes 1572872 | tf_op jit(solution)/shard_map/ppermute | solution.py:10
  9.0 1.6 copy.15
  10.6 1.0 dynamic-slice_bitcast_fusion
  11.6 2.1 %collective-permute-start.1 = (f32[256,256]{1,0:T(8,128)}, f32[256,256]{1,0:T(8,128)}, u32[]{:S(2)}, u32[]{:S(2)}) collective-permute-start(f32[256,256]{1,0:T(8,128)} %get-tuple-element.12), channel_id=1, source_target_pairs={{0,16},{8,24},{16,0},{24,8},{1,17},{9,25},{17,1},{25,9},{2,18},{10... | collective-permute-start | bytes 786440 | tf_op jit(solution)/shard_map/ppermute | solution.py:10
  13.6 1.4 collective-permute-start.2
  15.1 2.6 %collective-permute-start.7 = (f32[4,128,256]{2,1,0:T(8,128)}, f32[4,128,256]{2,1,0:T(8,128)}, u32[]{:S(2)}, u32[]{:S(2)}) collective-permute-start(f32[4,128,256]{2,1,0:T(8,128)} %param.6), channel_id=1, source_target_pairs={{0,2},{2,0},{1,3},{3,1},{4,6},{6,4},{5,7},{7,5},{8,10},{10,8},{9,1... | collective-permute-start | bytes 1572872 | tf_op jit(solution)/shard_map/ppermute | solution.py:10
  17.7 1.1 broadcast_select_fusion.2
  18.7 1.6 reverse.12
  20.4 0.9 broadcast_select_fusion.3
  21.3 0.9 constant_dynamic-update-slice_fusion.9
  22.2 2.3 %reshape.257 = f32[256,512,1]{1,0,2:T(8,128)} reshape(f32[256,2,256]{2,1,0:T(2,128)} %broadcast_select_fusion.2) | data formatting | bytes 1048576 | tf_op jit(solution)/shard_map/jit(_where)/select_n | solution.py:19
  24.5 3.2 %collective-permute-done = f32[256,256]{1,0:T(8,128)} collective-permute-done((f32[256,256]{1,0:T(8,128)}, f32[256,256]{1,0:T(8,128)}, u32[]{:S(2)}, u32[]{:S(2)}) %collective-permute-start) | collective-permute-done | bytes 262176 | tf_op jit(solution)/shard_map/ppermute | solution.py:10
  27.7 2.1 %collective-permute-start.3 = (f32[256,256]{1,0:T(8,128)S(1)}, f32[256,256]{1,0:T(8,128)S(1)}, u32[]{:S(2)}, u32[]{:S(2)}) collective-permute-start(f32[256,256]{1,0:T(8,128)S(1)} %bitcast.162), channel_id=1, source_target_pairs={{0,1},{1,0},{2,3},{3,2},{4,5},{5,4},{6,7},{7,6},{8,9},{9,8},{10,11... | collective-permute-start | bytes 786440 | tf_op jit(solution)/shard_map/ppermute | solution.py:10
  29.9 1.0 constant_dynamic-update-slice_fusion.6
  30.8 1.6 collective-permute-start.10
  32.4 1.0 constant_dynamic-update-slice_fusion.5
  33.8 1.6 collective-permute-start.13
  35.4 4.8 %collective-permute-done.7 = f32[4,128,256]{2,1,0:T(8,128)} collective-permute-done((f32[4,128,256]{2,1,0:T(8,128)}, f32[4,128,256]{2,1,0:T(8,128)}, u32[]{:S(2)}, u32[]{:S(2)}) %collective-permute-start.7) | collective-permute-done | bytes 524320 | tf_op jit(solution)/shard_map/ppermute | solution.py:10
  40.8 1.9 %constant_dynamic-update-slice_fusion.8 = f32[4,128,512]{2,1,0:T(8,128)} fusion(f32[4,128,512]{2,1,0:T(8,128)} %constant_dynamic-update-slice_fusion.9, f32[4,128,256]{2,1,0:T(8,128)} %collective-permute-done.7), kind=kLoop, calls=%fused_computation.60 | loop fusion | bytes 1048576 | tf_op jit(solution)/shard_map/concatenate | solution.py:60
  42.7 3.1 %collective-permute-done.3 = f32[256,256]{1,0:T(8,128)S(1)} collective-permute-done((f32[256,256]{1,0:T(8,128)S(1)}, f32[256,256]{1,0:T(8,128)S(1)}, u32[]{:S(2)}, u32[]{:S(2)}) %collective-permute-start.3) | collective-permute-done | bytes 262176 | tf_op jit(solution)/shard_map/ppermute | solution.py:10
  45.7 1.0 constant_dynamic-update-slice_fusion.4
  46.8 15.7 %collective-permute-done.4 = f32[256,256]{1,0:T(8,128)S(1)} collective-permute-done((f32[256,256]{1,0:T(8,128)}, f32[256,256]{1,0:T(8,128)S(1)}, u32[]{:S(2)}, u32[]{:S(2)}) %collective-permute-start.4) | collective-permute-done | bytes 262176 | tf_op jit(solution)/shard_map/ppermute | solution.py:10
  62.6 0.9 constant_dynamic-update-slice_fusion.26
  63.5 1.5 collective-permute-start.11
  65.5 2.7 %collective-permute-done.5 = f32[256,256]{1,0:T(8,128)S(1)} collective-permute-done((f32[256,256]{1,0:T(8,128)}, f32[256,256]{1,0:T(8,128)S(1)}, u32[]{:S(2)}, u32[]{:S(2)}) %collective-permute-start.5) | collective-permute-done | bytes 262176 | tf_op jit(solution)/shard_map/ppermute | solution.py:10
  68.2 1.5 collective-permute-start.15
  69.8 2.8 %collective-permute-done.6 = f32[256,256]{1,0:T(8,128)S(1)} collective-permute-done((f32[256,256]{1,0:T(8,128)}, f32[256,256]{1,0:T(8,128)S(1)}, u32[]{:S(2)}, u32[]{:S(2)}) %collective-permute-start.6) | collective-permute-done | bytes 262176 | tf_op jit(solution)/shard_map/ppermute | solution.py:10
  72.6 1.4 collective-permute-start.12
  75.6 6.9 %collective-permute-done.12 = f32[128,512]{1,0:T(8,128)S(1)} collective-permute-done((f32[128,512]{1,0:T(8,128)S(1)}, f32[128,512]{1,0:T(8,128)S(1)}, u32[]{:S(2)}, u32[]{:S(2)}) %collective-permute-start.12) | collective-permute-done | bytes 262176 | tf_op jit(solution)/shard_map/ppermute | solution.py:10
  83.7 1.8 %collective-permute-start.17 = (f32[128,512]{1,0:T(8,128)S(1)}, f32[128,512]{1,0:T(8,128)S(1)}, u32[]{:S(2)}, u32[]{:S(2)}) collective-permute-start(f32[128,512]{1,0:T(8,128)S(1)} %slice.77), channel_id=1, source_target_pairs={{0,8},{8,0},{16,24},{24,16},{1,9},{9,1},{17,25},{25,17},{2,10},{10... | collective-permute-start | bytes 786440 | tf_op jit(solution)/shard_map/ppermute | solution.py:10
  85.9 1.0 fusion.8
  87.0 2.0 %fusion.9 = f32[4,256]{1,0:T(4,128)S(1)} fusion(f32[4,256,512]{2,1,0:T(8,128)S(1)} %bitcast.140, f32[256,512]{1,0:T(8,128)S(1)} %collective-permute-done.9, f32[256,256]{1,0:T(8,128)} %collective-permute-done), kind=kOutput, calls=%fused_computation.20 | convolution fusion | flops 805829632 | bytes 2887680 | tf_op jit(solution)/shard_map/dot_general | solution.py:84
  89.0 2.0 %fusion.10 = f32[4,256]{1,0:T(4,128)S(1)} fusion(f32[4,256,512]{2,1,0:T(8,128)S(1)} %bitcast.141, f32[256,512]{1,0:T(8,128)S(1)} %collective-permute-done.10, f32[256,256]{1,0:T(8,128)} %collective-permute-done.1), kind=kOutput, calls=%fused_computation.21 | convolution fusion | flops 805829632 | bytes 2887680 | tf_op jit(solution)/shard_map/dot_general | solution.py:84
  91.0 2.0 %fusion.11 = f32[4,256]{1,0:T(4,128)S(1)} fusion(f32[4,256,512]{2,1,0:T(8,128)S(1)} %bitcast.142, f32[128,512]{1,0:T(8,128)S(1)} %collective-permute-done.12, f32[128,512]{1,0:T(8,128)S(1)} %collective-permute-done.11, f32[256,256]{1,0:T(8,128)} %collective-permute-done.2), kind=kOutput, calls=%fused_computation.22 | convolution fusion | flops 805960704 | bytes 2887680 | tf_op jit(solution)/shard_map/dot_general | solution.py:84
  93.0 1.0 fusion.12
  94.0 1.0 fusion.13
  95.1 1.0 fusion.14
  96.2 1.0 multiply_reduce_fusion
  97.7 1.6 collective-permute-start.19
  100.1 1.6 collective-permute-start.20
  101.7 1.8 collective-permute-start.21
  103.5 2.7 %collective-permute-start.23 = (f32[2,2,4,256]{3,2,0,1:T(4,128)S(1)}, f32[2,2,4,256]{3,2,0,1:T(4,128)S(1)}, u32[]{:S(2)}, u32[]{:S(2)}) collective-permute-start(f32[2,2,4,256]{3,2,0,1:T(4,128)S(1)} %get-tuple-element.18), channel_id=1, source_target_pairs={{0,17},{1,16},{8,25},{9,24},{16,1},{17,0},{24,9},{25,8},{2,19},{3,... | collective-permute-start | bytes 49160 | tf_op jit(solution)/shard_map/ppermute | solution.py:137
  106.2 1.4 collective-permute-start.24
  108.4 3.3 %collective-permute-done.24 = f32[2,2,4,256]{3,2,0,1:T(4,128)S(1)} collective-permute-done((f32[2,2,4,256]{3,2,0,1:T(4,128)S(1)}, f32[2,2,4,256]{3,2,0,1:T(4,128)S(1)}, u32[]{:S(2)}, u32[]{:S(2)}) %collective-permute-start.24) | collective-permute-done | bytes 16416 | tf_op jit(solution)/shard_map/ppermute | solution.py:137
  111.8 3.9 %collective-permute-start.25 = (f32[2,4,256]{2,1,0:T(4,128)S(1)}, f32[2,4,256]{2,1,0:T(4,128)S(1)}, u32[]{:S(2)}, u32[]{:S(2)}) collective-permute-start(f32[2,4,256]{2,1,0:T(4,128)S(1)} %get-tuple-element.22), channel_id=1, source_target_pairs={{0,2},{2,0},{1,3},{3,1},{4,6},{6,4},{5,7},{7,5},{8,10},{10,8},{9,1... | collective-permute-start | bytes 24584 | tf_op jit(solution)/shard_map/ppermute | solution.py:10
  117.7 0.9 collective-permute-done.26
  118.7 3.4 %convolution_bitcast_fusion = f32[2,2,4,256]{3,2,1,0:T(4,128)S(1)} fusion(f32[4,2048,1,1]{1,0,3,2:T(4,128)S(1)} %bitcast.179, f32[2,2,256,2048]{3,2,1,0:T(8,128)S(1)} %bitcast.155), kind=kOutput, calls=%fused_computation.28 | convolution fusion | flops 50331648 | bytes 8437760 | tf_op jit(solution)/shard_map/dot_general | solution.py:110
  122.1 3.0 %collective-permute-start.28 = (f32[2,4,256]{2,1,0:T(4,128)S(1)}, f32[2,4,256]{2,1,0:T(4,128)S(1)}, u32[]{:S(2)}, u32[]{:S(2)}) collective-permute-start(f32[2,4,256]{2,1,0:T(4,128)S(1)} %get-tuple-element.20), channel_id=1, source_target_pairs={{0,2},{1,3},{2,0},{3,1},{4,6},{5,7},{6,4},{7,5},{8,10},{9,11},{10,... | collective-permute-start | bytes 24584 | tf_op jit(solution)/shard_map/ppermute | solution.py:142
  125.1 1.3 collective-permute-start.29
  127.5 2.5 %collective-permute-done.27 = f32[2,4,256]{2,1,0:T(4,128)S(1)} collective-permute-done((f32[2,4,256]{2,1,0:T(4,128)S(1)}, f32[2,4,256]{2,1,0:T(4,128)S(1)}, u32[]{:S(2)}, u32[]{:S(2)}) %collective-permute-start.27) | collective-permute-done | bytes 8224 | tf_op jit(solution)/shard_map/ppermute | solution.py:142
  131.6 2.4 %collective-permute-start.32 = (f32[2,4,256]{2,1,0:T(4,128)S(1)}, f32[2,4,256]{2,1,0:T(4,128)S(1)}, u32[]{:S(2)}, u32[]{:S(2)}) collective-permute-start(f32[2,4,256]{2,1,0:T(4,128)S(1)} %reverse_add_fusion.1), channel_id=1, source_target_pairs={{0,24},{8,16},{16,8},{24,0},{1,25},{9,17},{17,9},{25,1},{2,26},{10... | collective-permute-start | bytes 24584 | tf_op jit(solution)/shard_map/ppermute | solution.py:10
  134.8 1.4 collective-permute-done.32
  136.3 1.0 broadcast_multiply_fusion
  137.3 1.7 slice_select_fusion.1
  139.0 3.5 %fusion.4 = f32[512,256]{1,0:T(8,128)S(1)} fusion(f32[512,2048]{1,0:T(8,128)S(1)} %bitcast.149, f32[2048,512]{1,0:T(8,128)} %constant_dynamic-update-slice_fusion.18), kind=kOutput, calls=%fused_computation.8 | convolution fusion | flops 1610612736 | bytes 6815744 | tf_op jit(solution)/shard_map/dot_general | solution.py:127
  142.5 3.5 %fusion = f32[512,256]{1,0:T(8,128)S(1)} fusion(f32[512,2048]{1,0:T(8,128)S(1)} %bitcast.150, f32[2048,512]{1,0:T(8,128)} %constant_dynamic-update-slice_fusion.18), kind=kOutput, calls=%fused_computation.4 | convolution fusion | flops 1610612736 | bytes 6815744 | tf_op jit(solution)/shard_map/dot_general | solution.py:127
  146.6 3.5 %fusion.15 = f32[512,256]{1,0:T(8,128)S(1)} fusion(f32[512,256]{1,0:T(8,128)S(1)} %collective-permute-done.33, f32[512,2048]{1,0:T(8,128)S(1)} %bitcast.147, f32[2048,512]{1,0:T(8,128)} %constant_dynamic-update-slice_fusion.18), kind=kOutput, calls=%fused_computation.26 | convolution fusion | flops 1610743808 | bytes 7340032 | tf_op jit(solution)/shard_map/dot_general | solution.py:128
  150.0 1.5 collective-permute-start.34
  151.7 3.5 %fusion.18 = f32[512,256]{1,0:T(8,128)S(1)} fusion(f32[512,256]{1,0:T(8,128)S(1)} %collective-permute-done.35, f32[512,2048]{1,0:T(8,128)S(1)} %bitcast.148, f32[2048,512]{1,0:T(8,128)} %constant_dynamic-update-slice_fusion.18), kind=kOutput, calls=%fused_computation.27 | convolution fusion | flops 1610743808 | bytes 7340032 | tf_op jit(solution)/shard_map/dot_general | solution.py:128
  155.2 20.4 %collective-permute-done.34 = f32[512,256]{1,0:T(8,128)S(1)} collective-permute-done((f32[512,256]{1,0:T(8,128)S(1)}, f32[512,256]{1,0:T(8,128)S(1)}, u32[]{:S(2)}, u32[]{:S(2)}) %collective-permute-start.34) | collective-permute-done | bytes 524320 | tf_op jit(solution)/shard_map/ppermute | solution.py:10
  175.6 0.9 multiply_add_fusion
  (107 shorter events, 15.1 us)
Async XLA Ops:
  6.1 40.6 %collective-permute-start.9 = (f32[256,512]{1,0:T(8,128)}, f32[256,512]{1,0:T(8,128)S(1)}, u32[]{:S(2)}, u32[]{:S(2)}) collective-permute-start(f32[256,512]{1,0:T(8,128)} %get-tuple-element.6), channel_id=1, source_target_pairs={{0,8},{8,0},{16,24},{24,16},{1,9},{9,1},{17,25},{25,17},{2,10},{10... | collective-permute-start | bytes 1572872 | tf_op jit(solution)/shard_map/ppermute | solution.py:10
  11.6 9.7 %copy-start.1 = (f32[4,128,256]{2,1,0:T(8,128)S(1)}, f32[4,128,256]{2,1,0:T(8,128)}, u32[]{:S(2)}) copy-start(f32[4,128,256]{2,1,0:T(8,128)} %param.6) | copy-start | bytes 1572868
  11.6 16.1 %collective-permute-start = (f32[256,256]{1,0:T(8,128)}, f32[256,256]{1,0:T(8,128)}, u32[]{:S(2)}, u32[]{:S(2)}) collective-permute-start(f32[256,256]{1,0:T(8,128)} %get-tuple-element.13), channel_id=1, source_target_pairs={{0,8},{8,0},{16,24},{24,16},{1,9},{9,1},{17,25},{25,17},{2,10},{10... | collective-permute-start | bytes 786440 | tf_op jit(solution)/shard_map/ppermute | solution.py:10
  11.6 19.3 %collective-permute-start.1 = (f32[256,256]{1,0:T(8,128)}, f32[256,256]{1,0:T(8,128)}, u32[]{:S(2)}, u32[]{:S(2)}) collective-permute-start(f32[256,256]{1,0:T(8,128)} %get-tuple-element.12), channel_id=1, source_target_pairs={{0,16},{8,24},{16,0},{24,8},{1,17},{9,25},{17,1},{25,9},{2,18},{10... | collective-permute-start | bytes 786440 | tf_op jit(solution)/shard_map/ppermute | solution.py:10
  13.6 20.2 %collective-permute-start.2 = (f32[256,256]{1,0:T(8,128)}, f32[256,256]{1,0:T(8,128)}, u32[]{:S(2)}, u32[]{:S(2)}) collective-permute-start(f32[256,256]{1,0:T(8,128)} %get-tuple-element.11), channel_id=1, source_target_pairs={{0,24},{8,16},{16,8},{24,0},{1,25},{9,17},{17,9},{25,1},{2,26},{10... | collective-permute-start | bytes 786440 | tf_op jit(solution)/shard_map/ppermute | solution.py:10
  15.1 25.1 %collective-permute-start.7 = (f32[4,128,256]{2,1,0:T(8,128)}, f32[4,128,256]{2,1,0:T(8,128)}, u32[]{:S(2)}, u32[]{:S(2)}) collective-permute-start(f32[4,128,256]{2,1,0:T(8,128)} %param.6), channel_id=1, source_target_pairs={{0,2},{2,0},{1,3},{3,1},{4,6},{6,4},{5,7},{7,5},{8,10},{10,8},{9,1... | collective-permute-start | bytes 1572872 | tf_op jit(solution)/shard_map/ppermute | solution.py:10
  27.7 18.0 %collective-permute-start.3 = (f32[256,256]{1,0:T(8,128)S(1)}, f32[256,256]{1,0:T(8,128)S(1)}, u32[]{:S(2)}, u32[]{:S(2)}) collective-permute-start(f32[256,256]{1,0:T(8,128)S(1)} %bitcast.162), channel_id=1, source_target_pairs={{0,1},{1,0},{2,3},{3,2},{4,5},{5,4},{6,7},{7,6},{8,9},{9,8},{10,11... | collective-permute-start | bytes 786440 | tf_op jit(solution)/shard_map/ppermute | solution.py:10
  30.8 32.7 %collective-permute-start.10 = (f32[256,512]{1,0:T(8,128)}, f32[256,512]{1,0:T(8,128)S(1)}, u32[]{:S(2)}, u32[]{:S(2)}) collective-permute-start(f32[256,512]{1,0:T(8,128)} %get-tuple-element.6), channel_id=1, source_target_pairs={{0,16},{8,24},{16,0},{24,8},{1,17},{9,25},{17,1},{25,9},{2,18},{10... | collective-permute-start | bytes 1572872 | tf_op jit(solution)/shard_map/ppermute | solution.py:10
  33.8 31.2 %collective-permute-start.13 = (f32[256,512]{1,0:T(8,128)}, f32[256,512]{1,0:T(8,128)S(1)}, u32[]{:S(2)}, u32[]{:S(2)}) collective-permute-start(f32[256,512]{1,0:T(8,128)} %broadcast_select_fusion.3), channel_id=1, source_target_pairs={{0,1},{1,0},{2,3},{3,2},{4,5},{5,4},{6,7},{7,6},{8,9},{9,8},{10,11... | collective-permute-start | bytes 1572872 | tf_op jit(solution)/shard_map/ppermute | solution.py:10
  40.2 22.4 %collective-permute-start.4 = (f32[256,256]{1,0:T(8,128)}, f32[256,256]{1,0:T(8,128)S(1)}, u32[]{:S(2)}, u32[]{:S(2)}) collective-permute-start(f32[256,256]{1,0:T(8,128)} %collective-permute-done), channel_id=1, source_target_pairs={{0,1},{1,0},{2,3},{3,2},{4,5},{5,4},{6,7},{7,6},{8,9},{9,8},{10,11... | collective-permute-start | bytes 786440 | tf_op jit(solution)/shard_map/ppermute | solution.py:10
  42.7 42.9 %copy-start = (f32[4,128,512]{2,1,0:T(8,128)S(1)}, f32[4,128,512]{2,1,0:T(8,128)}, u32[]{:S(2)}) copy-start(f32[4,128,512]{2,1,0:T(8,128)} %constant_dynamic-update-slice_fusion.8) | copy-start | bytes 3145732
  45.7 39.8 %collective-permute-start.8 = (f32[4,128,512]{2,1,0:T(8,128)}, f32[4,128,512]{2,1,0:T(8,128)S(1)}, u32[]{:S(2)}, u32[]{:S(2)}) collective-permute-start(f32[4,128,512]{2,1,0:T(8,128)} %constant_dynamic-update-slice_fusion.8), channel_id=1, source_target_pairs={{0,4},{4,0},{1,5},{5,1},{2,6},{6,2},{3,7},{7,3},{8,12},{12,8},{9,1... | collective-permute-start | bytes 3145736 | tf_op jit(solution)/shard_map/ppermute | solution.py:10
  46.7 21.5 %collective-permute-start.5 = (f32[256,256]{1,0:T(8,128)}, f32[256,256]{1,0:T(8,128)S(1)}, u32[]{:S(2)}, u32[]{:S(2)}) collective-permute-start(f32[256,256]{1,0:T(8,128)} %collective-permute-done.1), channel_id=1, source_target_pairs={{0,1},{1,0},{2,3},{3,2},{4,5},{5,4},{6,7},{7,6},{8,9},{9,8},{10,11... | collective-permute-start | bytes 786440 | tf_op jit(solution)/shard_map/ppermute | solution.py:10
  62.6 10.0 %collective-permute-start.6 = (f32[256,256]{1,0:T(8,128)}, f32[256,256]{1,0:T(8,128)S(1)}, u32[]{:S(2)}, u32[]{:S(2)}) collective-permute-start(f32[256,256]{1,0:T(8,128)} %collective-permute-done.2), channel_id=1, source_target_pairs={{0,1},{1,0},{2,3},{3,2},{4,5},{5,4},{6,7},{7,6},{8,9},{9,8},{10,11... | collective-permute-start | bytes 786440 | tf_op jit(solution)/shard_map/ppermute | solution.py:10
  63.5 11.3 %collective-permute-start.11 = (f32[128,512]{1,0:T(8,128)S(1)}, f32[128,512]{1,0:T(8,128)S(1)}, u32[]{:S(2)}, u32[]{:S(2)}) collective-permute-start(f32[128,512]{1,0:T(8,128)S(1)} %slice.74), channel_id=1, source_target_pairs={{0,16},{8,24},{16,0},{24,8},{1,17},{9,25},{17,1},{25,9},{2,18},{10... | collective-permute-start | bytes 786440 | tf_op jit(solution)/shard_map/ppermute | solution.py:10
  65.0 18.1 %collective-permute-start.14 = (f32[256,512]{1,0:T(8,128)S(1)}, f32[256,512]{1,0:T(8,128)S(1)}, u32[]{:S(2)}, u32[]{:S(2)}) collective-permute-start(f32[256,512]{1,0:T(8,128)S(1)} %collective-permute-done.13), channel_id=1, source_target_pairs={{0,8},{8,0},{16,24},{24,16},{1,9},{9,1},{17,25},{25,17},{2,10},{10... | collective-permute-start | bytes 1572872 | tf_op jit(solution)/shard_map/ppermute | solution.py:10
  68.2 15.5 %collective-permute-start.15 = (f32[256,512]{1,0:T(8,128)S(1)}, f32[256,512]{1,0:T(8,128)S(1)}, u32[]{:S(2)}, u32[]{:S(2)}) collective-permute-start(f32[256,512]{1,0:T(8,128)S(1)} %collective-permute-done.13), channel_id=1, source_target_pairs={{0,16},{8,24},{16,0},{24,8},{1,17},{9,25},{17,1},{25,9},{2,18},{10... | collective-permute-start | bytes 1572872 | tf_op jit(solution)/shard_map/ppermute | solution.py:10
  69.8 16.1 %copy-start.2 = (f32[256,512,1]{1,0,2:T(8,128)S(1)}, f32[256,512,1]{1,0,2:T(8,128)}, u32[]{:S(2)}) copy-start(f32[256,512,1]{1,0,2:T(8,128)} %reshape.257) | copy-start | bytes 1572868
  72.6 9.9 %collective-permute-start.12 = (f32[128,512]{1,0:T(8,128)S(1)}, f32[128,512]{1,0:T(8,128)S(1)}, u32[]{:S(2)}, u32[]{:S(2)}) collective-permute-start(f32[128,512]{1,0:T(8,128)S(1)} %slice.75), channel_id=1, source_target_pairs={{0,8},{8,0},{16,24},{24,16},{1,9},{9,1},{17,25},{25,17},{2,10},{10... | collective-permute-start | bytes 786440 | tf_op jit(solution)/shard_map/ppermute | solution.py:10
  83.2 13.0 %collective-permute-start.16 = (f32[128,512]{1,0:T(8,128)S(1)}, f32[128,512]{1,0:T(8,128)S(1)}, u32[]{:S(2)}, u32[]{:S(2)}) collective-permute-start(f32[128,512]{1,0:T(8,128)S(1)} %slice.76), channel_id=1, source_target_pairs={{0,16},{8,24},{16,0},{24,8},{1,17},{9,25},{17,1},{25,9},{2,18},{10... | collective-permute-start | bytes 786440 | tf_op jit(solution)/shard_map/ppermute | solution.py:10
  83.7 12.5 %collective-permute-start.17 = (f32[128,512]{1,0:T(8,128)S(1)}, f32[128,512]{1,0:T(8,128)S(1)}, u32[]{:S(2)}, u32[]{:S(2)}) collective-permute-start(f32[128,512]{1,0:T(8,128)S(1)} %slice.77), channel_id=1, source_target_pairs={{0,8},{8,0},{16,24},{24,16},{1,9},{9,1},{17,25},{25,17},{2,10},{10... | collective-permute-start | bytes 786440 | tf_op jit(solution)/shard_map/ppermute | solution.py:10
  93.0 25.7 %slice-start = ((s8[8388608]{0:T(1024)(128)(4,1)}), s8[4194304]{0:T(1024)(128)(4,1)S(1)}, s32[]{:S(2)}) async-start(s8[8388608]{0:T(1024)(128)(4,1)} %bitcast.153), calls=%async_computation | async-start | bytes 8388608
  95.1 23.6 %slice-start.1 = ((s8[8388608]{0:T(1024)(128)(4,1)}), s8[4194304]{0:T(1024)(128)(4,1)S(1)}, s32[]{:S(2)}) async-start(s8[8388608]{0:T(1024)(128)(4,1)} %bitcast.153), calls=%async_computation.1 | async-start | bytes 8388608
  97.3 6.2 %collective-permute-start.18 = (f32[2,2,4,256]{3,2,0,1:T(4,128)S(1)}, f32[2,2,4,256]{3,2,0,1:T(4,128)S(1)}, u32[]{:S(2)}, u32[]{:S(2)}) collective-permute-start(f32[2,2,4,256]{3,2,0,1:T(4,128)S(1)} %get-tuple-element.17), channel_id=1, source_target_pairs={{0,8},{8,0},{16,24},{24,16},{1,9},{9,1},{17,25},{25,17},{2,10},{10... | collective-permute-start | bytes 49160 | tf_op jit(solution)/shard_map/ppermute | solution.py:10
  97.7 8.6 %collective-permute-start.19 = (f32[2,2,4,256]{3,2,0,1:T(4,128)S(1)}, f32[2,2,4,256]{3,2,0,1:T(4,128)S(1)}, u32[]{:S(2)}, u32[]{:S(2)}) collective-permute-start(f32[2,2,4,256]{3,2,0,1:T(4,128)S(1)} %get-tuple-element.17), channel_id=1, source_target_pairs={{0,16},{8,24},{16,0},{24,8},{1,17},{9,25},{17,1},{25,9},{2,18},{10... | collective-permute-start | bytes 49160 | tf_op jit(solution)/shard_map/ppermute | solution.py:10
  100.1 8.3 %collective-permute-start.20 = (f32[2,2,4,256]{3,2,0,1:T(4,128)S(1)}, f32[2,2,4,256]{3,2,0,1:T(4,128)S(1)}, u32[]{:S(2)}, u32[]{:S(2)}) collective-permute-start(f32[2,2,4,256]{3,2,0,1:T(4,128)S(1)} %get-tuple-element.17), channel_id=1, source_target_pairs={{0,24},{8,16},{16,8},{24,0},{1,25},{9,17},{17,9},{25,1},{2,26},{10... | collective-permute-start | bytes 49160 | tf_op jit(solution)/shard_map/ppermute | solution.py:10
  101.7 6.7 %collective-permute-start.21 = (f32[2,2,4,256]{3,2,0,1:T(4,128)S(1)}, f32[2,2,4,256]{3,2,0,1:T(4,128)S(1)}, u32[]{:S(2)}, u32[]{:S(2)}) collective-permute-start(f32[2,2,4,256]{3,2,0,1:T(4,128)S(1)} %get-tuple-element.18), channel_id=1, source_target_pairs={{0,1},{1,0},{8,9},{9,8},{16,17},{17,16},{24,25},{25,24},{2,3},{3,2... | collective-permute-start | bytes 49160 | tf_op jit(solution)/shard_map/ppermute | solution.py:137
  103.5 4.9 %collective-permute-start.22 = (f32[2,2,4,256]{3,2,0,1:T(4,128)S(1)}, f32[2,2,4,256]{3,2,0,1:T(4,128)S(1)}, u32[]{:S(2)}, u32[]{:S(2)}) collective-permute-start(f32[2,2,4,256]{3,2,0,1:T(4,128)S(1)} %get-tuple-element.18), channel_id=1, source_target_pairs={{0,9},{1,8},{8,1},{9,0},{16,25},{17,24},{24,17},{25,16},{2,11},{3,... | collective-permute-start | bytes 49160 | tf_op jit(solution)/shard_map/ppermute | solution.py:137
  103.5 4.9 %collective-permute-start.23 = (f32[2,2,4,256]{3,2,0,1:T(4,128)S(1)}, f32[2,2,4,256]{3,2,0,1:T(4,128)S(1)}, u32[]{:S(2)}, u32[]{:S(2)}) collective-permute-start(f32[2,2,4,256]{3,2,0,1:T(4,128)S(1)} %get-tuple-element.18), channel_id=1, source_target_pairs={{0,17},{1,16},{8,25},{9,24},{16,1},{17,0},{24,9},{25,8},{2,19},{3,... | collective-permute-start | bytes 49160 | tf_op jit(solution)/shard_map/ppermute | solution.py:137
  106.2 5.5 %collective-permute-start.24 = (f32[2,2,4,256]{3,2,0,1:T(4,128)S(1)}, f32[2,2,4,256]{3,2,0,1:T(4,128)S(1)}, u32[]{:S(2)}, u32[]{:S(2)}) collective-permute-start(f32[2,2,4,256]{3,2,0,1:T(4,128)S(1)} %get-tuple-element.18), channel_id=1, source_target_pairs={{0,25},{1,24},{8,17},{9,16},{16,9},{17,8},{24,1},{25,0},{2,27},{3,... | collective-permute-start | bytes 49160 | tf_op jit(solution)/shard_map/ppermute | solution.py:137
  111.8 5.5 %collective-permute-start.25 = (f32[2,4,256]{2,1,0:T(4,128)S(1)}, f32[2,4,256]{2,1,0:T(4,128)S(1)}, u32[]{:S(2)}, u32[]{:S(2)}) collective-permute-start(f32[2,4,256]{2,1,0:T(4,128)S(1)} %get-tuple-element.22), channel_id=1, source_target_pairs={{0,2},{2,0},{1,3},{3,1},{4,6},{6,4},{5,7},{7,5},{8,10},{10,8},{9,1... | collective-permute-start | bytes 24584 | tf_op jit(solution)/shard_map/ppermute | solution.py:10
  117.4 1.2 collective-permute-start.26
  122.1 7.9 %collective-permute-start.28 = (f32[2,4,256]{2,1,0:T(4,128)S(1)}, f32[2,4,256]{2,1,0:T(4,128)S(1)}, u32[]{:S(2)}, u32[]{:S(2)}) collective-permute-start(f32[2,4,256]{2,1,0:T(4,128)S(1)} %get-tuple-element.20), channel_id=1, source_target_pairs={{0,2},{1,3},{2,0},{3,1},{4,6},{5,7},{6,4},{7,5},{8,10},{9,11},{10,... | collective-permute-start | bytes 24584 | tf_op jit(solution)/shard_map/ppermute | solution.py:142
  125.1 5.4 %collective-permute-start.29 = (f32[2,4,256]{2,1,0:T(4,128)S(1)}, f32[2,4,256]{2,1,0:T(4,128)S(1)}, u32[]{:S(2)}, u32[]{:S(2)}) collective-permute-start(f32[2,4,256]{2,1,0:T(4,128)S(1)} %get-tuple-element.20), channel_id=1, source_target_pairs={{0,3},{1,2},{2,1},{3,0},{4,7},{5,6},{6,5},{7,4},{8,11},{9,10},{10,... | collective-permute-start | bytes 24584 | tf_op jit(solution)/shard_map/ppermute | solution.py:142
  126.3 3.7 %collective-permute-start.27 = (f32[2,4,256]{2,1,0:T(4,128)S(1)}, f32[2,4,256]{2,1,0:T(4,128)S(1)}, u32[]{:S(2)}, u32[]{:S(2)}) collective-permute-start(f32[2,4,256]{2,1,0:T(4,128)S(1)} %get-tuple-element.19), channel_id=1, source_target_pairs={{0,1},{1,0},{2,3},{3,2},{4,5},{5,4},{6,7},{7,6},{8,9},{9,8},{10,11... | collective-permute-start | bytes 24584 | tf_op jit(solution)/shard_map/ppermute | solution.py:142
  130.5 4.2 %collective-permute-start.30 = (f32[2,4,256]{2,1,0:T(4,128)S(1)}, f32[2,4,256]{2,1,0:T(4,128)S(1)}, u32[]{:S(2)}, u32[]{:S(2)}) collective-permute-start(f32[2,4,256]{2,1,0:T(4,128)S(1)} %reverse_add_fusion.1), channel_id=1, source_target_pairs={{0,8},{8,0},{16,24},{24,16},{1,9},{9,1},{17,25},{25,17},{2,10},{10... | collective-permute-start | bytes 24584 | tf_op jit(solution)/shard_map/ppermute | solution.py:10
  131.1 3.7 %collective-permute-start.31 = (f32[2,4,256]{2,1,0:T(4,128)S(1)}, f32[2,4,256]{2,1,0:T(4,128)S(1)}, u32[]{:S(2)}, u32[]{:S(2)}) collective-permute-start(f32[2,4,256]{2,1,0:T(4,128)S(1)} %reverse_add_fusion.1), channel_id=1, source_target_pairs={{0,16},{8,24},{16,0},{24,8},{1,17},{9,25},{17,1},{25,9},{2,18},{10... | collective-permute-start | bytes 24584 | tf_op jit(solution)/shard_map/ppermute | solution.py:10
  131.6 4.5 %collective-permute-start.32 = (f32[2,4,256]{2,1,0:T(4,128)S(1)}, f32[2,4,256]{2,1,0:T(4,128)S(1)}, u32[]{:S(2)}, u32[]{:S(2)}) collective-permute-start(f32[2,4,256]{2,1,0:T(4,128)S(1)} %reverse_add_fusion.1), channel_id=1, source_target_pairs={{0,24},{8,16},{16,8},{24,0},{1,25},{9,17},{17,9},{25,1},{2,26},{10... | collective-permute-start | bytes 24584 | tf_op jit(solution)/shard_map/ppermute | solution.py:10
  142.4 4.1 %collective-permute-start.33 = (f32[512,256]{1,0:T(8,128)S(1)}, f32[512,256]{1,0:T(8,128)S(1)}, u32[]{:S(2)}, u32[]{:S(2)}) collective-permute-start(f32[512,256]{1,0:T(8,128)S(1)} %fusion.4), channel_id=1, source_target_pairs={{0,4},{4,0},{1,5},{5,1},{2,6},{6,2},{3,7},{7,3},{8,12},{12,8},{9,1... | collective-permute-start | bytes 1572872 | tf_op jit(solution)/shard_map/ppermute | solution.py:10
  146.0 5.6 %copy-start.3 = (f32[256]{0:T(256)S(1)}, f32[256]{0:T(256)}, u32[]{:S(2)}) copy-start(f32[256]{0:T(256)} %param.8) | copy-start | bytes 3076
  146.0 5.6 %copy-start.4 = (f32[128]{0:T(128)S(1)}, f32[128]{0:T(128)}, u32[]{:S(2)}) copy-start(f32[128]{0:T(128)} %param.7) | copy-start | bytes 1540
  146.0 5.7 %collective-permute-start.35 = (f32[512,256]{1,0:T(8,128)S(1)}, f32[512,256]{1,0:T(8,128)S(1)}, u32[]{:S(2)}, u32[]{:S(2)}) collective-permute-start(f32[512,256]{1,0:T(8,128)S(1)} %fusion), channel_id=1, source_target_pairs={{0,4},{4,0},{1,5},{5,1},{2,6},{6,2},{3,7},{7,3},{8,12},{12,8},{9,1... | collective-permute-start | bytes 1572872 | tf_op jit(solution)/shard_map/ppermute | solution.py:10
  150.0 25.5 %collective-permute-start.34 = (f32[512,256]{1,0:T(8,128)S(1)}, f32[512,256]{1,0:T(8,128)S(1)}, u32[]{:S(2)}, u32[]{:S(2)}) collective-permute-start(f32[512,256]{1,0:T(8,128)S(1)} %fusion.15), channel_id=1, source_target_pairs={{0,2},{2,0},{1,3},{3,1},{4,6},{6,4},{5,7},{7,5},{8,10},{10,8},{9,1... | collective-permute-start | bytes 1572872 | tf_op jit(solution)/shard_map/ppermute | solution.py:10

commit v2 on v1

v2 whole, which is shorter than its diff:
```python
import functools

import jax
import jax.numpy as jnp
from jax import lax
from jax.experimental import pallas as pl
from jax.experimental.pallas import tpu as pltpu
from jax.sharding import Mesh, PartitionSpec as P

HIGH = lax.Precision.HIGH
VMEM = pl.BlockSpec(memory_space=pltpu.VMEM)
SMEM = pl.BlockSpec(memory_space=pltpu.SMEM)
PARAMS = pltpu.CompilerParams(vmem_limit_bytes=14 * 1024 * 1024)


def swap(x, axis, size, mask):
    return lax.ppermute(x, axis, [(i, i ^ mask) for i in range(size)])


def relative(x, axis, index):
    size = x.shape[axis]
    bit = 1
    while bit < size:
        shape = x.shape[:axis] + (size // (2 * bit), 2, bit) + x.shape[axis + 1:]
        flipped = jnp.flip(x.reshape(shape), axis + 1).reshape(x.shape)
        x = jnp.where((index & bit) != 0, flipped, x)
        bit *= 2
    return x


def single(j):
    return j & (j - 1) == 0


def split(x):
    high = x.astype(jnp.bfloat16)
    return high, (x - high.astype(jnp.float32)).astype(jnp.bfloat16)


def pack_kernel(nchip, ntop, where, con_ref, val_ref, pair_ref, *outs):
    pts, nc = pair_ref.shape[1:]
    rc, top, pair = where[0], where[1], where[2]

    def con_tile(a, e):
        at = ((top ^ a) * 2 + (pair ^ e)) * nc
        return con_ref[:, pl.ds(pl.multiple_of(at, nc), nc)]

    def val_tile(j):
        at = (rc ^ j) * nc
        return val_ref[:, pl.ds(pl.multiple_of(at, nc), nc)].T

    for a in range(ntop):
        pair_ref[a] = con_tile(a, 1)
    pair_ref[ntop] = val_tile(0)
    for j in range(1, nchip):
        out = outs[j - 1]
        if single(j):
            for a in range(ntop):
                out[a] = con_tile(a, 0)
        out[out.shape[0] - 1] = val_tile(j)


def pack(nchip, ntop, aligned, rc, top, pair, orb_con, orb_val, nc):
    pts = orb_con.shape[0]
    if aligned:
        sizes = [ntop + 1] + [ntop + 1 if single(j) else 1 for j in range(1, nchip)]
        return pl.pallas_call(
            functools.partial(pack_kernel, nchip, ntop),
            out_shape=[jax.ShapeDtypeStruct((s, pts, nc), jnp.float32) for s in sizes],
            in_specs=[SMEM, VMEM, VMEM],
            out_specs=[VMEM] * nchip,
            compiler_params=PARAMS,
        )(jnp.stack([rc, top, pair]).astype(jnp.int32), orb_con, orb_val)

    def con_tile(a, e):
        return lax.dynamic_slice_in_dim(orb_con, ((top ^ a) * 2 + (pair ^ e)) * nc, nc, 1)

    def val_tile(j):
        return lax.dynamic_slice_in_dim(orb_val, (rc ^ j) * nc, nc, 1).T.reshape(pts, nc)

    out = [jnp.stack([con_tile(a, 1) for a in range(ntop)] + [val_tile(0)])]
    for j in range(1, nchip):
        con = [con_tile(a, 0) for a in range(ntop)] if single(j) else []
        out.append(jnp.stack(con + [val_tile(j)]))
    return out


def operands(tiles):
    arrays, at = [], []
    for array, index in tiles:
        where = [i for i, other in enumerate(arrays) if other is array]
        if not where:
            arrays.append(array)
            where = [len(arrays) - 1]
        at.append((where[0], index))
    return arrays, at


def density_kernel(nblk, ntop, nin, con_at, val_at, core_ref, *refs):
    x = refs[:2 * ntop]
    tiles = refs[2 * ntop:2 * ntop + nin]
    dens_ref = refs[2 * ntop + nin]
    keep = refs[2 * ntop + nin + 1:-2]
    left, right = refs[-2:]
    nb, nv, nc = x[0].shape
    core = core_ref[0]
    for a in range(ntop):
        for k in range(2):
            high, low = split(x[a * 2 + k][...].reshape(nb * nv, nc))
            rows = pl.ds(k * nb * nv, nb * nv)
            left[rows, pl.ds(a * nc, nc)] = high
            left[rows, pl.ds((ntop + a) * nc, nc)] = high
            left[rows, pl.ds((2 * ntop + a) * nc, nc)] = low
    for g in range(nblk):
        for a in range(ntop):
            array, index = con_at[g * ntop + a]
            high, low = split(tiles[array][index])
            keep[g][a, 0] = high
            keep[g][a, 1] = low
            right[g, :, pl.ds(a * nc, nc)] = high
            right[g, :, pl.ds((ntop + a) * nc, nc)] = low
            right[g, :, pl.ds((2 * ntop + a) * nc, nc)] = high
        through = lax.dot_general(
            left[...], right[g], (((1,), (1,)), ((), ())), preferred_element_type=jnp.float32
        )
        pts = through.shape[1]
        array, index = val_at[g]
        total = None
        for k in range(2):
            rows = tiles[array][index, pl.ds(pl.multiple_of((core ^ k) * nv, nv), nv), :]
            part = through[k * nb * nv:(k + 1) * nb * nv].reshape(nb, nv, pts) * rows[None]
            part = jnp.sum(part, axis=1)
            total = part if total is None else total + part
        dens_ref[g] = total


def densities(aligned, core, x, con, val):
    nblk, ntop = len(con), len(x)
    nb, nv, nc = x[0][0].shape
    if aligned:
        arrays, at = operands([t for row in con for t in row] + list(val))
        pts = arrays[0].shape[1]
        outs = pl.pallas_call(
            functools.partial(density_kernel, nblk, ntop, len(arrays), at[:nblk * ntop], at[nblk * ntop:]),
            out_shape=[jax.ShapeDtypeStruct((nblk, nb, pts), jnp.float32)]
            + [jax.ShapeDtypeStruct((ntop, 2, pts, nc), jnp.bfloat16)] * nblk,
            in_specs=[SMEM] + [VMEM] * (2 * ntop + len(arrays)),
            out_specs=[VMEM] * (nblk + 1),
            scratch_shapes=[
                pltpu.VMEM((2 * nb * nv, 3 * ntop * nc), jnp.bfloat16),
                pltpu.VMEM((nblk, pts, 3 * ntop * nc), jnp.bfloat16),
            ],
            compiler_params=PARAMS,
            cost_estimate=pl.CostEstimate(
                flops=2 * nblk * 2 * nb * nv * pts * 3 * ntop * nc, bytes_accessed=nblk * 2 ** 20, transcendentals=0
            ),
        )(core.astype(jnp.int32)[None], *[t for row in x for t in row], *arrays)
        return [outs[0][g] for g in range(nblk)], list(outs[1:])
    tiles = [jnp.where(core == 0, jnp.stack(row, 1), jnp.stack(row[::-1], 1)) for row in x]
    con = [[array[index] for array, index in row] for row in con]
    out = []
    for g in range(nblk):
        through = 0.0
        for a in range(ntop):
            through = through + jnp.einsum("bkvc,pc->bkvp", tiles[a], con[g][a], precision=HIGH)
        array, index = val[g]
        out.append(jnp.sum(through * array[index].reshape(1, 2, nv, -1), axis=(1, 2)))
    return out, con


def apply_kernel(nblk, nin, a, k, val_at, core_ref, pot_ref, *refs):
    val = refs[:nin]
    con = refs[nin:nin + nblk]
    out_ref, left, right = refs[nin + nblk:]
    nb, nv, nc = out_ref.shape
    pts = con[0].shape[2]
    core = core_ref[0]
    for g in range(nblk):
        array, index = val_at[g]
        rows = val[array][index, pl.ds(pl.multiple_of((core ^ k) * nv, nv), nv), :]
        for b in range(nb):
            high, low = split(rows * pot_ref[g, pl.ds(b, 1), :])
            at = pl.ds(b * nv, nv)
            left[at, pl.ds(3 * g * pts, pts)] = high
            left[at, pl.ds((3 * g + 1) * pts, pts)] = high
            left[at, pl.ds((3 * g + 2) * pts, pts)] = low
        right[pl.ds(3 * g * pts, pts), :] = con[g][a, 0]
        right[pl.ds((3 * g + 1) * pts, pts), :] = con[g][a, 1]
        right[pl.ds((3 * g + 2) * pts, pts), :] = con[g][a, 0]
    total = jnp.dot(left[...], right[...], preferred_element_type=jnp.float32)
    out_ref[...] = total.reshape(nb, nv, nc)


def applied(aligned, core, pot, val, con, a, k, shape):
    nb, nv, nc = shape
    nblk = len(val)
    if aligned:
        pts = pot.shape[2]
        arrays, at = operands(val)
        return pl.pallas_call(
            functools.partial(apply_kernel, nblk, len(arrays), a, k, at),
            out_shape=jax.ShapeDtypeStruct(shape, jnp.float32),
            in_specs=[SMEM] + [VMEM] * (1 + len(arrays) + nblk),
            out_specs=VMEM,
            scratch_shapes=[
                pltpu.VMEM((nb * nv, 3 * nblk * pts), jnp.bfloat16),
                pltpu.VMEM((3 * nblk * pts, nc), jnp.bfloat16),
            ],
            compiler_params=PARAMS,
            cost_estimate=pl.CostEstimate(
                flops=2 * nb * nv * 3 * nblk * pts * nc, bytes_accessed=4 * 2 ** 20, transcendentals=0
            ),
        )(core.astype(jnp.int32)[None], pot, *arrays, *con)
    out = 0.0
    for g in range(nblk):
        array, index = val[g]
        rows = lax.dynamic_slice_in_dim(array[index].reshape(2 * nv, -1), (core ^ k) * nv, nv, 0)
        out = out + jnp.einsum("vp,bp,pc->bvc", rows, pot[g], con[g][a], precision=HIGH)
    return out


def make(nchip, ntop):
    def rc_swap(x, mask):
        return swap(x, "rc", nchip, mask)

    def top_swap(x, mask):
        return swap(x, "top", ntop, mask)

    def pair_swap(x):
        return swap(x, "pair", 2, 1)

    def core_swap(x):
        return swap(x, "core", 2, 1)

    def col_swap(x, mask):
        n = 2 * ntop
        return lax.ppermute(x, ("top", "pair"), [(i, i ^ mask) for i in range(n)])

    def relay(tiles, j):
        high = 1 << (j.bit_length() - 1)
        low = j & -j
        out = []
        for a in range(ntop):
            mask = low if a % 2 else high
            array, index = tiles[j ^ mask][a]
            out.append((rc_swap(array[index:index + 1], mask), 0))
        return out

    def per_device(x_pairs, eps_val, eps_con, orb_val, orb_con, screened_w):
        rc = lax.axis_index("rc")
        core = lax.axis_index("core")
        top = lax.axis_index("top")
        pair = lax.axis_index("pair")
        nb, nv, nc = x_pairs.shape
        pts = orb_val.shape[0]
        aligned = nc % 128 == 0 and pts == nc and 2 * nv == nc

        packed = pack(nchip, ntop, aligned, rc, top, pair, orb_con, orb_val, nc)
        from_pair = pair_swap(packed[0])
        from_chip = {j: rc_swap(packed[j], j) for j in range(1, nchip)}
        x_tops = [x_pairs] + [top_swap(x_pairs, a) for a in range(1, ntop)]
        x_tops = lax.optimization_barrier(x_tops)
        x = [[t, core_swap(t)] for t in x_tops]

        val = [{0: (packed[0], ntop)}, {0: (from_pair, ntop)}]
        con = [{0: [(packed[1], a) for a in range(ntop)]}, {0: [(from_pair, a) for a in range(ntop)]}]
        for j in range(1, nchip):
            val[0][j] = (from_chip[j], from_chip[j].shape[0] - 1)
            if single(j):
                con[0][j] = [(from_chip[j], a) for a in range(ntop)]

        def take(tiles):
            return jnp.stack([array[index] for array, index in tiles])

        if nchip == 4:
            con[0][3] = [None] * ntop
            for mask in (2, 1):
                mine = [a for a in range(ntop) if (a % 2 == 0) == (mask == 2)]
                got = rc_swap(take([con[0][3 ^ mask][a] for a in mine] + con[1][0]), mask)
                for i, a in enumerate(mine):
                    con[0][3][a] = (got, i)
                con[1][mask] = [(got, len(mine) + a) for a in range(ntop)]
        else:
            for j in range(1, nchip):
                if single(j):
                    got = rc_swap(take(con[1][0]), j)
                    con[1][j] = [(got, a) for a in range(ntop)]
        val_pair = pair_swap(take([val[0][j] for j in range(1, nchip)]))
        for j in range(1, nchip):
            val[1][j] = (val_pair, j - 1)
        for e in range(2):
            for j in range(1, nchip):
                if j not in con[e]:
                    con[e][j] = relay(con[e], j)

        groups = [
            [(0, 0)] + [(0, j) for j in range(1, nchip) if single(j)] + [(1, 0)],
            [(0, j) for j in range(1, nchip) if not single(j)] + [(1, j) for j in range(1, nchip) if single(j)],
            [(1, j) for j in range(1, nchip) if not single(j)],
        ]
        dens, kept = {}, {}
        for group in groups:
            if group:
                d, kc = densities(aligned, core, x, [con[e][j] for e, j in group], [val[e][j] for e, j in group])
                dens.update(zip(group, d))
                kept.update(zip(group, kc))
        order = [(e, j) for e in range(2) for j in range(nchip)]
        part = jnp.stack([dens[at] for at in order], 0).reshape(2, nchip, nb, pts)

        part = relative(relative(part, 1, rc ^ (top * 2 + pair)), 0, pair)
        got = [part[:, 0]] + [col_swap(part[:, d], d) for d in range(1, nchip)]
        part = jnp.stack([got[2 * d] + got[2 * d + 1] for d in range(ntop)])
        part = relative(part, 0, top)
        total = part
        for a in range(1, nchip):
            total = total + rc_swap(part, a)
        other = core_swap(total)
        both = jnp.where(core == 0, jnp.stack([total, other]), jnp.stack([other, total]))
        density = jnp.transpose(both.reshape(-1, nb, pts), (1, 0, 2)).reshape(nb, -1)

        rows = lax.dot_general(density, screened_w, (((1,), (1,)), ((), ())), precision=HIGH)
        rows = jnp.transpose(rows.reshape(nb, ntop, 2, pts), (1, 2, 0, 3))
        rows = relative(rows, 0, top)
        row = rows[0]
        for d in range(1, nchip):
            row = row + col_swap(rows[d // 2], d)
        row = relative(row, 0, pair)
        pot = jnp.stack([row] + [rc_swap(row, j) for j in range(1, nchip)], 1).reshape(2 * nchip, nb, pts)

        vals = [val[e][j] for e, j in order]
        cons = [kept[at] for at in order]
        kernel = None
        for a in list(range(1, ntop)) + [0]:
            away = core_swap(applied(aligned, core, pot, vals, cons, a, 1, x_pairs.shape))
            step = applied(aligned, core, pot, vals, cons, a, 0, x_pairs.shape) + away
            if a:
                step, pot = lax.optimization_barrier((step, pot))
                step = top_swap(step, a)
            kernel = step if kernel is None else kernel + step
        diff = eps_con[None, None, :] - eps_val[None, :, None]
        return diff * x_pairs + kernel

    return per_device


def solution(mesh):
    nrow, ncol = mesh.shape["rowpt"], mesh.shape["colpt"]
    nchip, ntop = nrow // 2, ncol // 2
    fine = Mesh(mesh.devices.reshape(nchip, 2, ntop, 2), ("rc", "core", "top", "pair"))
    row, col = ("rc", "core"), ("top", "pair")
    in_specs = (P(None, row, col), P(row), P(col), P(row + col, None), P(row + col, None), P(row, col))
    return jax.shard_map(
        make(nchip, ntop), mesh=fine, in_specs=in_specs, out_specs=P(None, row, col), check_vma=False
    )
```

time: 177 us -> 143 us (0.81)
  matrix products: 28.4 us -> 7.03 us
  Pallas kernels: 0 us -> 20.2 us
  starting transfers between devices: 46 us -> 30.2 us
  local copies, waits for them, and re-layouts: 24 us -> 12 us
  other arithmetic: 7.98 us -> 3.61 us
    dot_general x12 -> x0, matrix products: 25 us -> none  [the longest x8 11.2 us: per_device(): lax.dot_general(x_all, con_blocks[e][j], (((1,), (1,)), ((), ())), precis...]
    pallas_call x0 -> x8, Pallas kernels: none -> 20.2 us  [the longest x3 11.8 us: densities(): pl.pallas_call(functools.partial(density_kernel, nblk, ntop, len(arrays),...]
    ppermute x29 -> x22, starting transfers between devices: 35.4 us -> 21.2 us  [swap(): return lax.ppermute(x, axis, [(i, i ^ mask) for i in range(size)])]
    dot_general x1, matrix products: 3.35 us -> 7.03 us  [per_device(): lax.dot_general(density, screened_w, (((1,), (1,)), ((), ())), precision=...]
    another operation x5 -> x2, local copies, waits for them, and re-layouts: 3.01 us -> 0.01 us  [the longest x1 0.01 us: per_device(): part = jnp.stack([dens[at] for at in order], 0).reshape(2, nchip, nb, pts)]
    concatenate x3 -> x0, local copies, waits for them, and re-layouts: 2.64 us -> none  [the longest x1 1.9 us: per_device(): x_own = jnp.concatenate(parts, axis=2)]
    select_n x5 -> x1, other arithmetic: 2.54 us -> 0.01 us  [per_device(): jnp.where(core == 0, jnp.stack([total, other]), jnp.stack([other, total]))]
    another operation x1 -> x8, other arithmetic: 0.01 us -> 2.41 us  [the longest x2 2.31 us: take(): return jnp.stack([array[index] for array, index in tiles])]
  transfers between devices with their start and end apart: 36 -> 28, of which waited for: 16 -> 16; matrix products, arithmetic and copies ran while one was open for 24% -> 3% of each run, Pallas kernels for 0% -> 9%
where the time goes in v2:
time: 143 us
  waiting for transfers between devices  69.5 us (49%)
  starting transfers between devices  30.2 us (21%)
  Pallas kernels  20.2 us (14%)
  local copies, waits for them, and re-layouts  12 us (8%)
  matrix products  7.03 us (5%)
  other arithmetic  3.61 us (3%)
    ppermute x22, waiting for transfers between devices, swap(): return lax.ppermute(x, axis, [(i, i ^ mask) for i in range(size)])  62.5 us
    ppermute x22, starting transfers between devices, swap(): return lax.ppermute(x, axis, [(i, i ^ mask) for i in range(size)])  21.2 us
    pallas_call x3, Pallas kernels, densities(): pl.pallas_call(functools.partial(density_kernel, nblk, ntop, len(arrays),...  11.8 us
    unnamed x60, local copies, waits for them, and re-layouts  9.89 us
    ppermute x6, starting transfers between devices, col_swap(): return lax.ppermute(x, ('top', 'pair'), [(i, i ^ mask) for i in range(n)])  8.95 us
    pallas_call x4, Pallas kernels, applied(): pl.pallas_call(functools.partial(apply_kernel, nblk, len(arrays), a, k, a...  7.44 us
    ppermute x6, waiting for transfers between devices, col_swap(): return lax.ppermute(x, ('top', 'pair'), [(i, i ^ mask) for i in range(n)])  7.06 us
    dot_general x1, matrix products, per_device(): lax.dot_general(density, screened_w, (((1,), (1,)), ((), ())), precision=...  7.03 us
  transfers between devices with their start and end apart: 28, of which 16 were waited for; matrix products, arithmetic and copies ran while one was open for 3% of the time, Pallas kernels for 9%

profile of v2, /device:TPU:0, one launch (start us, length us, event | category | flops | bytes accessed | tf_op | source)
XLA Modules:
  0.0 143.0 jit_solution(1221045504311349415)
XLA Ops:
  0.1 1.2 copy-done.22
  1.3 1.2 copy-done.23
  2.5 0.9 shard_map.64
  3.5 3.0 %collective-permute-start.3 = (f32[3,256,256]{2,1,0:T(8,128)S(1)}, f32[3,256,256]{2,1,0:T(8,128)S(1)}, u32[]{:S(2)}, u32[]{:S(2)}) collective-permute-start(f32[3,256,256]{2,1,0:T(8,128)S(1)} %get-tuple-element.26.refs_4_), channel_id=1, source_target_pairs={{0,8},{8,0},{16,24},{24,16},{1,9},{9,1},{17,25},{25,17},{2,10},{10... | collective-permute-start | bytes 2359304 | tf_op jit(solution)/shard_map/ppermute | solution.py:17
  6.5 1.5 %collective-permute-start.4 = (f32[3,256,256]{2,1,0:T(8,128)S(1)}, f32[3,256,256]{2,1,0:T(8,128)S(1)}, u32[]{:S(2)}, u32[]{:S(2)}) collective-permute-start(f32[3,256,256]{2,1,0:T(8,128)S(1)} %get-tuple-element.27), channel_id=1, source_target_pairs={{0,16},{8,24},{16,0},{24,8},{1,17},{9,25},{17,1},{25,9},{2,18},{10... | collective-permute-start | bytes 2359304 | tf_op jit(solution)/shard_map/ppermute | solution.py:17
  8.0 2.6 %collective-permute-start = (f32[4,128,256]{2,1,0:T(8,128)}, f32[4,128,256]{2,1,0:T(8,128)}, u32[]{:S(2)}, u32[]{:S(2)}) collective-permute-start(f32[4,128,256]{2,1,0:T(8,128)} %refs_0_.2), channel_id=1, source_target_pairs={{0,2},{2,0},{1,3},{3,1},{4,6},{6,4},{5,7},{7,5},{8,10},{10,8},{9,1... | collective-permute-start | bytes 1572872 | tf_op jit(solution)/shard_map/ppermute | solution.py:17
  10.6 1.6 %collective-permute-start.5 = (f32[3,256,256]{2,1,0:T(8,128)S(1)}, f32[3,256,256]{2,1,0:T(8,128)S(1)}, u32[]{:S(2)}, u32[]{:S(2)}) collective-permute-start(f32[3,256,256]{2,1,0:T(8,128)S(1)} %get-tuple-element.28.refs_8_.refs_0_), channel_id=1, source_target_pairs={{0,1},{1,0},{2,3},{3,2},{4,5},{5,4},{6,7},{7,6},{8,9},{9,8},{10,11... | collective-permute-start | bytes 2359304 | tf_op jit(solution)/shard_map/ppermute | solution.py:17
  12.2 0.5 collective-permute-start.8
  12.6 21.0 %collective-permute-done.refs_2_ = f32[4,128,256]{2,1,0:T(8,128)} collective-permute-done((f32[4,128,256]{2,1,0:T(8,128)}, f32[4,128,256]{2,1,0:T(8,128)}, u32[]{:S(2)}, u32[]{:S(2)}) %collective-permute-start) | collective-permute-done | bytes 524320 | tf_op jit(solution)/shard_map/ppermute | solution.py:17
  33.7 0.5 collective-permute-start.2
  34.3 4.9 %collective-permute-done.5.refs_7_.refs_4_ = f32[3,256,256]{2,1,0:T(8,128)S(1)} collective-permute-done((f32[3,256,256]{2,1,0:T(8,128)S(1)}, f32[3,256,256]{2,1,0:T(8,128)S(1)}, u32[]{:S(2)}, u32[]{:S(2)}) %collective-permute-start.5) | collective-permute-done | bytes 786464 | tf_op jit(solution)/shard_map/ppermute | solution.py:17
  39.2 1.3 pad_maximum_fusion
  40.5 0.5 collective-permute-start.7
  41.0 0.5 collective-permute-start.6
  41.5 1.0 pad_maximum_fusion.2
  42.5 1.7 %collective-permute-start.9 = (f32[3,256,256]{2,1,0:T(8,128)}, f32[3,256,256]{2,1,0:T(8,128)S(1)}, u32[]{:S(2)}, u32[]{:S(2)}) collective-permute-start(f32[3,256,256]{2,1,0:T(8,128)} %pad_maximum_fusion.2), channel_id=1, source_target_pairs={{0,1},{1,0},{2,3},{3,2},{4,5},{5,4},{6,7},{7,6},{8,9},{9,8},{10,11... | collective-permute-start | bytes 2359304 | tf_op jit(solution)/shard_map/ppermute | solution.py:17
  44.2 1.1 copy-done.1
  45.3 1.0 copy-done.19
  46.4 1.1 copy-done.25
  47.5 4.9 %shard_map.65 = (f32[4,4,256]{2,1,0:T(4,128)S(1)}, bf16[2,2,256,256]{3,2,1,0:T(8,128)(2,1)S(1)}, bf16[2,2,256,256]{3,2,1,0:T(8,128)(2,1)S(1)}, bf16[2,2,256,256]...) custom-call(s32[1]{0:T(128)} %bitcast.core_ref, f32[4,128,256]{2,1,0:T(8,128)S(1)} %copy-done.19, ...), custom_call_target="tpu_custom_call" | custom-call | flops 3221225472 | bytes 4194304 | tf_op jit(solution)/shard_map/pallas_call | solution.py:143
  52.4 0.8 copy-done.9
  53.2 5.1 %collective-permute-done.7.refs_5_ = f32[3,256,256]{2,1,0:T(8,128)} collective-permute-done((f32[3,256,256]{2,1,0:T(8,128)}, f32[3,256,256]{2,1,0:T(8,128)}, u32[]{:S(2)}, u32[]{:S(2)}) %collective-permute-start.7) | collective-permute-done | bytes 786464 | tf_op jit(solution)/shard_map/ppermute | solution.py:17
  58.3 1.0 slice.85
  59.3 0.6 collective-permute-start.10
  59.8 1.0 slice.86
  60.8 0.5 collective-permute-start.11
  61.4 4.5 %shard_map.66 = (f32[3,4,256]{2,1,0:T(4,128)S(1)}, bf16[2,2,256,256]{3,2,1,0:T(8,128)(2,1)S(1)}, bf16[2,2,256,256]{3,2,1,0:T(8,128)(2,1)S(1)}, bf16[2,2,256,256]{3,2,1,0:T(8,128)(2,1)S(1)}) custom-call(s32[1]{0:T(128)} %bitcast.core_ref, f32[4,128,256]{2,1,0:T(8,128)S(1)} %copy-done.20, f32[4,128,256]{2,1,0:T(8,128)} %collective-permute-done.1.refs_1_, ...), custom_call_target="tpu_custom_call" | custom-call | flops 2415919104 | bytes 3145728 | tf_op jit(solution)/shard_map/pallas_call | solution.py:143
  65.9 0.8 copy-done.11
  66.7 0.8 copy-done.13
  67.6 0.8 copy-done.15
  68.4 2.4 %shard_map.67 = (f32[1,4,256]{2,1,0:T(4,128)S(1)}, bf16[2,2,256,256]{3,2,1,0:T(8,128)(2,1)S(1)}) custom-call(s32[1]{0:T(128)} %bitcast.core_ref, f32[4,128,256]{2,1,0:T(8,128)S(1)} %copy-done.20, f32[4,128,256]{2,1,0:T(8,128)} %collective-permute-done.1.refs_1_, f32[4,128,256]{2,1,0:T(8,128)} %collective-permute-done.refs_2_, ...), custom_call_target="tpu_custom_call" | custom-call | flops 805306368 | bytes 1048576 | tf_op jit(solution)/shard_map/pallas_call | solution.py:143
  70.8 0.8 copy-done.17
  71.8 2.1 %collective-permute-start.12 = (f32[2,4,256]{2,1,0:T(4,128)S(1)}, f32[2,4,256]{2,1,0:T(4,128)S(1)}, u32[]{:S(2)}, u32[]{:S(2)}) collective-permute-start(f32[2,4,256]{2,1,0:T(4,128)S(1)} %get-tuple-element.49), channel_id=1, source_target_pairs={{0,1},{1,0},{2,3},{3,2},{4,5},{5,4},{6,7},{7,6},{8,9},{9,8},{10,11... | collective-permute-start | bytes 24584 | tf_op jit(solution)/shard_map/ppermute | solution.py:237
  73.8 1.2 collective-permute-start.13
  75.0 1.3 collective-permute-start.14
  76.3 2.1 %collective-permute-done.13 = f32[2,4,256]{2,1,0:T(4,128)S(1)} collective-permute-done((f32[2,4,256]{2,1,0:T(4,128)S(1)}, f32[2,4,256]{2,1,0:T(4,128)S(1)}, u32[]{:S(2)}, u32[]{:S(2)}) %collective-permute-start.13) | collective-permute-done | bytes 8224 | tf_op jit(solution)/shard_map/ppermute | solution.py:237
  78.4 2.1 %collective-permute-done.14 = f32[2,4,256]{2,1,0:T(4,128)S(1)} collective-permute-done((f32[2,4,256]{2,1,0:T(4,128)S(1)}, f32[2,4,256]{2,1,0:T(4,128)S(1)}, u32[]{:S(2)}, u32[]{:S(2)}) %collective-permute-start.14) | collective-permute-done | bytes 8224 | tf_op jit(solution)/shard_map/ppermute | solution.py:237
  80.5 1.6 %collective-permute-start.15 = (f32[2,2,4,256]{3,2,1,0:T(4,128)S(1)}, f32[2,2,4,256]{3,2,1,0:T(4,128)S(1)}, u32[]{:S(2)}, u32[]{:S(2)}) collective-permute-start(f32[2,2,4,256]{3,2,1,0:T(4,128)S(1)} %reverse_select_fusion.2), channel_id=1, source_target_pairs={{0,8},{8,0},{16,24},{24,16},{1,9},{9,1},{17,25},{25,17},{2,10},{10... | collective-permute-start | bytes 49160 | tf_op jit(solution)/shard_map/ppermute | solution.py:17
  82.0 1.5 %collective-permute-start.16 = (f32[2,2,4,256]{3,2,1,0:T(4,128)S(1)}, f32[2,2,4,256]{3,2,1,0:T(4,128)S(1)}, u32[]{:S(2)}, u32[]{:S(2)}) collective-permute-start(f32[2,2,4,256]{3,2,1,0:T(4,128)S(1)} %reverse_select_fusion.2), channel_id=1, source_target_pairs={{0,16},{8,24},{16,0},{24,8},{1,17},{9,25},{17,1},{25,9},{2,18},{10... | collective-permute-start | bytes 49160 | tf_op jit(solution)/shard_map/ppermute | solution.py:17
  83.6 0.5 collective-permute-start.17
  84.0 0.2 collective-permute-done.15
  84.3 1.5 %collective-permute-done.16 = f32[2,2,4,256]{3,2,1,0:T(4,128)S(1)} collective-permute-done((f32[2,2,4,256]{3,2,1,0:T(4,128)S(1)}, f32[2,2,4,256]{3,2,1,0:T(4,128)S(1)}, u32[]{:S(2)}, u32[]{:S(2)}) %collective-permute-start.16) | collective-permute-done | bytes 16416 | tf_op jit(solution)/shard_map/ppermute | solution.py:17
  85.8 2.4 %collective-permute-done.17 = f32[2,2,4,256]{3,2,1,0:T(4,128)S(1)} collective-permute-done((f32[2,2,4,256]{3,2,1,0:T(4,128)S(1)}, f32[2,2,4,256]{3,2,1,0:T(4,128)S(1)}, u32[]{:S(2)}, u32[]{:S(2)}) %collective-permute-start.17) | collective-permute-done | bytes 16416 | tf_op jit(solution)/shard_map/ppermute | solution.py:17
  88.4 1.1 collective-permute-done.18
  89.5 7.0 %convolution_bitcast_fusion = f32[2,2,4,256]{3,2,1,0:T(4,128)S(1)} fusion(f32[4,2048,1,1]{1,0,3,2:T(4,128)S(1)} %bitcast.68, f32[2,2,256,2048]{3,2,1,0:T(8,128)} %bitcast.63), kind=kOutput, calls=%fused_computation | convolution fusion | flops 50331648 | bytes 8437760 | tf_op jit(solution)/shard_map/dot_general | solution.py:321
  96.6 1.8 %collective-permute-start.20 = (f32[2,4,256]{2,1,0:T(4,128)S(1)}, f32[2,4,256]{2,1,0:T(4,128)S(1)}, u32[]{:S(2)}, u32[]{:S(2)}) collective-permute-start(f32[2,4,256]{2,1,0:T(4,128)S(1)} %get-tuple-element.53), channel_id=1, source_target_pairs={{0,2},{1,3},{2,0},{3,1},{4,6},{5,7},{6,4},{7,5},{8,10},{9,11},{10,... | collective-permute-start | bytes 24584 | tf_op jit(solution)/shard_map/ppermute | solution.py:237
  98.4 2.6 %collective-permute-start.21 = (f32[2,4,256]{2,1,0:T(4,128)S(1)}, f32[2,4,256]{2,1,0:T(4,128)S(1)}, u32[]{:S(2)}, u32[]{:S(2)}) collective-permute-start(f32[2,4,256]{2,1,0:T(4,128)S(1)} %get-tuple-element.53), channel_id=1, source_target_pairs={{0,3},{1,2},{2,1},{3,0},{4,7},{5,6},{6,5},{7,4},{8,11},{9,10},{10,... | collective-permute-start | bytes 24584 | tf_op jit(solution)/shard_map/ppermute | solution.py:237
  101.0 0.2 collective-permute-done.20
  101.3 2.6 %collective-permute-done.21 = f32[2,4,256]{2,1,0:T(4,128)S(1)} collective-permute-done((f32[2,4,256]{2,1,0:T(4,128)S(1)}, f32[2,4,256]{2,1,0:T(4,128)S(1)}, u32[]{:S(2)}, u32[]{:S(2)}) %collective-permute-start.21) | collective-permute-done | bytes 8224 | tf_op jit(solution)/shard_map/ppermute | solution.py:237
  103.9 0.6 collective-permute-start.22
  104.5 0.5 collective-permute-start.23
  105.0 2.5 %collective-permute-start.24 = (f32[2,4,256]{2,1,0:T(4,128)S(1)}, f32[2,4,256]{2,1,0:T(4,128)S(1)}, u32[]{:S(2)}, u32[]{:S(2)}) collective-permute-start(f32[2,4,256]{2,1,0:T(4,128)S(1)} %reverse_select_fusion.3), channel_id=1, source_target_pairs={{0,24},{8,16},{16,8},{24,0},{1,25},{9,17},{17,9},{25,1},{2,26},{10... | collective-permute-start | bytes 24584 | tf_op jit(solution)/shard_map/ppermute | solution.py:17
  107.5 0.2 collective-permute-done.22
  107.6 0.5 collective-permute-done.23
  108.2 1.4 collective-permute-done.24
  109.7 2.0 %shard_map.69 = f32[4,128,256]{2,1,0:T(8,128)S(1)} custom-call(s32[1]{0:T(128)} %bitcast.core_ref, f32[8,4,256]{2,1,0:T(4,128)S(1)} %bitcast.59, f32[3,256,256]{2,1,0:T(8,128)S(1)} %copy-done.2, f32[3,256,256]{2,1,0:T(8,128)S(1)} %collective-permute-done.3.refs_5_.refs_1_, f32[3,256,256]{2,1,0:T(8,128)S(1)} %collective-permute-done.4.refs_6_.refs_2_, ...), custom_call_target="tpu_custom_call" | custom-call | flops 1610612736 | bytes 4194304 | tf_op jit(solution)/shard_map/pallas_call | solution.py:200
  111.8 1.8 %shard_map.68 = f32[4,128,256]{2,1,0:T(8,128)S(1)} custom-call(s32[1]{0:T(128)} %bitcast.core_ref, f32[8,4,256]{2,1,0:T(4,128)S(1)} %bitcast.60, f32[3,256,256]{2,1,0:T(8,128)S(1)} %copy-done.2, f32[3,256,256]{2,1,0:T(8,128)S(1)} %collective-permute-done.3.refs_5_.refs_1_, f32[3,256,256]{2,1,0:T(8,128)S(1)} %collective-permute-done.4.refs_6_.refs_2_, ...), custom_call_target="tpu_custom_call" | custom-call | flops 1610612736 | bytes 4194304 | tf_op jit(solution)/shard_map/pallas_call | solution.py:200
  113.6 0.1 collective-permute-done.25
  113.8 1.8 %shard_map.71 = f32[4,128,256]{2,1,0:T(8,128)S(1)} custom-call(s32[1]{0:T(128)} %bitcast.core_ref, f32[8,4,256]{2,1,0:T(4,128)S(1)} %bitcast.61, f32[3,256,256]{2,1,0:T(8,128)S(1)} %copy-done.2, f32[3,256,256]{2,1,0:T(8,128)S(1)} %collective-permute-done.3.refs_5_.refs_1_, f32[3,256,256]{2,1,0:T(8,128)S(1)} %collective-permute-done.4.refs_6_.refs_2_, ...), custom_call_target="tpu_custom_call" | custom-call | flops 1610612736 | bytes 4194304 | tf_op jit(solution)/shard_map/pallas_call | solution.py:200
  115.6 0.5 collective-permute-start.27
  116.1 0.1 broadcast_subtract_fusion
  116.2 1.8 %shard_map.70 = f32[4,128,256]{2,1,0:T(8,128)S(1)} custom-call(s32[1]{0:T(128)} %bitcast.core_ref, f32[8,4,256]{2,1,0:T(4,128)S(1)} %bitcast.62, f32[3,256,256]{2,1,0:T(8,128)S(1)} %copy-done.2, f32[3,256,256]{2,1,0:T(8,128)S(1)} %collective-permute-done.3.refs_5_.refs_1_, f32[3,256,256]{2,1,0:T(8,128)S(1)} %collective-permute-done.4.refs_6_.refs_2_, ...), custom_call_target="tpu_custom_call" | custom-call | flops 1610612736 | bytes 4194304 | tf_op jit(solution)/shard_map/pallas_call | solution.py:200
  118.0 24.0 %collective-permute-done.26 = f32[4,128,256]{2,1,0:T(8,128)S(1)} collective-permute-done((f32[4,128,256]{2,1,0:T(8,128)S(1)}, f32[4,128,256]{2,1,0:T(8,128)S(1)}, u32[]{:S(2)}, u32[]{:S(2)}) %collective-permute-start.26) | collective-permute-done | bytes 524320 | tf_op jit(solution)/shard_map/ppermute | solution.py:17
  142.1 0.9 add_add_fusion
  (94 shorter events, 0.8 us)
Async XLA Ops:
  0.1 1.2 copy-start.22
  1.3 1.2 copy-start.23
  3.4 38.0 %copy-start = (f32[3,256,256]{2,1,0:T(8,128)}, f32[3,256,256]{2,1,0:T(8,128)S(1)}, u32[]{:S(2)}) copy-start(f32[3,256,256]{2,1,0:T(8,128)S(1)} %get-tuple-element.28.refs_8_.refs_0_) | copy-start | bytes 2359300
  3.5 39.0 %copy-start.24 = (f32[3,256,256]{2,1,0:T(8,128)}, f32[3,256,256]{2,1,0:T(8,128)S(1)}, u32[]{:S(2)}) copy-start(f32[3,256,256]{2,1,0:T(8,128)S(1)} %get-tuple-element.26.refs_4_) | copy-start | bytes 2359300
  3.5 30.2 %collective-permute-start.3 = (f32[3,256,256]{2,1,0:T(8,128)S(1)}, f32[3,256,256]{2,1,0:T(8,128)S(1)}, u32[]{:S(2)}, u32[]{:S(2)}) collective-permute-start(f32[3,256,256]{2,1,0:T(8,128)S(1)} %get-tuple-element.26.refs_4_), channel_id=1, source_target_pairs={{0,8},{8,0},{16,24},{24,16},{1,9},{9,1},{17,25},{25,17},{2,10},{10... | collective-permute-start | bytes 2359304 | tf_op jit(solution)/shard_map/ppermute | solution.py:17
  6.5 27.7 %collective-permute-start.4 = (f32[3,256,256]{2,1,0:T(8,128)S(1)}, f32[3,256,256]{2,1,0:T(8,128)S(1)}, u32[]{:S(2)}, u32[]{:S(2)}) collective-permute-start(f32[3,256,256]{2,1,0:T(8,128)S(1)} %get-tuple-element.27), channel_id=1, source_target_pairs={{0,16},{8,24},{16,0},{24,8},{1,17},{9,25},{17,1},{25,9},{2,18},{10... | collective-permute-start | bytes 2359304 | tf_op jit(solution)/shard_map/ppermute | solution.py:17
  8.0 25.7 %collective-permute-start = (f32[4,128,256]{2,1,0:T(8,128)}, f32[4,128,256]{2,1,0:T(8,128)}, u32[]{:S(2)}, u32[]{:S(2)}) collective-permute-start(f32[4,128,256]{2,1,0:T(8,128)} %refs_0_.2), channel_id=1, source_target_pairs={{0,2},{2,0},{1,3},{3,1},{4,6},{6,4},{5,7},{7,5},{8,10},{10,8},{9,1... | collective-permute-start | bytes 1572872 | tf_op jit(solution)/shard_map/ppermute | solution.py:17
  10.6 28.6 %collective-permute-start.5 = (f32[3,256,256]{2,1,0:T(8,128)S(1)}, f32[3,256,256]{2,1,0:T(8,128)S(1)}, u32[]{:S(2)}, u32[]{:S(2)}) collective-permute-start(f32[3,256,256]{2,1,0:T(8,128)S(1)} %get-tuple-element.28.refs_8_.refs_0_), channel_id=1, source_target_pairs={{0,1},{1,0},{2,3},{3,2},{4,5},{5,4},{6,7},{7,6},{8,9},{9,8},{10,11... | collective-permute-start | bytes 2359304 | tf_op jit(solution)/shard_map/ppermute | solution.py:17
  12.2 29.3 %collective-permute-start.8 = (f32[1,256,256]{2,1,0:T(8,128)S(1)}, f32[1,256,256]{2,1,0:T(8,128)S(1)}, u32[]{:S(2)}, u32[]{:S(2)}) collective-permute-start(f32[1,256,256]{2,1,0:T(8,128)S(1)} %get-tuple-element.30), channel_id=1, source_target_pairs={{0,24},{8,16},{16,8},{24,0},{1,25},{9,17},{17,9},{25,1},{2,26},{10... | collective-permute-start | bytes 786440 | tf_op jit(solution)/shard_map/ppermute | solution.py:17
  33.6 10.5 %collective-permute-start.1 = (f32[4,128,256]{2,1,0:T(8,128)}, f32[4,128,256]{2,1,0:T(8,128)}, u32[]{:S(2)}, u32[]{:S(2)}) collective-permute-start(f32[4,128,256]{2,1,0:T(8,128)} %refs_0_.2), channel_id=1, source_target_pairs={{0,4},{4,0},{1,5},{5,1},{2,6},{6,2},{3,7},{7,3},{8,12},{12,8},{9,1... | collective-permute-start | bytes 1572872 | tf_op jit(solution)/shard_map/ppermute | solution.py:17
  33.7 10.5 %collective-permute-start.2 = (f32[4,128,256]{2,1,0:T(8,128)}, f32[4,128,256]{2,1,0:T(8,128)}, u32[]{:S(2)}, u32[]{:S(2)}) collective-permute-start(f32[4,128,256]{2,1,0:T(8,128)} %collective-permute-done.refs_2_), channel_id=1, source_target_pairs={{0,4},{4,0},{1,5},{5,1},{2,6},{6,2},{3,7},{7,3},{8,12},{12,8},{9,1... | collective-permute-start | bytes 1572872 | tf_op jit(solution)/shard_map/ppermute | solution.py:17
  40.5 17.8 %collective-permute-start.7 = (f32[3,256,256]{2,1,0:T(8,128)}, f32[3,256,256]{2,1,0:T(8,128)}, u32[]{:S(2)}, u32[]{:S(2)}) collective-permute-start(f32[3,256,256]{2,1,0:T(8,128)} %get-tuple-element.47), channel_id=1, source_target_pairs={{0,8},{8,0},{16,24},{24,16},{1,9},{9,1},{17,25},{25,17},{2,10},{10... | collective-permute-start | bytes 2359304 | tf_op jit(solution)/shard_map/ppermute | solution.py:17
  41.0 18.8 %collective-permute-start.6 = (f32[3,256,256]{2,1,0:T(8,128)}, f32[3,256,256]{2,1,0:T(8,128)}, u32[]{:S(2)}, u32[]{:S(2)}) collective-permute-start(f32[3,256,256]{2,1,0:T(8,128)} %get-tuple-element.48), channel_id=1, source_target_pairs={{0,16},{8,24},{16,0},{24,8},{1,17},{9,25},{17,1},{25,9},{2,18},{10... | collective-permute-start | bytes 2359304 | tf_op jit(solution)/shard_map/ppermute | solution.py:17
  42.5 18.9 %collective-permute-start.9 = (f32[3,256,256]{2,1,0:T(8,128)}, f32[3,256,256]{2,1,0:T(8,128)S(1)}, u32[]{:S(2)}, u32[]{:S(2)}) collective-permute-start(f32[3,256,256]{2,1,0:T(8,128)} %pad_maximum_fusion.2), channel_id=1, source_target_pairs={{0,1},{1,0},{2,3},{3,2},{4,5},{5,4},{6,7},{7,6},{8,9},{9,8},{10,11... | collective-permute-start | bytes 2359304 | tf_op jit(solution)/shard_map/ppermute | solution.py:17
  44.2 1.1 copy-start.1
  45.3 1.0 copy-start.19
  46.4 1.1 copy-start.25
  47.5 13.9 %copy-start.20 = (f32[4,128,256]{2,1,0:T(8,128)S(1)}, f32[4,128,256]{2,1,0:T(8,128)}, u32[]{:S(2)}) copy-start(f32[4,128,256]{2,1,0:T(8,128)} %refs_0_.2) | copy-start | bytes 1572868
  52.4 0.8 copy-start.9
  53.2 7.6 %copy-start.3 = (bf16[2,2,256,256]{3,2,1,0:T(8,128)(2,1)}, bf16[2,2,256,256]{3,2,1,0:T(8,128)(2,1)S(1)}, u32[]{:S(2)}) copy-start(bf16[2,2,256,256]{3,2,1,0:T(8,128)(2,1)S(1)} %get-tuple-element.33.refs_6_) | copy-start | bytes 1572868
  53.2 8.2 %copy-start.5 = (bf16[2,2,256,256]{3,2,1,0:T(8,128)(2,1)}, bf16[2,2,256,256]{3,2,1,0:T(8,128)(2,1)S(1)}, u32[]{:S(2)}) copy-start(bf16[2,2,256,256]{3,2,1,0:T(8,128)(2,1)S(1)} %get-tuple-element.34.refs_7_) | copy-start | bytes 1572868
  53.2 12.7 %copy-start.7 = (bf16[2,2,256,256]{3,2,1,0:T(8,128)(2,1)}, bf16[2,2,256,256]{3,2,1,0:T(8,128)(2,1)S(1)}, u32[]{:S(2)}) copy-start(bf16[2,2,256,256]{3,2,1,0:T(8,128)(2,1)S(1)} %get-tuple-element.35.refs_8_) | copy-start | bytes 1572868
  59.3 9.1 %collective-permute-start.10 = (f32[1,256,256]{2,1,0:T(8,128)S(1)}, f32[1,256,256]{2,1,0:T(8,128)S(1)}, u32[]{:S(2)}, u32[]{:S(2)}) collective-permute-start(f32[1,256,256]{2,1,0:T(8,128)S(1)} %slice.85), channel_id=1, source_target_pairs={{0,16},{8,24},{16,0},{24,8},{1,17},{9,25},{17,1},{25,9},{2,18},{10... | collective-permute-start | bytes 786440 | tf_op jit(solution)/shard_map/ppermute | solution.py:17
  60.8 7.6 %collective-permute-start.11 = (f32[1,256,256]{2,1,0:T(8,128)S(1)}, f32[1,256,256]{2,1,0:T(8,128)S(1)}, u32[]{:S(2)}, u32[]{:S(2)}) collective-permute-start(f32[1,256,256]{2,1,0:T(8,128)S(1)} %slice.86), channel_id=1, source_target_pairs={{0,8},{8,0},{16,24},{24,16},{1,9},{9,1},{17,25},{25,17},{2,10},{10... | collective-permute-start | bytes 786440 | tf_op jit(solution)/shard_map/ppermute | solution.py:17
  65.9 0.8 copy-start.11
  66.7 0.8 copy-start.13
  67.6 0.8 copy-start.15
  70.8 0.8 copy-start.17
  71.8 4.5 %collective-permute-start.12 = (f32[2,4,256]{2,1,0:T(4,128)S(1)}, f32[2,4,256]{2,1,0:T(4,128)S(1)}, u32[]{:S(2)}, u32[]{:S(2)}) collective-permute-start(f32[2,4,256]{2,1,0:T(4,128)S(1)} %get-tuple-element.49), channel_id=1, source_target_pairs={{0,1},{1,0},{2,3},{3,2},{4,5},{5,4},{6,7},{7,6},{8,9},{9,8},{10,11... | collective-permute-start | bytes 24584 | tf_op jit(solution)/shard_map/ppermute | solution.py:237
  73.8 4.5 %collective-permute-start.13 = (f32[2,4,256]{2,1,0:T(4,128)S(1)}, f32[2,4,256]{2,1,0:T(4,128)S(1)}, u32[]{:S(2)}, u32[]{:S(2)}) collective-permute-start(f32[2,4,256]{2,1,0:T(4,128)S(1)} %get-tuple-element.51), channel_id=1, source_target_pairs={{0,2},{1,3},{2,0},{3,1},{4,6},{5,7},{6,4},{7,5},{8,10},{9,11},{10,... | collective-permute-start | bytes 24584 | tf_op jit(solution)/shard_map/ppermute | solution.py:237
  75.0 5.4 %collective-permute-start.14 = (f32[2,4,256]{2,1,0:T(4,128)S(1)}, f32[2,4,256]{2,1,0:T(4,128)S(1)}, u32[]{:S(2)}, u32[]{:S(2)}) collective-permute-start(f32[2,4,256]{2,1,0:T(4,128)S(1)} %get-tuple-element.50), channel_id=1, source_target_pairs={{0,3},{1,2},{2,1},{3,0},{4,7},{5,6},{6,5},{7,4},{8,11},{9,10},{10,... | collective-permute-start | bytes 24584 | tf_op jit(solution)/shard_map/ppermute | solution.py:237
  80.5 3.8 %collective-permute-start.15 = (f32[2,2,4,256]{3,2,1,0:T(4,128)S(1)}, f32[2,2,4,256]{3,2,1,0:T(4,128)S(1)}, u32[]{:S(2)}, u32[]{:S(2)}) collective-permute-start(f32[2,2,4,256]{3,2,1,0:T(4,128)S(1)} %reverse_select_fusion.2), channel_id=1, source_target_pairs={{0,8},{8,0},{16,24},{24,16},{1,9},{9,1},{17,25},{25,17},{2,10},{10... | collective-permute-start | bytes 49160 | tf_op jit(solution)/shard_map/ppermute | solution.py:17
  82.0 3.7 %collective-permute-start.16 = (f32[2,2,4,256]{3,2,1,0:T(4,128)S(1)}, f32[2,2,4,256]{3,2,1,0:T(4,128)S(1)}, u32[]{:S(2)}, u32[]{:S(2)}) collective-permute-start(f32[2,2,4,256]{3,2,1,0:T(4,128)S(1)} %reverse_select_fusion.2), channel_id=1, source_target_pairs={{0,16},{8,24},{16,0},{24,8},{1,17},{9,25},{17,1},{25,9},{2,18},{10... | collective-permute-start | bytes 49160 | tf_op jit(solution)/shard_map/ppermute | solution.py:17
  83.6 4.6 %collective-permute-start.17 = (f32[2,2,4,256]{3,2,1,0:T(4,128)S(1)}, f32[2,2,4,256]{3,2,1,0:T(4,128)S(1)}, u32[]{:S(2)}, u32[]{:S(2)}) collective-permute-start(f32[2,2,4,256]{3,2,1,0:T(4,128)S(1)} %reverse_select_fusion.2), channel_id=1, source_target_pairs={{0,24},{8,16},{16,8},{24,0},{1,25},{9,17},{17,9},{25,1},{2,26},{10... | collective-permute-start | bytes 49160 | tf_op jit(solution)/shard_map/ppermute | solution.py:17
  88.2 1.2 collective-permute-start.18
  88.3 21.3 %copy-start.2 = (f32[3,256,256]{2,1,0:T(8,128)S(1)}, f32[3,256,256]{2,1,0:T(8,128)}, u32[]{:S(2)}) copy-start(f32[3,256,256]{2,1,0:T(8,128)} %copy-done) | copy-start | bytes 2359300
  88.3 21.3 %copy-start.4 = (bf16[2,2,256,256]{3,2,1,0:T(8,128)(2,1)S(1)}, bf16[2,2,256,256]{3,2,1,0:T(8,128)(2,1)}, u32[]{:S(2)}) copy-start(bf16[2,2,256,256]{3,2,1,0:T(8,128)(2,1)} %copy-done.3) | copy-start | bytes 1572868
  88.3 21.3 %copy-start.6 = (bf16[2,2,256,256]{3,2,1,0:T(8,128)(2,1)S(1)}, bf16[2,2,256,256]{3,2,1,0:T(8,128)(2,1)}, u32[]{:S(2)}) copy-start(bf16[2,2,256,256]{3,2,1,0:T(8,128)(2,1)} %copy-done.5) | copy-start | bytes 1572868
  88.3 21.3 %copy-start.8 = (bf16[2,2,256,256]{3,2,1,0:T(8,128)(2,1)S(1)}, bf16[2,2,256,256]{3,2,1,0:T(8,128)(2,1)}, u32[]{:S(2)}) copy-start(bf16[2,2,256,256]{3,2,1,0:T(8,128)(2,1)} %copy-done.7) | copy-start | bytes 1572868
  88.3 21.3 %copy-start.10 = (bf16[2,2,256,256]{3,2,1,0:T(8,128)(2,1)S(1)}, bf16[2,2,256,256]{3,2,1,0:T(8,128)(2,1)}, u32[]{:S(2)}) copy-start(bf16[2,2,256,256]{3,2,1,0:T(8,128)(2,1)} %copy-done.9) | copy-start | bytes 1572868
  88.4 21.3 %copy-start.12 = (bf16[2,2,256,256]{3,2,1,0:T(8,128)(2,1)S(1)}, bf16[2,2,256,256]{3,2,1,0:T(8,128)(2,1)}, u32[]{:S(2)}) copy-start(bf16[2,2,256,256]{3,2,1,0:T(8,128)(2,1)} %copy-done.11) | copy-start | bytes 1572868
  88.4 21.3 %copy-start.14 = (bf16[2,2,256,256]{3,2,1,0:T(8,128)(2,1)S(1)}, bf16[2,2,256,256]{3,2,1,0:T(8,128)(2,1)}, u32[]{:S(2)}) copy-start(bf16[2,2,256,256]{3,2,1,0:T(8,128)(2,1)} %copy-done.13) | copy-start | bytes 1572868
  88.4 21.3 %copy-start.16 = (bf16[2,2,256,256]{3,2,1,0:T(8,128)(2,1)S(1)}, bf16[2,2,256,256]{3,2,1,0:T(8,128)(2,1)}, u32[]{:S(2)}) copy-start(bf16[2,2,256,256]{3,2,1,0:T(8,128)(2,1)} %copy-done.15) | copy-start | bytes 1572868
  88.4 21.3 %copy-start.18 = (bf16[2,2,256,256]{3,2,1,0:T(8,128)(2,1)S(1)}, bf16[2,2,256,256]{3,2,1,0:T(8,128)(2,1)}, u32[]{:S(2)}) copy-start(bf16[2,2,256,256]{3,2,1,0:T(8,128)(2,1)} %copy-done.17) | copy-start | bytes 1572868
  96.6 4.5 %collective-permute-start.19 = (f32[2,4,256]{2,1,0:T(4,128)S(1)}, f32[2,4,256]{2,1,0:T(4,128)S(1)}, u32[]{:S(2)}, u32[]{:S(2)}) collective-permute-start(f32[2,4,256]{2,1,0:T(4,128)S(1)} %get-tuple-element.52), channel_id=1, source_target_pairs={{0,1},{1,0},{2,3},{3,2},{4,5},{5,4},{6,7},{7,6},{8,9},{9,8},{10,11... | collective-permute-start | bytes 24584 | tf_op jit(solution)/shard_map/ppermute | solution.py:237
  96.6 4.6 %collective-permute-start.20 = (f32[2,4,256]{2,1,0:T(4,128)S(1)}, f32[2,4,256]{2,1,0:T(4,128)S(1)}, u32[]{:S(2)}, u32[]{:S(2)}) collective-permute-start(f32[2,4,256]{2,1,0:T(4,128)S(1)} %get-tuple-element.53), channel_id=1, source_target_pairs={{0,2},{1,3},{2,0},{3,1},{4,6},{5,7},{6,4},{7,5},{8,10},{9,11},{10,... | collective-permute-start | bytes 24584 | tf_op jit(solution)/shard_map/ppermute | solution.py:237
  98.4 5.4 %collective-permute-start.21 = (f32[2,4,256]{2,1,0:T(4,128)S(1)}, f32[2,4,256]{2,1,0:T(4,128)S(1)}, u32[]{:S(2)}, u32[]{:S(2)}) collective-permute-start(f32[2,4,256]{2,1,0:T(4,128)S(1)} %get-tuple-element.53), channel_id=1, source_target_pairs={{0,3},{1,2},{2,1},{3,0},{4,7},{5,6},{6,5},{7,4},{8,11},{9,10},{10,... | collective-permute-start | bytes 24584 | tf_op jit(solution)/shard_map/ppermute | solution.py:237
  103.9 3.7 %collective-permute-start.22 = (f32[2,4,256]{2,1,0:T(4,128)S(1)}, f32[2,4,256]{2,1,0:T(4,128)S(1)}, u32[]{:S(2)}, u32[]{:S(2)}) collective-permute-start(f32[2,4,256]{2,1,0:T(4,128)S(1)} %reverse_select_fusion.3), channel_id=1, source_target_pairs={{0,8},{8,0},{16,24},{24,16},{1,9},{9,1},{17,25},{25,17},{2,10},{10... | collective-permute-start | bytes 24584 | tf_op jit(solution)/shard_map/ppermute | solution.py:17
  104.5 3.7 %collective-permute-start.23 = (f32[2,4,256]{2,1,0:T(4,128)S(1)}, f32[2,4,256]{2,1,0:T(4,128)S(1)}, u32[]{:S(2)}, u32[]{:S(2)}) collective-permute-start(f32[2,4,256]{2,1,0:T(4,128)S(1)} %reverse_select_fusion.3), channel_id=1, source_target_pairs={{0,16},{8,24},{16,0},{24,8},{1,17},{9,25},{17,1},{25,9},{2,18},{10... | collective-permute-start | bytes 24584 | tf_op jit(solution)/shard_map/ppermute | solution.py:17
  105.0 4.5 %collective-permute-start.24 = (f32[2,4,256]{2,1,0:T(4,128)S(1)}, f32[2,4,256]{2,1,0:T(4,128)S(1)}, u32[]{:S(2)}, u32[]{:S(2)}) collective-permute-start(f32[2,4,256]{2,1,0:T(4,128)S(1)} %reverse_select_fusion.3), channel_id=1, source_target_pairs={{0,24},{8,16},{16,8},{24,0},{1,25},{9,17},{17,9},{25,1},{2,26},{10... | collective-permute-start | bytes 24584 | tf_op jit(solution)/shard_map/ppermute | solution.py:17
  111.7 4.4 %copy-start.26 = (f32[256]{0:T(256)S(1)}, f32[256]{0:T(256)}, u32[]{:S(2)}) copy-start(f32[256]{0:T(256)} %param.8) | copy-start | bytes 3076
  111.7 4.4 %copy-start.27 = (f32[128]{0:T(128)S(1)}, f32[128]{0:T(128)}, u32[]{:S(2)}) copy-start(f32[128]{0:T(128)} %param.7) | copy-start | bytes 1540
  111.7 2.0 %collective-permute-start.25 = (f32[4,128,256]{2,1,0:T(8,128)S(1)}, f32[4,128,256]{2,1,0:T(8,128)S(1)}, u32[]{:S(2)}, u32[]{:S(2)}) collective-permute-start(f32[4,128,256]{2,1,0:T(8,128)S(1)} %shard_map.69), channel_id=1, source_target_pairs={{0,4},{4,0},{1,5},{5,1},{2,6},{6,2},{3,7},{7,3},{8,12},{12,8},{9,1... | collective-permute-start | bytes 1572872 | tf_op jit(solution)/shard_map/ppermute | solution.py:17
  113.8 28.3 %copy-start.21 = (f32[4,128,256]{2,1,0:T(8,128)S(1)}, f32[4,128,256]{2,1,0:T(8,128)}, u32[]{:S(2)}) copy-start(f32[4,128,256]{2,1,0:T(8,128)} %refs_0_.2) | copy-start | bytes 1572868
  115.6 2.4 %collective-permute-start.27 = (f32[4,128,256]{2,1,0:T(8,128)S(1)}, f32[4,128,256]{2,1,0:T(8,128)S(1)}, u32[]{:S(2)}, u32[]{:S(2)}) collective-permute-start(f32[4,128,256]{2,1,0:T(8,128)S(1)} %shard_map.71), channel_id=1, source_target_pairs={{0,4},{4,0},{1,5},{5,1},{2,6},{6,2},{3,7},{7,3},{8,12},{12,8},{9,1... | collective-permute-start | bytes 1572872 | tf_op jit(solution)/shard_map/ppermute | solution.py:17
  116.1 26.0 %collective-permute-start.26 = (f32[4,128,256]{2,1,0:T(8,128)S(1)}, f32[4,128,256]{2,1,0:T(8,128)S(1)}, u32[]{:S(2)}, u32[]{:S(2)}) collective-permute-start(f32[4,128,256]{2,1,0:T(8,128)S(1)} %add.48), channel_id=1, source_target_pairs={{0,2},{2,0},{1,3},{3,1},{4,6},{6,4},{5,7},{7,5},{8,10},{10,8},{9,1... | collective-permute-start | bytes 1572872 | tf_op jit(solution)/shard_map/ppermute | solution.py:17

commit v3 on v2

v3 whole, which is shorter than its diff:
```python
import functools

import jax
import jax.numpy as jnp
from jax import lax
from jax.experimental import pallas as pl
from jax.experimental.pallas import tpu as pltpu
from jax.sharding import Mesh, PartitionSpec as P

HIGH = lax.Precision.HIGH
VMEM = pl.BlockSpec(memory_space=pltpu.VMEM)
ANY = pl.BlockSpec(memory_space=pl.ANY)
SMEM = pl.BlockSpec(memory_space=pltpu.SMEM)
COST = pl.CostEstimate(flops=2 * 10**9, bytes_accessed=4 * 2**20, transcendentals=0)
PARAMS = pltpu.CompilerParams(vmem_limit_bytes=14 * 1024 * 1024)


def swap(x, axis, size, mask):
    return lax.ppermute(x, axis, [(i, i ^ mask) for i in range(size)])


def relative(x, axis, index):
    size = x.shape[axis]
    bit = 1
    while bit < size:
        shape = x.shape[:axis] + (size // (2 * bit), 2, bit) + x.shape[axis + 1:]
        flipped = jnp.flip(x.reshape(shape), axis + 1).reshape(x.shape)
        x = jnp.where((index & bit) != 0, flipped, x)
        bit *= 2
    return x


def ordered(first, then):
    return lax.optimization_barrier((first, then))


def single(j):
    return j & (j - 1) == 0


def split(x):
    high = x.astype(jnp.bfloat16)
    return high, (x - high.astype(jnp.float32)).astype(jnp.bfloat16)


def pack_kernel(nchip, ntop, where, con_ref, val_ref, *outs):
    nc = outs[0].shape[2]
    rc, top, pair = where[0], where[1], where[2]

    def con_tile(a, e):
        at = ((top ^ a) * 2 + (pair ^ e)) * nc
        return con_ref[:, pl.ds(pl.multiple_of(at, nc), nc)]

    def val_tile(j):
        at = (rc ^ j) * nc
        return val_ref[:, pl.ds(pl.multiple_of(at, nc), nc)].T

    for j in range(nchip + 1):
        out = outs[j]
        if j == 0 or (j < nchip and single(j)):
            for a in range(ntop):
                out[a] = con_tile(a, int(j == 0))
        if j:
            out[out.shape[0] - 1] = val_tile(j % nchip)


def pack(nchip, ntop, aligned, rc, top, pair, orb_con, orb_val, nc):
    pts = orb_con.shape[0]
    if aligned:
        sizes = [ntop] + [ntop + 1 if single(j) else 1 for j in range(1, nchip)] + [1]
        return pl.pallas_call(
            functools.partial(pack_kernel, nchip, ntop),
            out_shape=[jax.ShapeDtypeStruct((s, pts, nc), jnp.float32) for s in sizes],
            in_specs=[SMEM, VMEM, VMEM],
            out_specs=[VMEM] * (nchip + 1),
            compiler_params=PARAMS,
            cost_estimate=COST,
        )(jnp.stack([rc, top, pair]).astype(jnp.int32), orb_con, orb_val)

    def con_tile(a, e):
        return lax.dynamic_slice_in_dim(orb_con, ((top ^ a) * 2 + (pair ^ e)) * nc, nc, 1)

    def val_tile(j):
        return lax.dynamic_slice_in_dim(orb_val, (rc ^ j) * nc, nc, 1).T.reshape(pts, nc)

    out = [jnp.stack([con_tile(a, 1) for a in range(ntop)])]
    for j in range(1, nchip):
        con = [con_tile(a, 0) for a in range(ntop)] if single(j) else []
        out.append(jnp.stack(con + [val_tile(j)]))
    return out + [val_tile(0)[None]]


def operands(tiles):
    arrays, at = [], []
    for array, index in tiles:
        where = [i for i, other in enumerate(arrays) if other is array]
        if not where:
            arrays.append(array)
            where = [len(arrays) - 1]
        at.append((where[0], index))
    return arrays, at


def halves_kernel(x_refs, out_ref):
    nb, nv, nc = x_refs[0].shape
    width = out_ref.shape[1] // 2
    for i, ref in enumerate(x_refs):
        a, k = i // 2, i % 2
        high, low = split(ref[...].reshape(nb * nv, nc))
        rows = pl.ds(k * nb * nv, nb * nv)
        out_ref[rows, pl.ds(a * nc, nc)] = high
        out_ref[rows, pl.ds(width + a * nc, nc)] = low


def halves(x):
    flat = [t for row in x for t in row]
    nb, nv, nc = flat[0].shape
    return pl.pallas_call(
        lambda *refs: halves_kernel(refs[:-1], refs[-1]),
        out_shape=jax.ShapeDtypeStruct((2 * nb * nv, 2 * len(x) * nc), jnp.bfloat16),
        in_specs=[VMEM] * len(flat),
        out_specs=VMEM,
        compiler_params=PARAMS,
        cost_estimate=COST,
    )(*flat)


def density_kernel(nblk, ntop, shape, con_at, val_at, core_ref, x_ref, *refs):
    tiles, (dens_ref, right) = refs[:-2], refs[-2:]
    nb, nv, nc = shape
    width = ntop * nc
    core = core_ref[0]
    for g in range(nblk):
        for a in range(ntop):
            array, index = con_at[g * ntop + a]
            high, low = split(tiles[array][index])
            right[g, :, pl.ds(a * nc, nc)] = high
            right[g, :, pl.ds(width + a * nc, nc)] = high
            right[g, :, pl.ds(2 * width + a * nc, nc)] = low
        array, index = val_at[g]
        total = None
        for k in range(2):
            at = pl.ds(k * nb * nv, nb * nv)
            left = jnp.concatenate([x_ref[at, :], x_ref[at, pl.ds(0, width)]], axis=1)
            through = lax.dot_general(
                left, right[g], (((1,), (1,)), ((), ())), preferred_element_type=jnp.float32
            )
            rows = tiles[array][index, pl.ds(pl.multiple_of((core ^ k) * nv, nv), nv), :]
            part = jnp.sum(through.reshape(nb, nv, -1) * rows[None], axis=1)
            total = part if total is None else total + part
        dens_ref[g] = total


def densities(aligned, core, shape, x, con, val):
    nblk, ntop = len(con), len(con[0])
    nb, nv, nc = shape
    if aligned:
        arrays, at = operands([t for row in con for t in row] + list(val))
        pts = arrays[0].shape[1]
        return pl.pallas_call(
            functools.partial(density_kernel, nblk, ntop, shape, at[:nblk * ntop], at[nblk * ntop:]),
            out_shape=jax.ShapeDtypeStruct((nblk, nb, pts), jnp.float32),
            in_specs=[SMEM] + [VMEM] * (1 + len(arrays)),
            out_specs=VMEM,
            scratch_shapes=[pltpu.VMEM((nblk, pts, 3 * ntop * nc), jnp.bfloat16)],
            compiler_params=PARAMS,
            cost_estimate=COST,
        )(core.astype(jnp.int32)[None], x, *arrays)
    out = []
    for g in range(nblk):
        through = 0.0
        for a in range(ntop):
            array, index = con[g][a]
            through = through + jnp.einsum("bkvc,pc->bkvp", x[a], array[index], precision=HIGH)
        array, index = val[g]
        out.append(jnp.sum(through * array[index].reshape(1, 2, nv, -1), axis=(1, 2)))
    return jnp.stack(out)


def route_kernel(order, nchip, where, *refs):
    groups, out_ref, held = refs[:-2], refs[-2], refs[-1]
    nb = held.shape[1]
    rc, pair = where[0], where[1]
    at = 0
    for ref in groups:
        for g in range(ref.shape[0]):
            held[order[at]] = ref[g]
            at += 1
    for z in range(nchip):
        for p in range(2):
            piece = held[(pair ^ p) * nchip + (rc ^ z)]
            for d in range(out_ref.shape[0] // nchip):
                out_ref[d * nchip + z, pl.ds(p * nb, nb), :] = piece


def route(aligned, nchip, rc, pair, order, groups):
    nb, pts = groups[0].shape[1:]
    if aligned:
        return pl.pallas_call(
            functools.partial(route_kernel, order, nchip),
            out_shape=jax.ShapeDtypeStruct((2 * nchip * nchip, 2 * nb, pts), jnp.float32),
            in_specs=[SMEM] + [VMEM] * len(groups),
            out_specs=VMEM,
            scratch_shapes=[pltpu.VMEM((2 * nchip, nb, pts), jnp.float32)],
            compiler_params=PARAMS,
            cost_estimate=COST,
        )(jnp.stack([rc, pair]).astype(jnp.int32), *groups)
    flat = jnp.concatenate(groups)
    flat = jnp.stack([flat[order.index(i)] for i in range(2 * nchip)]).reshape(2, nchip, nb, pts)
    flat = jnp.transpose(relative(relative(flat, 1, rc), 0, pair), (1, 0, 2, 3)).reshape(nchip, 2 * nb, pts)
    return jnp.tile(flat, (2 * nchip, 1, 1))


def screen_kernel(nchip, ntop, top_ref, got_ref, w_ref, *refs):
    outs, (dens, left) = refs[:ntop], refs[ntop:]
    nb = got_ref.shape[1] // 2
    pts = got_ref.shape[2]
    top = top_ref[0]
    for k in range(2):
        for t in range(ntop):
            total = None
            for r in range(nchip):
                for p in range(2):
                    piece = got_ref[((r * 2 + k) * ntop + t) * 2 + p]
                    total = piece if total is None else total + piece
            for p in range(2):
                dens[:, pl.ds(((k * ntop + t) * 2 + p) * pts, pts)] = total[p * nb:(p + 1) * nb]
    high, low = split(dens[...])
    left[...] = jnp.zeros_like(left)
    left[pl.ds(0, nb), :] = high
    left[pl.ds(nb, nb), :] = low
    for a in range(ntop):
        for p in range(2):
            at = pl.multiple_of(((top ^ a) * 2 + p) * pts, pts)
            high, low = split(w_ref[pl.ds(at, pts), :])
            dims = (((1,), (1,)), ((), ()))
            total = lax.dot_general(left[...], high, dims, preferred_element_type=jnp.float32)
            extra = lax.dot_general(left[...], low, dims, preferred_element_type=jnp.float32)
            outs[a][pl.ds(p * nb, nb), :] = total[:nb] + total[nb:2 * nb] + extra[:nb]


def screen(aligned, nchip, ntop, top, got, screened_w):
    nb, pts = got.shape[1] // 2, got.shape[2]
    if aligned:
        nq = screened_w.shape[1]
        return pl.pallas_call(
            functools.partial(screen_kernel, nchip, ntop),
            out_shape=[jax.ShapeDtypeStruct((2 * nb, pts), jnp.float32)] * ntop,
            in_specs=[SMEM, VMEM, VMEM],
            out_specs=[VMEM] * ntop,
            scratch_shapes=[pltpu.VMEM((nb, nq), jnp.float32), pltpu.VMEM((16, nq), jnp.bfloat16)],
            compiler_params=PARAMS,
            cost_estimate=COST,
        )(top.astype(jnp.int32)[None], got, screened_w)
    density = jnp.sum(got.reshape(nchip, 2, ntop, 2, 2, nb, pts), axis=(0, 3))
    density = jnp.transpose(density.reshape(-1, nb, pts), (1, 0, 2)).reshape(nb, -1)
    rows = lax.dot_general(density, screened_w, (((1,), (1,)), ((), ())), precision=HIGH)
    rows = jnp.transpose(rows.reshape(nb, ntop, 2, pts), (1, 2, 0, 3)).reshape(ntop, 2 * nb, pts)
    rows = relative(rows, 0, top)
    return [rows[a] for a in range(ntop)]


def gather_kernel(ntop, nin, con_at, val_at, core_ref, *refs):
    tiles, rights, val_refs = refs[:nin], refs[nin:nin + ntop], refs[nin + ntop:]
    nblk, nv, pts = val_refs[0].shape
    core = core_ref[0]
    for g in range(nblk):
        for a in range(ntop):
            array, index = con_at[a * nblk + g]
            high, low = split(tiles[array][index])
            rights[a][pl.ds(3 * g * pts, pts), :] = high
            rights[a][pl.ds((3 * g + 1) * pts, pts), :] = low
            rights[a][pl.ds((3 * g + 2) * pts, pts), :] = high
        array, index = val_at[g]
        for k in range(2):
            val_refs[k][g] = tiles[array][index, pl.ds(pl.multiple_of((core ^ k) * nv, nv), nv), :]


def gathered(aligned, core, after, val, con, nv):
    nblk, ntop = len(val), len(con)
    arrays, at = operands([t for row in con for t in row] + val)
    after, *arrays = lax.optimization_barrier((after, *arrays))
    tiles = [(arrays[i], index) for i, index in at]
    if aligned:
        _, pts, nc = arrays[0].shape
        outs = pl.pallas_call(
            functools.partial(gather_kernel, ntop, len(arrays), at[:nblk * ntop], at[nblk * ntop:]),
            out_shape=[jax.ShapeDtypeStruct((3 * nblk * pts, nc), jnp.bfloat16)] * ntop
            + [jax.ShapeDtypeStruct((nblk, nv, pts), jnp.float32)] * 2,
            in_specs=[SMEM] + [VMEM] * len(arrays),
            out_specs=[VMEM] * (ntop + 2),
            compiler_params=PARAMS,
            cost_estimate=COST,
        )(core.astype(jnp.int32)[None], *arrays)
        return after, outs[ntop:], outs[:ntop]
    tiles = [array[index] for array, index in tiles]
    rows = jnp.stack(tiles[nblk * ntop:]).reshape(nblk, 2, nv, -1)
    vals = [jnp.where(core == k, rows[:, 0], rows[:, 1]) for k in range(2)]
    return after, vals, [jnp.stack(tiles[a * nblk:(a + 1) * nblk]) for a in range(ntop)]


def apply_kernel(nchip, pair_ref, *refs):
    pots, (val_ref, right, out_ref, left) = refs[:nchip], refs[nchip:]
    nb, nv, nc = out_ref.shape
    pts = val_ref.shape[2]
    pair = pair_ref[0]
    for j in range(nchip):
        both = pots[j][...]
        for e in range(2):
            g = e * nchip + j
            pot = jnp.where((pair ^ e) == 0, both[:nb], both[nb:])
            rows = val_ref[g]
            for b in range(nb):
                high, low = split(rows * pot[b:b + 1])
                at = pl.ds(b * nv, nv)
                left[at, pl.ds(3 * g * pts, pts)] = high
                left[at, pl.ds((3 * g + 1) * pts, pts)] = high
                left[at, pl.ds((3 * g + 2) * pts, pts)] = low
    total = jnp.dot(left[...], right[...], preferred_element_type=jnp.float32)
    out_ref[...] = total.reshape(nb, nv, nc)


def applied(aligned, pair, pots, val, con, shape):
    nb, nv, nc = shape
    nblk = val.shape[0]
    nchip = nblk // 2
    pts = pots[0].shape[1]
    if aligned:
        return pl.pallas_call(
            functools.partial(apply_kernel, nchip),
            out_shape=jax.ShapeDtypeStruct(shape, jnp.float32),
            in_specs=[SMEM] + [VMEM] * (nchip + 2),
            out_specs=VMEM,
            scratch_shapes=[pltpu.VMEM((nb * nv, 3 * nblk * pts), jnp.bfloat16)],
            compiler_params=PARAMS,
            cost_estimate=COST,
        )(pair.astype(jnp.int32)[None], *pots, val, con)
    pot = relative(jnp.stack(pots).reshape(nchip, 2, nb, pts), 1, pair)
    pot = jnp.transpose(pot, (1, 0, 2, 3)).reshape(nblk, nb, pts)
    return jnp.einsum("gvp,gbp,gpc->bvc", val.reshape(nblk, nv, pts), pot, con.reshape(nblk, pts, nc), precision=HIGH)


def make(nchip, ntop):
    def rc_swap(x, mask):
        return swap(x, "rc", nchip, mask)

    def top_swap(x, mask):
        return swap(x, "top", ntop, mask)

    def pair_swap(x):
        return swap(x, "pair", 2, 1)

    def core_swap(x):
        return swap(x, "core", 2, 1)

    def col_swap(x, mask):
        n = 2 * ntop
        return lax.ppermute(x, ("top", "pair"), [(i, i ^ mask) for i in range(n)])

    def relay(tiles, j):
        high = 1 << (j.bit_length() - 1)
        low = j & -j
        out = []
        for a in range(ntop):
            mask = low if a % 2 else high
            array, index = tiles[j ^ mask][a]
            out.append((rc_swap(array[index:index + 1], mask), 0))
        return out

    def per_device(x_pairs, eps_val, eps_con, orb_val, orb_con, screened_w):
        rc = lax.axis_index("rc")
        core = lax.axis_index("core")
        top = lax.axis_index("top")
        pair = lax.axis_index("pair")
        nb, nv, nc = x_pairs.shape
        pts = orb_val.shape[0]
        aligned = nc % 128 == 0 and pts == nc and 2 * nv == nc

        packed = pack(nchip, ntop, aligned, rc, top, pair, orb_con, orb_val, nc)
        from_pair = pair_swap(packed[0])
        from_chip = {j: rc_swap(packed[j], j) for j in range(1, nchip)}
        x_tops = [x_pairs] + [top_swap(x_pairs, a) for a in range(1, ntop)]
        x_tops, from_pair, from_chip = lax.optimization_barrier((x_tops, from_pair, from_chip))

        val = [{0: (packed[-1], 0)}, {}]
        con = [{0: [(packed[1], a) for a in range(ntop)]}, {0: [(from_pair, a) for a in range(ntop)]}]
        singles = [j for j in range(1, nchip) if single(j)]
        others = [j for j in range(1, nchip) if not single(j)]
        for j in range(1, nchip):
            val[0][j] = (from_chip[j], from_chip[j].shape[0] - 1)
            if single(j):
                con[0][j] = [(from_chip[j], a) for a in range(ntop)]

        def pair_val(part):
            got = pair_swap(jnp.stack([val[0][j][0][val[0][j][1]] for j in part]))
            for i, j in enumerate(part):
                val[1][j] = (got, i)

        pair_val([0] + singles)
        if nchip == 4:
            con[0][3] = [None] * ntop
            for mask in (2, 1):
                mine = [a for a in range(ntop) if (a % 2 == 0) == (mask == 2)]
                tiles = [con[0][3 ^ mask][a] for a in mine] + con[1][0]
                got = rc_swap(jnp.stack([array[index] for array, index in tiles]), mask)
                for i, a in enumerate(mine):
                    con[0][3][a] = (got, i)
                con[1][mask] = [(got, len(mine) + a) for a in range(ntop)]
        else:
            for j in others:
                con[0][j] = relay(con[0], j)
            for j in singles:
                got = rc_swap(from_pair, j)
                con[1][j] = [(got, a) for a in range(ntop)]

        x = [[t, core_swap(t)] for t in x_tops]
        if aligned:
            x = halves(x)
        else:
            x = [jnp.where(core == 0, jnp.stack(row, 1), jnp.stack(row[::-1], 1)) for row in x]

        def density(group):
            return densities(
                aligned, core, x_pairs.shape, x, [con[e][j] for e, j in group], [val[e][j] for e, j in group]
            )

        groups = [[(0, 0)] + [(0, j) for j in singles]]
        dens = [density(groups[0])]
        if others:
            arrays = [con[1][j][0][0] for j in singles] + [val[0][j][0] for j in others]
            dens[0], arrays = ordered(dens[0], arrays)
            con[1].update({j: [(arrays[i], index) for _, index in con[1][j]] for i, j in enumerate(singles)})
            for i, j in enumerate(others):
                val[0][j] = (arrays[len(singles) + i], val[0][j][1])
            for j in others:
                con[1][j] = relay(con[1], j)
            pair_val(others)
        groups += [
            [(0, j) for j in others],
            [(1, 0)] + [(1, j) for j in singles],
            [(1, j) for j in others],
        ]
        groups = [group for group in groups if group]
        dens += [density(group) for group in groups[1:]]
        order = [e * nchip + j for group in groups for e, j in group]
        part = route(aligned, nchip, rc, pair, order, dens)
        got = lax.all_to_all(part, ("rc", "core", "top", "pair"), 0, 0, tiled=True)
        rows = screen(aligned, nchip, ntop, top, got, screened_w)
        vals = [val[e][j] for e in range(2) for j in range(nchip)]
        cons = [[con[e][j][a] for e in range(2) for j in range(nchip)] for a in range(ntop)]
        rows = list(rows)
        rows[0], vals, cons = gathered(aligned, core, rows[0], vals, cons, nv)
        row = rows[0]
        for d in range(1, 2 * ntop):
            row = row + col_swap(rows[d // 2], d)
        pots = [row] + [rc_swap(row, j) for j in range(1, nchip)]

        def apply(a, k):
            return applied(aligned, pair, pots, vals[k], cons[a], x_pairs.shape)

        base = (eps_con[None, None, :] - eps_val[None, :, None]) * x_pairs
        for a in list(range(1, ntop)) + [0]:
            away, step = apply(a, 1), apply(a, 0)
            if a:
                step, pots[0] = lax.optimization_barrier((step + core_swap(away), pots[0]))
                base = base + top_swap(step, a)
        return lax.optimization_barrier(base) + step + core_swap(away)

    return per_device


def solution(mesh):
    nrow, ncol = mesh.shape["rowpt"], mesh.shape["colpt"]
    nchip, ntop = nrow // 2, ncol // 2
    fine = Mesh(mesh.devices.reshape(nchip, 2, ntop, 2), ("rc", "core", "top", "pair"))
    row, col = ("rc", "core"), ("top", "pair")
    in_specs = (P(None, row, col), P(row), P(col), P(row + col, None), P(row + col, None), P(row, col))
    return jax.shard_map(
        make(nchip, ntop), mesh=fine, in_specs=in_specs, out_specs=P(None, row, col), check_vma=False
    )
```

time: 143 us -> 130 us (0.909)
  blocking collectives: 0 us -> 13.8 us
  local copies, waits for them, and re-layouts: 12 us -> 2.6 us
  starting transfers between devices: 30.2 us -> 21.9 us
  waiting for transfers between devices: 69.5 us -> 62.3 us
  matrix products: 7.03 us -> 0 us
  Pallas kernels: 20.2 us -> 23.7 us
    all_to_all x0 -> x1, blocking collectives: none -> 13.8 us  [per_device(): got = lax.all_to_all(part, ('rc', 'core', 'top', 'pair'), 0, 0, tiled=True)]
    unnamed x60 -> x24, local copies, waits for them, and re-layouts: 9.89 us -> 2.5 us
    dot_general x1 -> x0, matrix products: 7.03 us -> none  [per_device(): lax.dot_general(density, screened_w, (((1,), (1,)), ((), ())), precision=...]
    ppermute x6 -> x3, starting transfers between devices: 8.95 us -> 4.4 us  [col_swap(): return lax.ppermute(x, ('top', 'pair'), [(i, i ^ mask) for i in range(n)])]
    ppermute x22 -> x19, starting transfers between devices: 21.2 us -> 17.5 us  [swap(): return lax.ppermute(x, axis, [(i, i ^ mask) for i in range(size)])]
    ppermute x6 -> x3, waiting for transfers between devices: 7.06 us -> 3.38 us  [col_swap(): return lax.ppermute(x, ('top', 'pair'), [(i, i ^ mask) for i in range(n)])]
    ppermute x22 -> x19, waiting for transfers between devices: 62.5 us -> 58.9 us  [swap(): return lax.ppermute(x, axis, [(i, i ^ mask) for i in range(size)])]
    pallas_call x7 -> x12, Pallas kernels: 19.3 us -> 22.8 us  [the longest x4 8.52 us: densities(): pl.pallas_call(functools.partial(density_kernel, nblk, ntop, shape, at[:n...]
  transfers between devices with their start and end apart: 28 -> 22, of which waited for: 16 -> 12; matrix products, arithmetic and copies ran while one was open for 3% -> 3% of each run, Pallas kernels for 9% -> 13%
where the time goes in v3:
time: 130 us; the launch traced here: 129 us
  waiting for transfers between devices  62.3 us (48%)
  Pallas kernels  23.7 us (18%)
  starting transfers between devices  21.9 us (17%)
  blocking collectives  13.8 us (11%)
  other arithmetic  4.56 us (4%)
  local copies, waits for them, and re-layouts  2.6 us (2%)
    ppermute x19, waiting for transfers between devices, swap(): return lax.ppermute(x, axis, [(i, i ^ mask) for i in range(size)])  58.9 us
    ppermute x19, starting transfers between devices, swap(): return lax.ppermute(x, axis, [(i, i ^ mask) for i in range(size)])  17.5 us
    all_to_all x1, blocking collectives, per_device(): got = lax.all_to_all(part, ('rc', 'core', 'top', 'pair'), 0, 0, tiled=True)  13.8 us
    pallas_call x4, Pallas kernels, densities(): pl.pallas_call(functools.partial(density_kernel, nblk, ntop, shape, at[:n...  8.52 us
    pallas_call x4, Pallas kernels, applied(): pl.pallas_call(functools.partial(apply_kernel, nchip), out_shape=jax.Shap...  7.36 us
    ppermute x3, starting transfers between devices, col_swap(): return lax.ppermute(x, ('top', 'pair'), [(i, i ^ mask) for i in range(n)])  4.4 us
    ppermute x3, waiting for transfers between devices, col_swap(): return lax.ppermute(x, ('top', 'pair'), [(i, i ^ mask) for i in range(n)])  3.38 us
  transfers between devices with their start and end apart: 22, of which 12 were waited for; matrix products, arithmetic and copies ran while one was open for 3% of the time, Pallas kernels for 13%

profile of v3, /device:TPU:0, one launch (start us, length us, event | category | flops | bytes accessed | tf_op | source)
XLA Modules:
  0.0 129.2 jit_solution(924292848915162200)
XLA Ops:
  0.0 0.1 pad_add_fusion.1.where
  0.1 1.2 copy-done.6
  1.3 1.2 copy-done.7
  2.5 0.9 shard_map.64
  3.5 3.0 %collective-permute-start.2 = (f32[3,256,256]{2,1,0:T(8,128)S(1)}, f32[3,256,256]{2,1,0:T(8,128)S(1)}, u32[]{:S(2)}, u32[]{:S(2)}) collective-permute-start(f32[3,256,256]{2,1,0:T(8,128)S(1)} %get-tuple-element.61.refs_0_), channel_id=1, source_target_pairs={{0,8},{8,0},{16,24},{24,16},{1,9},{9,1},{17,25},{25,17},{2,10},{10... | collective-permute-start | bytes 2359304 | tf_op jit(solution)/shard_map/ppermute | solution.py:19
  6.5 1.5 %collective-permute-start.3 = (f32[3,256,256]{2,1,0:T(8,128)S(1)}, f32[3,256,256]{2,1,0:T(8,128)S(1)}, u32[]{:S(2)}, u32[]{:S(2)}) collective-permute-start(f32[3,256,256]{2,1,0:T(8,128)S(1)} %get-tuple-element.45), channel_id=1, source_target_pairs={{0,16},{8,24},{16,0},{24,8},{1,17},{9,25},{17,1},{25,9},{2,18},{10... | collective-permute-start | bytes 2359304 | tf_op jit(solution)/shard_map/ppermute | solution.py:19
  8.0 1.6 %collective-permute-start.1 = (f32[2,256,256]{2,1,0:T(8,128)S(1)}, f32[2,256,256]{2,1,0:T(8,128)S(1)}, u32[]{:S(2)}, u32[]{:S(2)}) collective-permute-start(f32[2,256,256]{2,1,0:T(8,128)S(1)} %get-tuple-element.43), channel_id=1, source_target_pairs={{0,1},{1,0},{2,3},{3,2},{4,5},{5,4},{6,7},{7,6},{8,9},{9,8},{10,11... | collective-permute-start | bytes 1572872 | tf_op jit(solution)/shard_map/ppermute | solution.py:19
  9.6 2.6 %collective-permute-start = (f32[4,128,256]{2,1,0:T(8,128)}, f32[4,128,256]{2,1,0:T(8,128)}, u32[]{:S(2)}, u32[]{:S(2)}) collective-permute-start(f32[4,128,256]{2,1,0:T(8,128)} %refs_0_), channel_id=1, source_target_pairs={{0,2},{2,0},{1,3},{3,1},{4,6},{6,4},{5,7},{7,5},{8,10},{10,8},{9,1... | collective-permute-start | bytes 1572872 | tf_op jit(solution)/shard_map/ppermute | solution.py:19
  12.1 0.5 collective-permute-start.4
  12.6 18.3 %collective-permute-done.4.refs_2_.refs_11_ = f32[1,256,256]{2,1,0:T(8,128)S(1)} collective-permute-done((f32[1,256,256]{2,1,0:T(8,128)S(1)}, f32[1,256,256]{2,1,0:T(8,128)S(1)}, u32[]{:S(2)}, u32[]{:S(2)}) %collective-permute-start.4) | collective-permute-done | bytes 262176 | tf_op jit(solution)/shard_map/ppermute | solution.py:19
  30.9 1.1 collective-permute-done.1.refs_0_.refs_4_
  32.0 2.9 %collective-permute-done.refs_2_ = f32[4,128,256]{2,1,0:T(8,128)} collective-permute-done((f32[4,128,256]{2,1,0:T(8,128)}, f32[4,128,256]{2,1,0:T(8,128)}, u32[]{:S(2)}, u32[]{:S(2)}) %collective-permute-start) | collective-permute-done | bytes 524320 | tf_op jit(solution)/shard_map/ppermute | solution.py:19
  34.9 0.0 collective-permute-start.5
  34.9 0.5 collective-permute-start.6
  35.4 0.1 fusion
  35.5 1.3 %pad_maximum_fusion = (f32[3,256,256]{2,1,0:T(8,128)}, f32[3,256,256]{2,1,0:T(8,128)}) fusion(f32[2,256,256]{2,1,0:T(8,128)S(1)} %collective-permute-done.1.refs_0_.refs_4_, f32[1,256,256]{2,1,0:T(8,128)S(1)} %get-tuple-element.82, f32[1,256,256]{2,1,0:T(8,128)S(1)} %get-tuple-element.87), kind=kLoop, calls=%fused_computation | loop fusion | flops 393216 | bytes 2621440 | tf_op jit(solution)/shard_map/stack | solution.py:405
  36.8 0.5 collective-permute-start.7
  37.3 0.5 collective-permute-start.8
  37.8 0.9 pad_maximum_fusion.2
  38.8 0.3 collective-permute-start.9
  39.0 0.1 pad_add_fusion.where
  39.1 2.0 %shard_map.65.x_ref = bf16[1024,1024]{1,0:T(8,128)(2,1)S(1)} custom-call(f32[4,128,256]{2,1,0:T(8,128)} %refs_0_, f32[4,128,256]{2,1,0:T(8,128)} %collective-permute-done.5.refs_1_, f32[4,128,256]{2,1,0:T(8,128)} %collective-permute-done.refs_2_, f32[4,128,256]{2,1,0:T(8,128)} %collective-permute-done.6.refs_3_), custom_call_target="tpu_custom_call" | custom-call | flops 2000000000 | bytes 4194304 | tf_op jit(solution)/shard_map/pallas_call | solution.py:118
  41.2 2.7 %shard_map.66.refs_0_ = f32[3,4,256]{2,1,0:T(4,128)S(1)} custom-call(s32[1]{0:T(128)} %bitcast.3.core_ref, bf16[1024,1024]{1,0:T(8,128)(2,1)S(1)} %shard_map.65.x_ref, f32[3,256,256]{2,1,0:T(8,128)S(1)} %copy-done.3, f32[3,256,256]{2,1,0:T(8,128)S(1)} %collective-permute-done.2.refs_1_, f32[3,256,256]{2,1,0:T(8,128)S(1)} %collective-permute-done.3.refs_2_, ...), custom_call_target="tpu_custom_call" | custom-call | flops 2000000000 | bytes 4194304 | tf_op jit(solution)/shard_map/pallas_call | solution.py:160
  43.8 12.7 %collective-permute-done.7.refs_1_.refs_5_.refs_8_ = f32[3,256,256]{2,1,0:T(8,128)S(1)} collective-permute-done((f32[3,256,256]{2,1,0:T(8,128)}, f32[3,256,256]{2,1,0:T(8,128)S(1)}, u32[]{:S(2)}, u32[]{:S(2)}) %collective-permute-start.7) | collective-permute-done | bytes 786464 | tf_op jit(solution)/shard_map/ppermute | solution.py:19
  56.5 0.3 collective-permute-done.8.refs_0_.refs_2_.refs_3_.refs_6_
  56.8 0.6 collective-permute-start.10
  57.4 0.0 copy-start.1
  57.4 1.6 %collective-permute-start.11 = (f32[1,256,256]{2,1,0:T(8,128)S(1)}, f32[1,256,256]{2,1,0:T(8,128)S(1)}, u32[]{:S(2)}, u32[]{:S(2)}) collective-permute-start(f32[1,256,256]{2,1,0:T(8,128)S(1)} %slice.29), channel_id=1, source_target_pairs={{0,8},{8,0},{16,24},{24,16},{1,9},{9,1},{17,25},{25,17},{2,10},{10... | collective-permute-start | bytes 786440 | tf_op jit(solution)/shard_map/ppermute | solution.py:19
  58.9 0.2 collective-permute-start.12
  59.2 1.0 shard_map.67.refs_1_
  60.2 3.8 %shard_map.68.refs_2_ = f32[3,4,256]{2,1,0:T(4,128)S(1)} custom-call(s32[1]{0:T(128)} %bitcast.3.core_ref, bf16[1024,1024]{1,0:T(8,128)(2,1)S(1)} %shard_map.65.x_ref, f32[2,256,256]{2,1,0:T(8,128)S(1)} %copy-done.1, f32[3,256,256]{2,1,0:T(8,128)S(1)} %collective-permute-done.7.refs_1_.refs_5_.refs_8_, ...), custom_call_target="tpu_custom_call" | custom-call | flops 2000000000 | bytes 4194304 | tf_op jit(solution)/shard_map/pallas_call | solution.py:160
  64.0 0.1 collective-permute-done.10.refs_0_.refs_7_
  64.1 0.3 collective-permute-done.11.refs_1_.refs_9_
  64.5 1.1 collective-permute-done.12.refs_2_.refs_13_
  65.6 1.0 shard_map.69.refs_3_
  66.7 0.0 slice-start.1
  66.7 0.6 shard_map.70
  67.3 13.8 %all_to_all.5.got_ref = f32[32,8,256]{2,1,0:T(8,128)S(1)} all-to-all(f32[32,8,256]{2,1,0:T(8,128)S(1)} %shard_map.70), channel_id=1, replica_groups=mesh['rc'=4,'core'=2,'top'=2,'pair'=2] {'rc','core','top','pair'}, dimensions={0} | all-to-all | bytes 524288 | tf_op jit(solution)/shard_map/all_to_all | solution.py:447
  81.1 2.3 %shard_map.71 = (f32[8,256]{1,0:T(8,128)S(1)}, f32[8,256]{1,0:T(8,128)S(1)}) custom-call(s32[1]{0:T(128)} %bitcast.1.top_ref, f32[32,8,256]{2,1,0:T(8,128)S(1)} %all_to_all.5.got_ref, f32[1024,2048]{1,0:T(8,128)S(1)} %bitcast.5), custom_call_target="tpu_custom_call" | custom-call | flops 2000000000 | bytes 4194304 | tf_op jit(solution)/shard_map/pallas_call | solution.py:246
  83.4 1.1 collective-permute-start.13
  84.5 1.2 collective-permute-start.14
  85.7 2.1 %collective-permute-start.15 = (f32[8,256]{1,0:T(8,128)S(1)}, f32[8,256]{1,0:T(8,128)S(1)}, u32[]{:S(2)}, u32[]{:S(2)}) collective-permute-start(f32[8,256]{1,0:T(8,128)S(1)} %get-tuple-element.60), channel_id=1, source_target_pairs={{0,3},{1,2},{2,1},{3,0},{4,7},{5,6},{6,5},{7,4},{8,11},{9,10},{10,... | collective-permute-start | bytes 24584 | tf_op jit(solution)/shard_map/ppermute | solution.py:358
  87.8 1.3 collective-permute-done.14
  89.1 2.1 %collective-permute-done.15 = f32[8,256]{1,0:T(8,128)S(1)} collective-permute-done((f32[8,256]{1,0:T(8,128)S(1)}, f32[8,256]{1,0:T(8,128)S(1)}, u32[]{:S(2)}, u32[]{:S(2)}) %collective-permute-start.15) | collective-permute-done | bytes 8224 | tf_op jit(solution)/shard_map/ppermute | solution.py:358
  91.2 1.2 collective-permute-start.16
  92.4 0.4 collective-permute-start.17
  92.8 1.9 %collective-permute-start.18 = (f32[8,256]{1,0:T(8,128)S(1)}, f32[8,256]{1,0:T(8,128)S(1)}, u32[]{:S(2)}, u32[]{:S(2)}) collective-permute-start(f32[8,256]{1,0:T(8,128)S(1)} %add_add_fusion.1.refs_0_), channel_id=1, source_target_pairs={{0,24},{8,16},{16,8},{24,0},{1,25},{9,17},{17,9},{25,1},{2,26},{10... | collective-permute-start | bytes 24584 | tf_op jit(solution)/shard_map/ppermute | solution.py:19
  94.7 2.0 %shard_map.72 = (bf16[6144,256]{1,0:T(8,128)(2,1)S(1)}, bf16[6144,256]{1,0:T(8,128)(2,1)S(1)}, f32[8,128,256]{2,1,0:T(8,128)S(1)}, f32[8,128,256]{2,1,0:T(8,128)S(1)}) custom-call(s32[1]{0:T(128)} %bitcast.3.core_ref, f32[3,256,256]{2,1,0:T(8,128)S(1)} %copy-done.3, f32[3,256,256]{2,1,0:T(8,128)S(1)} %collective-permute-done.2.refs_1_, ...), custom_call_target="tpu_custom_call" | custom-call | flops 2000000000 | bytes 4194304 | tf_op jit(solution)/shard_map/pallas_call | solution.py:286
  96.8 0.6 collective-permute-done.18.refs_3_
  97.4 1.8 %shard_map.74 = f32[4,128,256]{2,1,0:T(8,128)S(1)} custom-call(s32[1]{0:T(128)} %bitcast.pair_ref, f32[8,256]{1,0:T(8,128)S(1)} %add_add_fusion.1.refs_0_, f32[8,256]{1,0:T(8,128)S(1)} %collective-permute-done.16.refs_1_, f32[8,256]{1,0:T(8,128)S(1)} %collective-permute-done.17.refs_2_, f32[8,256]{1,0:T(8,128)S(1)} %collective-permute-done.18.refs_3_, ...), custom_call_target="tpu_custom_call" | custom-call | flops 2000000000 | bytes 4194304 | tf_op jit(solution)/shard_map/pallas_call | solution.py:329
  99.2 0.1 collective-permute-start.19
  99.3 1.9 %shard_map.73 = f32[4,128,256]{2,1,0:T(8,128)S(1)} custom-call(s32[1]{0:T(128)} %bitcast.pair_ref, f32[8,256]{1,0:T(8,128)S(1)} %add_add_fusion.1.refs_0_, f32[8,256]{1,0:T(8,128)S(1)} %collective-permute-done.16.refs_1_, f32[8,256]{1,0:T(8,128)S(1)} %collective-permute-done.17.refs_2_, f32[8,256]{1,0:T(8,128)S(1)} %collective-permute-done.18.refs_3_, ...), custom_call_target="tpu_custom_call" | custom-call | flops 2000000000 | bytes 4194304 | tf_op jit(solution)/shard_map/pallas_call | solution.py:329
  101.1 0.0 collective-permute-done.19
  101.2 0.1 add.24
  101.2 0.1 collective-permute-start.20
  101.3 0.0 copy-start.8
  101.3 0.0 copy-start.9
  101.3 1.8 %shard_map.76 = f32[4,128,256]{2,1,0:T(8,128)S(1)} custom-call(s32[1]{0:T(128)} %bitcast.pair_ref, f32[8,256]{1,0:T(8,128)S(1)} %add_add_fusion.1.refs_0_, f32[8,256]{1,0:T(8,128)S(1)} %collective-permute-done.16.refs_1_, f32[8,256]{1,0:T(8,128)S(1)} %collective-permute-done.17.refs_2_, f32[8,256]{1,0:T(8,128)S(1)} %collective-permute-done.18.refs_3_, ...), custom_call_target="tpu_custom_call" | custom-call | flops 2000000000 | bytes 4194304 | tf_op jit(solution)/shard_map/pallas_call | solution.py:329
  103.2 0.5 collective-permute-start.21
  103.7 0.1 broadcast_subtract_fusion
  103.8 1.9 %shard_map.75 = f32[4,128,256]{2,1,0:T(8,128)S(1)} custom-call(s32[1]{0:T(128)} %bitcast.pair_ref, f32[8,256]{1,0:T(8,128)S(1)} %add_add_fusion.1.refs_0_, f32[8,256]{1,0:T(8,128)S(1)} %collective-permute-done.16.refs_1_, f32[8,256]{1,0:T(8,128)S(1)} %collective-permute-done.17.refs_2_, f32[8,256]{1,0:T(8,128)S(1)} %collective-permute-done.18.refs_3_, ...), custom_call_target="tpu_custom_call" | custom-call | flops 2000000000 | bytes 4194304 | tf_op jit(solution)/shard_map/pallas_call | solution.py:329
  105.7 21.4 %collective-permute-done.20 = f32[4,128,256]{2,1,0:T(8,128)S(1)} collective-permute-done((f32[4,128,256]{2,1,0:T(8,128)S(1)}, f32[4,128,256]{2,1,0:T(8,128)S(1)}, u32[]{:S(2)}, u32[]{:S(2)}) %collective-permute-start.20) | collective-permute-done | bytes 524320 | tf_op jit(solution)/shard_map/ppermute | solution.py:19
  127.1 1.1 multiply_add_fusion
  128.3 0.9 add_add_fusion
  (31 shorter events, 0.1 us)
Async XLA Ops:
  0.1 1.2 copy-start.6
  1.3 1.2 copy-start.7
  3.4 35.3 %copy-start.2 = (f32[3,256,256]{2,1,0:T(8,128)}, f32[3,256,256]{2,1,0:T(8,128)S(1)}, u32[]{:S(2)}) copy-start(f32[3,256,256]{2,1,0:T(8,128)S(1)} %get-tuple-element.61.refs_0_) | copy-start | bytes 2359300
  3.5 31.4 %collective-permute-start.2 = (f32[3,256,256]{2,1,0:T(8,128)S(1)}, f32[3,256,256]{2,1,0:T(8,128)S(1)}, u32[]{:S(2)}, u32[]{:S(2)}) collective-permute-start(f32[3,256,256]{2,1,0:T(8,128)S(1)} %get-tuple-element.61.refs_0_), channel_id=1, source_target_pairs={{0,8},{8,0},{16,24},{24,16},{1,9},{9,1},{17,25},{25,17},{2,10},{10... | collective-permute-start | bytes 2359304 | tf_op jit(solution)/shard_map/ppermute | solution.py:19
  6.5 28.4 %collective-permute-start.3 = (f32[3,256,256]{2,1,0:T(8,128)S(1)}, f32[3,256,256]{2,1,0:T(8,128)S(1)}, u32[]{:S(2)}, u32[]{:S(2)}) collective-permute-start(f32[3,256,256]{2,1,0:T(8,128)S(1)} %get-tuple-element.45), channel_id=1, source_target_pairs={{0,16},{8,24},{16,0},{24,8},{1,17},{9,25},{17,1},{25,9},{2,18},{10... | collective-permute-start | bytes 2359304 | tf_op jit(solution)/shard_map/ppermute | solution.py:19
  8.0 24.0 %collective-permute-start.1 = (f32[2,256,256]{2,1,0:T(8,128)S(1)}, f32[2,256,256]{2,1,0:T(8,128)S(1)}, u32[]{:S(2)}, u32[]{:S(2)}) collective-permute-start(f32[2,256,256]{2,1,0:T(8,128)S(1)} %get-tuple-element.43), channel_id=1, source_target_pairs={{0,1},{1,0},{2,3},{3,2},{4,5},{5,4},{6,7},{7,6},{8,9},{9,8},{10,11... | collective-permute-start | bytes 1572872 | tf_op jit(solution)/shard_map/ppermute | solution.py:19
  9.6 25.3 %collective-permute-start = (f32[4,128,256]{2,1,0:T(8,128)}, f32[4,128,256]{2,1,0:T(8,128)}, u32[]{:S(2)}, u32[]{:S(2)}) collective-permute-start(f32[4,128,256]{2,1,0:T(8,128)} %refs_0_), channel_id=1, source_target_pairs={{0,2},{2,0},{1,3},{3,1},{4,6},{6,4},{5,7},{7,5},{8,10},{10,8},{9,1... | collective-permute-start | bytes 1572872 | tf_op jit(solution)/shard_map/ppermute | solution.py:19
  12.1 18.8 %collective-permute-start.4 = (f32[1,256,256]{2,1,0:T(8,128)S(1)}, f32[1,256,256]{2,1,0:T(8,128)S(1)}, u32[]{:S(2)}, u32[]{:S(2)}) collective-permute-start(f32[1,256,256]{2,1,0:T(8,128)S(1)} %get-tuple-element.46), channel_id=1, source_target_pairs={{0,24},{8,16},{16,8},{24,0},{1,25},{9,17},{17,9},{25,1},{2,26},{10... | collective-permute-start | bytes 786440 | tf_op jit(solution)/shard_map/ppermute | solution.py:19
  30.9 7.8 %copy-start.4 = (f32[1,256,256]{2,1,0:T(8,128)}, f32[1,256,256]{2,1,0:T(8,128)S(1)}, u32[]{:S(2)}) copy-start(f32[1,256,256]{2,1,0:T(8,128)S(1)} %collective-permute-done.4.refs_2_.refs_11_) | copy-start | bytes 786436
  32.0 6.8 %copy-start = (f32[2,256,256]{2,1,0:T(8,128)}, f32[2,256,256]{2,1,0:T(8,128)S(1)}, u32[]{:S(2)}) copy-start(f32[2,256,256]{2,1,0:T(8,128)S(1)} %collective-permute-done.1.refs_0_.refs_4_) | copy-start | bytes 1572868
  34.9 4.2 %collective-permute-start.5 = (f32[4,128,256]{2,1,0:T(8,128)}, f32[4,128,256]{2,1,0:T(8,128)}, u32[]{:S(2)}, u32[]{:S(2)}) collective-permute-start(f32[4,128,256]{2,1,0:T(8,128)} %refs_0_), channel_id=1, source_target_pairs={{0,4},{4,0},{1,5},{5,1},{2,6},{6,2},{3,7},{7,3},{8,12},{12,8},{9,1... | collective-permute-start | bytes 1572872 | tf_op jit(solution)/shard_map/ppermute | solution.py:19
  34.9 4.2 %collective-permute-start.6 = (f32[4,128,256]{2,1,0:T(8,128)}, f32[4,128,256]{2,1,0:T(8,128)}, u32[]{:S(2)}, u32[]{:S(2)}) collective-permute-start(f32[4,128,256]{2,1,0:T(8,128)} %collective-permute-done.refs_2_), channel_id=1, source_target_pairs={{0,4},{4,0},{1,5},{5,1},{2,6},{6,2},{3,7},{7,3},{8,12},{12,8},{9,1... | collective-permute-start | bytes 1572872 | tf_op jit(solution)/shard_map/ppermute | solution.py:19
  36.8 19.7 %collective-permute-start.7 = (f32[3,256,256]{2,1,0:T(8,128)}, f32[3,256,256]{2,1,0:T(8,128)S(1)}, u32[]{:S(2)}, u32[]{:S(2)}) collective-permute-start(f32[3,256,256]{2,1,0:T(8,128)} %get-tuple-element.86), channel_id=1, source_target_pairs={{0,8},{8,0},{16,24},{24,16},{1,9},{9,1},{17,25},{25,17},{2,10},{10... | collective-permute-start | bytes 2359304 | tf_op jit(solution)/shard_map/ppermute | solution.py:19
  37.3 19.5 %collective-permute-start.8 = (f32[3,256,256]{2,1,0:T(8,128)}, f32[3,256,256]{2,1,0:T(8,128)S(1)}, u32[]{:S(2)}, u32[]{:S(2)}) collective-permute-start(f32[3,256,256]{2,1,0:T(8,128)} %get-tuple-element.85), channel_id=1, source_target_pairs={{0,16},{8,24},{16,0},{24,8},{1,17},{9,25},{17,1},{25,9},{2,18},{10... | collective-permute-start | bytes 2359304 | tf_op jit(solution)/shard_map/ppermute | solution.py:19
  38.8 21.5 %collective-permute-start.9 = (f32[3,256,256]{2,1,0:T(8,128)}, f32[3,256,256]{2,1,0:T(8,128)}, u32[]{:S(2)}, u32[]{:S(2)}) collective-permute-start(f32[3,256,256]{2,1,0:T(8,128)} %pad_maximum_fusion.2), channel_id=1, source_target_pairs={{0,1},{1,0},{2,3},{3,2},{4,5},{5,4},{6,7},{7,6},{8,9},{9,8},{10,11... | collective-permute-start | bytes 2359304 | tf_op jit(solution)/shard_map/ppermute | solution.py:19
  39.1 2.0 %copy-start.3 = (f32[3,256,256]{2,1,0:T(8,128)S(1)}, f32[3,256,256]{2,1,0:T(8,128)}, u32[]{:S(2)}) copy-start(f32[3,256,256]{2,1,0:T(8,128)} %copy-done.2) | copy-start | bytes 2359300
  41.1 17.8 %copy-start.5 = (f32[1,256,256]{2,1,0:T(8,128)S(1)}, f32[1,256,256]{2,1,0:T(8,128)}, u32[]{:S(2)}) copy-start(f32[1,256,256]{2,1,0:T(8,128)} %copy-done.4) | copy-start | bytes 786436
  56.8 7.4 %collective-permute-start.10 = (f32[1,256,256]{2,1,0:T(8,128)S(1)}, f32[1,256,256]{2,1,0:T(8,128)S(1)}, u32[]{:S(2)}, u32[]{:S(2)}) collective-permute-start(f32[1,256,256]{2,1,0:T(8,128)S(1)} %slice.28), channel_id=1, source_target_pairs={{0,16},{8,24},{16,0},{24,8},{1,17},{9,25},{17,1},{25,9},{2,18},{10... | collective-permute-start | bytes 786440 | tf_op jit(solution)/shard_map/ppermute | solution.py:19
  57.4 2.8 %copy-start.1 = (f32[2,256,256]{2,1,0:T(8,128)S(1)}, f32[2,256,256]{2,1,0:T(8,128)}, u32[]{:S(2)}) copy-start(f32[2,256,256]{2,1,0:T(8,128)} %copy-done) | copy-start | bytes 1572868
  57.4 7.1 %collective-permute-start.11 = (f32[1,256,256]{2,1,0:T(8,128)S(1)}, f32[1,256,256]{2,1,0:T(8,128)S(1)}, u32[]{:S(2)}, u32[]{:S(2)}) collective-permute-start(f32[1,256,256]{2,1,0:T(8,128)S(1)} %slice.29), channel_id=1, source_target_pairs={{0,8},{8,0},{16,24},{24,16},{1,9},{9,1},{17,25},{25,17},{2,10},{10... | collective-permute-start | bytes 786440 | tf_op jit(solution)/shard_map/ppermute | solution.py:19
  58.9 6.7 %collective-permute-start.12 = (f32[1,256,256]{2,1,0:T(8,128)S(1)}, f32[1,256,256]{2,1,0:T(8,128)S(1)}, u32[]{:S(2)}, u32[]{:S(2)}) collective-permute-start(f32[1,256,256]{2,1,0:T(8,128)S(1)} %copy-done.5), channel_id=1, source_target_pairs={{0,1},{1,0},{2,3},{3,2},{4,5},{5,4},{6,7},{7,6},{8,9},{9,8},{10,11... | collective-permute-start | bytes 786440 | tf_op jit(solution)/shard_map/ppermute | solution.py:19
  65.6 15.5 %slice-start = ((s8[8388608]{0:T(1024)(128)(4,1)}), s8[4194304]{0:T(1024)(128)(4,1)S(1)}, s32[]{:S(2)}) async-start(s8[8388608]{0:T(1024)(128)(4,1)} %bitcast.4), calls=%async_computation.1 | async-start | bytes 8388608
  66.7 14.4 %slice-start.1 = ((s8[8388608]{0:T(1024)(128)(4,1)}), s8[4194304]{0:T(1024)(128)(4,1)S(1)}, s32[]{:S(2)}) async-start(s8[8388608]{0:T(1024)(128)(4,1)} %bitcast.4), calls=%async_computation.2 | async-start | bytes 8388608
  83.4 4.4 %collective-permute-start.13 = (f32[8,256]{1,0:T(8,128)S(1)}, f32[8,256]{1,0:T(8,128)S(1)}, u32[]{:S(2)}, u32[]{:S(2)}) collective-permute-start(f32[8,256]{1,0:T(8,128)S(1)} %get-tuple-element.59), channel_id=1, source_target_pairs={{0,1},{1,0},{2,3},{3,2},{4,5},{5,4},{6,7},{7,6},{8,9},{9,8},{10,11... | collective-permute-start | bytes 24584 | tf_op jit(solution)/shard_map/ppermute | solution.py:358
  84.5 4.5 %collective-permute-start.14 = (f32[8,256]{1,0:T(8,128)S(1)}, f32[8,256]{1,0:T(8,128)S(1)}, u32[]{:S(2)}, u32[]{:S(2)}) collective-permute-start(f32[8,256]{1,0:T(8,128)S(1)} %get-tuple-element.60), channel_id=1, source_target_pairs={{0,2},{1,3},{2,0},{3,1},{4,6},{5,7},{6,4},{7,5},{8,10},{9,11},{10,... | collective-permute-start | bytes 24584 | tf_op jit(solution)/shard_map/ppermute | solution.py:358
  85.7 5.4 %collective-permute-start.15 = (f32[8,256]{1,0:T(8,128)S(1)}, f32[8,256]{1,0:T(8,128)S(1)}, u32[]{:S(2)}, u32[]{:S(2)}) collective-permute-start(f32[8,256]{1,0:T(8,128)S(1)} %get-tuple-element.60), channel_id=1, source_target_pairs={{0,3},{1,2},{2,1},{3,0},{4,7},{5,6},{6,5},{7,4},{8,11},{9,10},{10,... | collective-permute-start | bytes 24584 | tf_op jit(solution)/shard_map/ppermute | solution.py:358
  91.2 5.5 %collective-permute-start.16 = (f32[8,256]{1,0:T(8,128)S(1)}, f32[8,256]{1,0:T(8,128)S(1)}, u32[]{:S(2)}, u32[]{:S(2)}) collective-permute-start(f32[8,256]{1,0:T(8,128)S(1)} %add_add_fusion.1.refs_0_), channel_id=1, source_target_pairs={{0,8},{8,0},{16,24},{24,16},{1,9},{9,1},{17,25},{25,17},{2,10},{10... | collective-permute-start | bytes 24584 | tf_op jit(solution)/shard_map/ppermute | solution.py:19
  92.4 4.4 %collective-permute-start.17 = (f32[8,256]{1,0:T(8,128)S(1)}, f32[8,256]{1,0:T(8,128)S(1)}, u32[]{:S(2)}, u32[]{:S(2)}) collective-permute-start(f32[8,256]{1,0:T(8,128)S(1)} %add_add_fusion.1.refs_0_), channel_id=1, source_target_pairs={{0,16},{8,24},{16,0},{24,8},{1,17},{9,25},{17,1},{25,9},{2,18},{10... | collective-permute-start | bytes 24584 | tf_op jit(solution)/shard_map/ppermute | solution.py:19
  92.8 4.5 %collective-permute-start.18 = (f32[8,256]{1,0:T(8,128)S(1)}, f32[8,256]{1,0:T(8,128)S(1)}, u32[]{:S(2)}, u32[]{:S(2)}) collective-permute-start(f32[8,256]{1,0:T(8,128)S(1)} %add_add_fusion.1.refs_0_), channel_id=1, source_target_pairs={{0,24},{8,16},{16,8},{24,0},{1,25},{9,17},{17,9},{25,1},{2,26},{10... | collective-permute-start | bytes 24584 | tf_op jit(solution)/shard_map/ppermute | solution.py:19
  99.2 2.0 %collective-permute-start.19 = (f32[4,128,256]{2,1,0:T(8,128)S(1)}, f32[4,128,256]{2,1,0:T(8,128)S(1)}, u32[]{:S(2)}, u32[]{:S(2)}) collective-permute-start(f32[4,128,256]{2,1,0:T(8,128)S(1)} %shard_map.74), channel_id=1, source_target_pairs={{0,4},{4,0},{1,5},{5,1},{2,6},{6,2},{3,7},{7,3},{8,12},{12,8},{9,1... | collective-permute-start | bytes 1572872 | tf_op jit(solution)/shard_map/ppermute | solution.py:19
  101.2 25.9 %collective-permute-start.20 = (f32[4,128,256]{2,1,0:T(8,128)S(1)}, f32[4,128,256]{2,1,0:T(8,128)S(1)}, u32[]{:S(2)}, u32[]{:S(2)}) collective-permute-start(f32[4,128,256]{2,1,0:T(8,128)S(1)} %add.24), channel_id=1, source_target_pairs={{0,2},{2,0},{1,3},{3,1},{4,6},{6,4},{5,7},{7,5},{8,10},{10,8},{9,1... | collective-permute-start | bytes 1572872 | tf_op jit(solution)/shard_map/ppermute | solution.py:19
  101.3 2.4 %copy-start.8 = (f32[256]{0:T(256)S(1)}, f32[256]{0:T(256)}, u32[]{:S(2)}) copy-start(f32[256]{0:T(256)} %param.8) | copy-start | bytes 3076
  101.3 2.4 %copy-start.9 = (f32[128]{0:T(128)S(1)}, f32[128]{0:T(128)}, u32[]{:S(2)}) copy-start(f32[128]{0:T(128)} %param.7) | copy-start | bytes 1540
  103.2 25.1 %collective-permute-start.21 = (f32[4,128,256]{2,1,0:T(8,128)S(1)}, f32[4,128,256]{2,1,0:T(8,128)S(1)}, u32[]{:S(2)}, u32[]{:S(2)}) collective-permute-start(f32[4,128,256]{2,1,0:T(8,128)S(1)} %shard_map.76), channel_id=1, source_target_pairs={{0,4},{4,0},{1,5},{5,1},{2,6},{6,2},{3,7},{7,3},{8,12},{12,8},{9,1... | collective-permute-start | bytes 1572872 | tf_op jit(solution)/shard_map/ppermute | solution.py:19

commit v4 on v3

--- a/solution.py
+++ b/solution.py
@@ -380,7 +380,7 @@
         from_pair = pair_swap(packed[0])
         from_chip = {j: rc_swap(packed[j], j) for j in range(1, nchip)}
         x_tops = [x_pairs] + [top_swap(x_pairs, a) for a in range(1, ntop)]
-        x_tops, from_pair, from_chip = lax.optimization_barrier((x_tops, from_pair, from_chip))
+        from_pair, from_chip = lax.optimization_barrier((from_pair, from_chip))
 
         val = [{0: (packed[-1], 0)}, {}]
         con = [{0: [(packed[1], a) for a in range(ntop)]}, {0: [(from_pair, a) for a in range(ntop)]}]
@@ -397,21 +397,11 @@
                 val[1][j] = (got, i)
 
         pair_val([0] + singles)
-        if nchip == 4:
-            con[0][3] = [None] * ntop
-            for mask in (2, 1):
-                mine = [a for a in range(ntop) if (a % 2 == 0) == (mask == 2)]
-                tiles = [con[0][3 ^ mask][a] for a in mine] + con[1][0]
-                got = rc_swap(jnp.stack([array[index] for array, index in tiles]), mask)
-                for i, a in enumerate(mine):
-                    con[0][3][a] = (got, i)
-                con[1][mask] = [(got, len(mine) + a) for a in range(ntop)]
-        else:
-            for j in others:
-                con[0][j] = relay(con[0], j)
-            for j in singles:
-                got = rc_swap(from_pair, j)
-                con[1][j] = [(got, a) for a in range(ntop)]
+        for j in singles:
+            got = rc_swap(from_pair, j)
+            con[1][j] = [(got, a) for a in range(ntop)]
+        for j in others:
+            con[0][j] = relay(con[0], j)
 
         x = [[t, core_swap(t)] for t in x_tops]
         if aligned:
@@ -459,12 +449,18 @@
             return applied(aligned, pair, pots, vals[k], cons[a], x_pairs.shape)
 
         base = (eps_con[None, None, :] - eps_val[None, :, None]) * x_pairs
+        sent = None
         for a in list(range(1, ntop)) + [0]:
             away, step = apply(a, 1), apply(a, 0)
             if a:
                 step, pots[0] = lax.optimization_barrier((step + core_swap(away), pots[0]))
-                base = base + top_swap(step, a)
-        return lax.optimization_barrier(base) + step + core_swap(away)
+                piece = top_swap(step, a)
+                sent = piece if sent is None else sent + piece
+            else:
+                size = nb // 4
+                parts = [core_swap(away[i * size:(i + 1) * size]) for i in range(4)]
+                base = lax.optimization_barrier(base + step + jnp.concatenate(parts, axis=0))
+        return base if sent is None else base + sent
 
     return per_device
 

time: 130 us -> 127 us (0.977)
  waiting for transfers between devices: 62.3 us -> 56.4 us
  starting transfers between devices: 21.9 us -> 26.5 us
  other arithmetic: 4.56 us -> 2.23 us
  local copies, waits for them, and re-layouts: 2.6 us -> 4.05 us
    ppermute x19 -> x24, waiting for transfers between devices: 58.9 us -> 53 us  [swap(): return lax.ppermute(x, axis, [(i, i ^ mask) for i in range(size)])]
    ppermute x19 -> x24, starting transfers between devices: 17.5 us -> 22.1 us  [swap(): return lax.ppermute(x, axis, [(i, i ^ mask) for i in range(size)])]
    slice x1 -> x2, local copies, waits for them, and re-layouts: 0.07 us -> 1.49 us  [pair_val(): got = pair_swap(jnp.stack([val[0][j][0][val[0][j][1]] for j in part]))]
  transfers between devices with their start and end apart: 22 -> 27, of which waited for: 12 -> 11; matrix products, arithmetic and copies ran while one was open for 3% -> 2% of each run, Pallas kernels for 13% -> 14%
where the time goes in v4:
time: 127 us; the launch traced here: 126 us
  waiting for transfers between devices  56.4 us (44%)
  starting transfers between devices  26.5 us (21%)
  Pallas kernels  23.7 us (19%)
  blocking collectives  13.3 us (10%)
  local copies, waits for them, and re-layouts  4.05 us (3%)
  other arithmetic  2.23 us (2%)
    ppermute x24, waiting for transfers between devices, swap(): return lax.ppermute(x, axis, [(i, i ^ mask) for i in range(size)])  53 us
    ppermute x24, starting transfers between devices, swap(): return lax.ppermute(x, axis, [(i, i ^ mask) for i in range(size)])  22.1 us
    all_to_all x1, blocking collectives, per_device(): got = lax.all_to_all(part, ('rc', 'core', 'top', 'pair'), 0, 0, tiled=True)  13.3 us
    pallas_call x4, Pallas kernels, densities(): pl.pallas_call(functools.partial(density_kernel, nblk, ntop, shape, at[:n...  8.8 us
    pallas_call x4, Pallas kernels, applied(): pl.pallas_call(functools.partial(apply_kernel, nchip), out_shape=jax.Shap...  7.16 us
    ppermute x3, starting transfers between devices, col_swap(): return lax.ppermute(x, ('top', 'pair'), [(i, i ^ mask) for i in range(n)])  4.4 us
    ppermute x3, waiting for transfers between devices, col_swap(): return lax.ppermute(x, ('top', 'pair'), [(i, i ^ mask) for i in range(n)])  3.38 us
  transfers between devices with their start and end apart: 27, of which 11 were waited for; matrix products, arithmetic and copies ran while one was open for 2% of the time, Pallas kernels for 14%

profile of v4, /device:TPU:0, one launch (start us, length us, event | category | flops | bytes accessed | tf_op | source)
XLA Modules:
  0.0 126.4 jit_solution(8278313466737071857)
XLA Ops:
  0.0 0.1 pad_add_fusion.1.where
  0.1 1.2 copy-done.1
  1.3 1.2 copy-done.2
  2.5 0.9 shard_map.65
  3.5 3.0 %collective-permute-start.4 = (f32[3,256,256]{2,1,0:T(8,128)S(1)}, f32[3,256,256]{2,1,0:T(8,128)S(1)}, u32[]{:S(2)}, u32[]{:S(2)}) collective-permute-start(f32[3,256,256]{2,1,0:T(8,128)S(1)} %get-tuple-element.57.refs_0_), channel_id=1, source_target_pairs={{0,8},{8,0},{16,24},{24,16},{1,9},{9,1},{17,25},{25,17},{2,10},{10... | collective-permute-start | bytes 2359304 | tf_op jit(solution)/shard_map/ppermute | solution.py:19
  6.5 1.5 %collective-permute-start.5 = (f32[3,256,256]{2,1,0:T(8,128)S(1)}, f32[3,256,256]{2,1,0:T(8,128)S(1)}, u32[]{:S(2)}, u32[]{:S(2)}) collective-permute-start(f32[3,256,256]{2,1,0:T(8,128)S(1)} %get-tuple-element.43), channel_id=1, source_target_pairs={{0,16},{8,24},{16,0},{24,8},{1,17},{9,25},{17,1},{25,9},{2,18},{10... | collective-permute-start | bytes 2359304 | tf_op jit(solution)/shard_map/ppermute | solution.py:19
  8.0 2.6 %collective-permute-start.1 = (f32[4,128,256]{2,1,0:T(8,128)S(1)}, f32[4,128,256]{2,1,0:T(8,128)}, u32[]{:S(2)}, u32[]{:S(2)}) collective-permute-start(f32[4,128,256]{2,1,0:T(8,128)S(1)} %copy-done), channel_id=1, source_target_pairs={{0,2},{2,0},{1,3},{3,1},{4,6},{6,4},{5,7},{7,5},{8,10},{10,8},{9,1... | collective-permute-start | bytes 1572872 | tf_op jit(solution)/shard_map/ppermute | solution.py:19
  10.6 1.6 %collective-permute-start.3 = (f32[2,256,256]{2,1,0:T(8,128)S(1)}, f32[2,256,256]{2,1,0:T(8,128)}, u32[]{:S(2)}, u32[]{:S(2)}) collective-permute-start(f32[2,256,256]{2,1,0:T(8,128)S(1)} %get-tuple-element.42), channel_id=1, source_target_pairs={{0,1},{1,0},{2,3},{3,2},{4,5},{5,4},{6,7},{7,6},{8,9},{9,8},{10,11... | collective-permute-start | bytes 1572872 | tf_op jit(solution)/shard_map/ppermute | solution.py:19
  12.2 0.5 collective-permute-start.6
  12.6 18.3 %collective-permute-done.6.refs_2_.refs_11_ = f32[1,256,256]{2,1,0:T(8,128)S(1)} collective-permute-done((f32[1,256,256]{2,1,0:T(8,128)S(1)}, f32[1,256,256]{2,1,0:T(8,128)S(1)}, u32[]{:S(2)}, u32[]{:S(2)}) %collective-permute-start.6) | collective-permute-done | bytes 262176 | tf_op jit(solution)/shard_map/ppermute | solution.py:19
  30.9 0.0 collective-permute-start
  30.9 2.5 %collective-permute-done.1.refs_2_ = f32[4,128,256]{2,1,0:T(8,128)} collective-permute-done((f32[4,128,256]{2,1,0:T(8,128)S(1)}, f32[4,128,256]{2,1,0:T(8,128)}, u32[]{:S(2)}, u32[]{:S(2)}) %collective-permute-start.1) | collective-permute-done | bytes 524320 | tf_op jit(solution)/shard_map/ppermute | solution.py:19
  33.4 0.2 collective-permute-done.3.refs_0_.refs_4_
  33.6 0.7 fusion
  34.4 0.7 fusion.1
  35.1 0.9 pad_maximum_fusion
  36.1 1.4 %collective-permute-start.11 = (f32[3,256,256]{2,1,0:T(8,128)}, f32[3,256,256]{2,1,0:T(8,128)}, u32[]{:S(2)}, u32[]{:S(2)}) collective-permute-start(f32[3,256,256]{2,1,0:T(8,128)} %pad_maximum_fusion), channel_id=1, source_target_pairs={{0,1},{1,0},{2,3},{3,2},{4,5},{5,4},{6,7},{7,6},{8,9},{9,8},{10,11... | collective-permute-start | bytes 2359304 | tf_op jit(solution)/shard_map/ppermute | solution.py:19
  37.5 0.5 collective-permute-start.7
  38.0 0.5 collective-permute-start.8
  38.5 0.1 pad_add_fusion.where
  38.6 1.5 %collective-permute-start.10 = (f32[1,256,256]{2,1,0:T(8,128)}, f32[1,256,256]{2,1,0:T(8,128)S(1)}, u32[]{:S(2)}, u32[]{:S(2)}) collective-permute-start(f32[1,256,256]{2,1,0:T(8,128)} %get-tuple-element.80), channel_id=1, source_target_pairs={{0,8},{8,0},{16,24},{24,16},{1,9},{9,1},{17,25},{25,17},{2,10},{10... | collective-permute-start | bytes 786440 | tf_op jit(solution)/shard_map/ppermute | solution.py:19
  40.1 1.5 %collective-permute-start.9 = (f32[1,256,256]{2,1,0:T(8,128)}, f32[1,256,256]{2,1,0:T(8,128)S(1)}, u32[]{:S(2)}, u32[]{:S(2)}) collective-permute-start(f32[1,256,256]{2,1,0:T(8,128)} %get-tuple-element.78), channel_id=1, source_target_pairs={{0,16},{8,24},{16,0},{24,8},{1,17},{9,25},{17,1},{25,9},{2,18},{10... | collective-permute-start | bytes 786440 | tf_op jit(solution)/shard_map/ppermute | solution.py:19
  41.6 1.8 %shard_map.64.x_ref = bf16[1024,1024]{1,0:T(8,128)(2,1)S(1)} custom-call(f32[4,128,256]{2,1,0:T(8,128)S(1)} %copy-done, f32[4,128,256]{2,1,0:T(8,128)} %collective-permute-done.refs_1_, f32[4,128,256]{2,1,0:T(8,128)} %collective-permute-done.1.refs_2_, f32[4,128,256]{2,1,0:T(8,128)} %collective-permute-done.2.refs_3_), custom_call_target="tpu_custom_call" | custom-call | flops 2000000000 | bytes 4194304 | tf_op jit(solution)/shard_map/pallas_call | solution.py:118
  43.4 2.7 %shard_map.66.refs_0_ = f32[3,4,256]{2,1,0:T(4,128)S(1)} custom-call(s32[1]{0:T(128)} %bitcast.3.core_ref, bf16[1024,1024]{1,0:T(8,128)(2,1)S(1)} %shard_map.64.x_ref, f32[3,256,256]{2,1,0:T(8,128)S(1)} %copy-done.4, f32[3,256,256]{2,1,0:T(8,128)S(1)} %collective-permute-done.4.refs_1_, f32[3,256,256]{2,1,0:T(8,128)S(1)} %collective-permute-done.5.refs_2_, ...), custom_call_target="tpu_custom_call" | custom-call | flops 2000000000 | bytes 4194304 | tf_op jit(solution)/shard_map/pallas_call | solution.py:160
  46.2 6.4 %collective-permute-done.7.refs_1_.refs_5_ = f32[2,256,256]{2,1,0:T(8,128)S(1)} collective-permute-done((f32[2,256,256]{2,1,0:T(8,128)}, f32[2,256,256]{2,1,0:T(8,128)S(1)}, u32[]{:S(2)}, u32[]{:S(2)}) %collective-permute-start.7) | collective-permute-done | bytes 524320 | tf_op jit(solution)/shard_map/ppermute | solution.py:19
  52.6 0.5 collective-permute-done.8.refs_2_.refs_6_
  53.1 0.6 collective-permute-start.12
  53.7 1.6 %collective-permute-start.13 = (f32[1,256,256]{2,1,0:T(8,128)S(1)}, f32[1,256,256]{2,1,0:T(8,128)S(1)}, u32[]{:S(2)}, u32[]{:S(2)}) collective-permute-start(f32[1,256,256]{2,1,0:T(8,128)S(1)} %slice.35), channel_id=1, source_target_pairs={{0,8},{8,0},{16,24},{24,16},{1,9},{9,1},{17,25},{25,17},{2,10},{10... | collective-permute-start | bytes 786440 | tf_op jit(solution)/shard_map/ppermute | solution.py:19
  55.3 2.9 %collective-permute-done.10.refs_1_.refs_8_ = f32[1,256,256]{2,1,0:T(8,128)S(1)} collective-permute-done((f32[1,256,256]{2,1,0:T(8,128)}, f32[1,256,256]{2,1,0:T(8,128)S(1)}, u32[]{:S(2)}, u32[]{:S(2)}) %collective-permute-start.10) | collective-permute-done | bytes 262176 | tf_op jit(solution)/shard_map/ppermute | solution.py:19
  58.2 0.5 collective-permute-start.14
  58.7 0.0 collective-permute-done.9.refs_0_.refs_3_
  58.7 1.0 shard_map.67.refs_1_
  59.8 4.0 %shard_map.68.refs_2_ = f32[3,4,256]{2,1,0:T(4,128)S(1)} custom-call(s32[1]{0:T(128)} %bitcast.3.core_ref, bf16[1024,1024]{1,0:T(8,128)(2,1)S(1)} %shard_map.64.x_ref, f32[2,256,256]{2,1,0:T(8,128)} %collective-permute-done.3.refs_0_.refs_4_, f32[2,256,256]{2,1,0:T(8,128)S(1)} %collective-permute-done.7.refs_1_.refs_5_, ...), custom_call_target="tpu_custom_call" | custom-call | flops 2000000000 | bytes 4194304 | tf_op jit(solution)/shard_map/pallas_call | solution.py:160
  63.8 0.7 collective-permute-done.14.refs_2_.refs_13_
  64.6 1.0 shard_map.69.refs_3_
  65.6 0.0 slice-start.1
  65.6 0.6 shard_map.70
  66.2 13.3 %all_to_all.5.got_ref = f32[32,8,256]{2,1,0:T(8,128)S(1)} all-to-all(f32[32,8,256]{2,1,0:T(8,128)S(1)} %shard_map.70), channel_id=1, replica_groups=mesh['rc'=4,'core'=2,'top'=2,'pair'=2] {'rc','core','top','pair'}, dimensions={0} | all-to-all | bytes 524288 | tf_op jit(solution)/shard_map/all_to_all | solution.py:437
  79.5 2.3 %shard_map.71 = (f32[8,256]{1,0:T(8,128)S(1)}, f32[8,256]{1,0:T(8,128)S(1)}) custom-call(s32[1]{0:T(128)} %bitcast.1.top_ref, f32[32,8,256]{2,1,0:T(8,128)S(1)} %all_to_all.5.got_ref, f32[1024,2048]{1,0:T(8,128)S(1)} %bitcast.5), custom_call_target="tpu_custom_call" | custom-call | flops 2000000000 | bytes 4194304 | tf_op jit(solution)/shard_map/pallas_call | solution.py:246
  81.8 1.1 collective-permute-start.15
  82.9 1.2 collective-permute-start.16
  84.1 2.1 %collective-permute-start.17 = (f32[8,256]{1,0:T(8,128)S(1)}, f32[8,256]{1,0:T(8,128)S(1)}, u32[]{:S(2)}, u32[]{:S(2)}) collective-permute-start(f32[8,256]{1,0:T(8,128)S(1)} %get-tuple-element.56), channel_id=1, source_target_pairs={{0,3},{1,2},{2,1},{3,0},{4,7},{5,6},{6,5},{7,4},{8,11},{9,10},{10,... | collective-permute-start | bytes 24584 | tf_op jit(solution)/shard_map/ppermute | solution.py:358
  86.2 1.3 collective-permute-done.16
  87.5 2.1 %collective-permute-done.17 = f32[8,256]{1,0:T(8,128)S(1)} collective-permute-done((f32[8,256]{1,0:T(8,128)S(1)}, f32[8,256]{1,0:T(8,128)S(1)}, u32[]{:S(2)}, u32[]{:S(2)}) %collective-permute-start.17) | collective-permute-done | bytes 8224 | tf_op jit(solution)/shard_map/ppermute | solution.py:358
  89.6 1.2 collective-permute-start.18
  90.8 0.4 collective-permute-start.19
  91.2 1.9 %collective-permute-start.20 = (f32[8,256]{1,0:T(8,128)S(1)}, f32[8,256]{1,0:T(8,128)S(1)}, u32[]{:S(2)}, u32[]{:S(2)}) collective-permute-start(f32[8,256]{1,0:T(8,128)S(1)} %add_add_fusion.refs_0_), channel_id=1, source_target_pairs={{0,24},{8,16},{16,8},{24,0},{1,25},{9,17},{17,9},{25,1},{2,26},{10... | collective-permute-start | bytes 24584 | tf_op jit(solution)/shard_map/ppermute | solution.py:19
  93.1 2.2 %shard_map.72 = (bf16[6144,256]{1,0:T(8,128)(2,1)S(1)}, bf16[6144,256]{1,0:T(8,128)(2,1)S(1)}, f32[8,128,256]{2,1,0:T(8,128)S(1)}, f32[8,128,256]{2,1,0:T(8,128)S(1)}) custom-call(s32[1]{0:T(128)} %bitcast.3.core_ref, f32[3,256,256]{2,1,0:T(8,128)S(1)} %copy-done.4, f32[3,256,256]{2,1,0:T(8,128)S(1)} %collective-permute-done.4.refs_1_, ...), custom_call_target="tpu_custom_call" | custom-call | flops 2000000000 | bytes 4194304 | tf_op jit(solution)/shard_map/pallas_call | solution.py:286
  95.3 0.5 collective-permute-done.20.refs_3_
  95.8 1.8 %shard_map.74 = f32[4,128,256]{2,1,0:T(8,128)S(1)} custom-call(s32[1]{0:T(128)} %bitcast.pair_ref, f32[8,256]{1,0:T(8,128)S(1)} %add_add_fusion.refs_0_, f32[8,256]{1,0:T(8,128)S(1)} %collective-permute-done.18.refs_1_, f32[8,256]{1,0:T(8,128)S(1)} %collective-permute-done.19.refs_2_, f32[8,256]{1,0:T(8,128)S(1)} %collective-permute-done.20.refs_3_, ...), custom_call_target="tpu_custom_call" | custom-call | flops 2000000000 | bytes 4194304 | tf_op jit(solution)/shard_map/pallas_call | solution.py:329
  97.6 0.1 collective-permute-start.21
  97.7 0.1 broadcast_subtract_fusion
  97.7 1.8 %shard_map.73 = f32[4,128,256]{2,1,0:T(8,128)S(1)} custom-call(s32[1]{0:T(128)} %bitcast.pair_ref, f32[8,256]{1,0:T(8,128)S(1)} %add_add_fusion.refs_0_, f32[8,256]{1,0:T(8,128)S(1)} %collective-permute-done.18.refs_1_, f32[8,256]{1,0:T(8,128)S(1)} %collective-permute-done.19.refs_2_, f32[8,256]{1,0:T(8,128)S(1)} %collective-permute-done.20.refs_3_, ...), custom_call_target="tpu_custom_call" | custom-call | flops 2000000000 | bytes 4194304 | tf_op jit(solution)/shard_map/pallas_call | solution.py:329
  99.5 0.1 add.24
  99.6 0.1 collective-permute-start.26
  99.7 1.8 %shard_map.76 = f32[4,128,256]{2,1,0:T(8,128)S(1)} custom-call(s32[1]{0:T(128)} %bitcast.pair_ref, f32[8,256]{1,0:T(8,128)S(1)} %add_add_fusion.refs_0_, f32[8,256]{1,0:T(8,128)S(1)} %collective-permute-done.18.refs_1_, f32[8,256]{1,0:T(8,128)S(1)} %collective-permute-done.19.refs_2_, f32[8,256]{1,0:T(8,128)S(1)} %collective-permute-done.20.refs_3_, ...), custom_call_target="tpu_custom_call" | custom-call | flops 2000000000 | bytes 4194304 | tf_op jit(solution)/shard_map/pallas_call | solution.py:329
  101.5 0.5 collective-permute-start.22
  102.1 0.1 collective-permute-start.23
  102.2 0.4 collective-permute-start.24
  102.6 0.1 collective-permute-start.25
  102.7 1.8 %shard_map.75 = f32[4,128,256]{2,1,0:T(8,128)S(1)} custom-call(s32[1]{0:T(128)} %bitcast.pair_ref, f32[8,256]{1,0:T(8,128)S(1)} %add_add_fusion.refs_0_, f32[8,256]{1,0:T(8,128)S(1)} %collective-permute-done.18.refs_1_, f32[8,256]{1,0:T(8,128)S(1)} %collective-permute-done.19.refs_2_, f32[8,256]{1,0:T(8,128)S(1)} %collective-permute-done.20.refs_3_, ...), custom_call_target="tpu_custom_call" | custom-call | flops 2000000000 | bytes 4194304 | tf_op jit(solution)/shard_map/pallas_call | solution.py:329
  104.5 0.1 maximum_add_fusion
  104.7 20.9 %collective-permute-done.26 = f32[4,128,256]{2,1,0:T(8,128)S(1)} collective-permute-done((f32[4,128,256]{2,1,0:T(8,128)S(1)}, f32[4,128,256]{2,1,0:T(8,128)S(1)}, u32[]{:S(2)}, u32[]{:S(2)}) %collective-permute-start.26) | collective-permute-done | bytes 524320 | tf_op jit(solution)/shard_map/ppermute | solution.py:19
  125.5 0.9 add.27
  (40 shorter events, 0.2 us)
Async XLA Ops:
  0.1 1.2 copy-start.1
  1.3 1.2 copy-start.2
  2.5 5.5 %copy-start = (f32[4,128,256]{2,1,0:T(8,128)S(1)}, f32[4,128,256]{2,1,0:T(8,128)}, u32[]{:S(2)}) copy-start(f32[4,128,256]{2,1,0:T(8,128)} %refs_0_.1) | copy-start | bytes 1572868
  3.4 34.1 %copy-start.3 = (f32[3,256,256]{2,1,0:T(8,128)}, f32[3,256,256]{2,1,0:T(8,128)S(1)}, u32[]{:S(2)}) copy-start(f32[3,256,256]{2,1,0:T(8,128)S(1)} %get-tuple-element.57.refs_0_) | copy-start | bytes 2359300
  3.5 30.2 %collective-permute-start.4 = (f32[3,256,256]{2,1,0:T(8,128)S(1)}, f32[3,256,256]{2,1,0:T(8,128)S(1)}, u32[]{:S(2)}, u32[]{:S(2)}) collective-permute-start(f32[3,256,256]{2,1,0:T(8,128)S(1)} %get-tuple-element.57.refs_0_), channel_id=1, source_target_pairs={{0,8},{8,0},{16,24},{24,16},{1,9},{9,1},{17,25},{25,17},{2,10},{10... | collective-permute-start | bytes 2359304 | tf_op jit(solution)/shard_map/ppermute | solution.py:19
  6.5 27.2 %collective-permute-start.5 = (f32[3,256,256]{2,1,0:T(8,128)S(1)}, f32[3,256,256]{2,1,0:T(8,128)S(1)}, u32[]{:S(2)}, u32[]{:S(2)}) collective-permute-start(f32[3,256,256]{2,1,0:T(8,128)S(1)} %get-tuple-element.43), channel_id=1, source_target_pairs={{0,16},{8,24},{16,0},{24,8},{1,17},{9,25},{17,1},{25,9},{2,18},{10... | collective-permute-start | bytes 2359304 | tf_op jit(solution)/shard_map/ppermute | solution.py:19
  8.0 25.5 %collective-permute-start.1 = (f32[4,128,256]{2,1,0:T(8,128)S(1)}, f32[4,128,256]{2,1,0:T(8,128)}, u32[]{:S(2)}, u32[]{:S(2)}) collective-permute-start(f32[4,128,256]{2,1,0:T(8,128)S(1)} %copy-done), channel_id=1, source_target_pairs={{0,2},{2,0},{1,3},{3,1},{4,6},{6,4},{5,7},{7,5},{8,10},{10,8},{9,1... | collective-permute-start | bytes 1572872 | tf_op jit(solution)/shard_map/ppermute | solution.py:19
  10.6 23.1 %collective-permute-start.3 = (f32[2,256,256]{2,1,0:T(8,128)S(1)}, f32[2,256,256]{2,1,0:T(8,128)}, u32[]{:S(2)}, u32[]{:S(2)}) collective-permute-start(f32[2,256,256]{2,1,0:T(8,128)S(1)} %get-tuple-element.42), channel_id=1, source_target_pairs={{0,1},{1,0},{2,3},{3,2},{4,5},{5,4},{6,7},{7,6},{8,9},{9,8},{10,11... | collective-permute-start | bytes 1572872 | tf_op jit(solution)/shard_map/ppermute | solution.py:19
  12.2 18.8 %collective-permute-start.6 = (f32[1,256,256]{2,1,0:T(8,128)S(1)}, f32[1,256,256]{2,1,0:T(8,128)S(1)}, u32[]{:S(2)}, u32[]{:S(2)}) collective-permute-start(f32[1,256,256]{2,1,0:T(8,128)S(1)} %get-tuple-element.44), channel_id=1, source_target_pairs={{0,24},{8,16},{16,8},{24,0},{1,25},{9,17},{17,9},{25,1},{2,26},{10... | collective-permute-start | bytes 786440 | tf_op jit(solution)/shard_map/ppermute | solution.py:19
  30.9 2.7 %copy-start.5 = (f32[1,256,256]{2,1,0:T(8,128)}, f32[1,256,256]{2,1,0:T(8,128)S(1)}, u32[]{:S(2)}) copy-start(f32[1,256,256]{2,1,0:T(8,128)S(1)} %collective-permute-done.6.refs_2_.refs_11_) | copy-start | bytes 786436
  30.9 7.7 %collective-permute-start = (f32[4,128,256]{2,1,0:T(8,128)S(1)}, f32[4,128,256]{2,1,0:T(8,128)}, u32[]{:S(2)}, u32[]{:S(2)}) collective-permute-start(f32[4,128,256]{2,1,0:T(8,128)S(1)} %copy-done), channel_id=1, source_target_pairs={{0,4},{4,0},{1,5},{5,1},{2,6},{6,2},{3,7},{7,3},{8,12},{12,8},{9,1... | collective-permute-start | bytes 1572872 | tf_op jit(solution)/shard_map/ppermute | solution.py:19
  33.4 6.7 %collective-permute-start.2 = (f32[4,128,256]{2,1,0:T(8,128)}, f32[4,128,256]{2,1,0:T(8,128)}, u32[]{:S(2)}, u32[]{:S(2)}) collective-permute-start(f32[4,128,256]{2,1,0:T(8,128)} %collective-permute-done.1.refs_2_), channel_id=1, source_target_pairs={{0,4},{4,0},{1,5},{5,1},{2,6},{6,2},{3,7},{7,3},{8,12},{12,8},{9,1... | collective-permute-start | bytes 1572872 | tf_op jit(solution)/shard_map/ppermute | solution.py:19
  36.1 23.7 %collective-permute-start.11 = (f32[3,256,256]{2,1,0:T(8,128)}, f32[3,256,256]{2,1,0:T(8,128)}, u32[]{:S(2)}, u32[]{:S(2)}) collective-permute-start(f32[3,256,256]{2,1,0:T(8,128)} %pad_maximum_fusion), channel_id=1, source_target_pairs={{0,1},{1,0},{2,3},{3,2},{4,5},{5,4},{6,7},{7,6},{8,9},{9,8},{10,11... | collective-permute-start | bytes 2359304 | tf_op jit(solution)/shard_map/ppermute | solution.py:19
  37.5 15.1 %collective-permute-start.7 = (f32[2,256,256]{2,1,0:T(8,128)}, f32[2,256,256]{2,1,0:T(8,128)S(1)}, u32[]{:S(2)}, u32[]{:S(2)}) collective-permute-start(f32[2,256,256]{2,1,0:T(8,128)} %collective-permute-done.3.refs_0_.refs_4_), channel_id=1, source_target_pairs={{0,8},{8,0},{16,24},{24,16},{1,9},{9,1},{17,25},{25,17},{2,10},{10... | collective-permute-start | bytes 1572872 | tf_op jit(solution)/shard_map/ppermute | solution.py:19
  38.0 15.1 %collective-permute-start.8 = (f32[2,256,256]{2,1,0:T(8,128)}, f32[2,256,256]{2,1,0:T(8,128)S(1)}, u32[]{:S(2)}, u32[]{:S(2)}) collective-permute-start(f32[2,256,256]{2,1,0:T(8,128)} %collective-permute-done.3.refs_0_.refs_4_), channel_id=1, source_target_pairs={{0,16},{8,24},{16,0},{24,8},{1,17},{9,25},{17,1},{25,9},{2,18},{10... | collective-permute-start | bytes 1572872 | tf_op jit(solution)/shard_map/ppermute | solution.py:19
  38.6 19.6 %collective-permute-start.10 = (f32[1,256,256]{2,1,0:T(8,128)}, f32[1,256,256]{2,1,0:T(8,128)S(1)}, u32[]{:S(2)}, u32[]{:S(2)}) collective-permute-start(f32[1,256,256]{2,1,0:T(8,128)} %get-tuple-element.80), channel_id=1, source_target_pairs={{0,8},{8,0},{16,24},{24,16},{1,9},{9,1},{17,25},{25,17},{2,10},{10... | collective-permute-start | bytes 786440 | tf_op jit(solution)/shard_map/ppermute | solution.py:19
  40.1 3.3 %copy-start.4 = (f32[3,256,256]{2,1,0:T(8,128)S(1)}, f32[3,256,256]{2,1,0:T(8,128)}, u32[]{:S(2)}) copy-start(f32[3,256,256]{2,1,0:T(8,128)} %copy-done.3) | copy-start | bytes 2359300
  40.1 18.6 %collective-permute-start.9 = (f32[1,256,256]{2,1,0:T(8,128)}, f32[1,256,256]{2,1,0:T(8,128)S(1)}, u32[]{:S(2)}, u32[]{:S(2)}) collective-permute-start(f32[1,256,256]{2,1,0:T(8,128)} %get-tuple-element.78), channel_id=1, source_target_pairs={{0,16},{8,24},{16,0},{24,8},{1,17},{9,25},{17,1},{25,9},{2,18},{10... | collective-permute-start | bytes 786440 | tf_op jit(solution)/shard_map/ppermute | solution.py:19
  43.4 14.8 %copy-start.6 = (f32[1,256,256]{2,1,0:T(8,128)S(1)}, f32[1,256,256]{2,1,0:T(8,128)}, u32[]{:S(2)}) copy-start(f32[1,256,256]{2,1,0:T(8,128)} %copy-done.5) | copy-start | bytes 786436
  53.1 10.7 %collective-permute-start.12 = (f32[1,256,256]{2,1,0:T(8,128)S(1)}, f32[1,256,256]{2,1,0:T(8,128)S(1)}, u32[]{:S(2)}, u32[]{:S(2)}) collective-permute-start(f32[1,256,256]{2,1,0:T(8,128)S(1)} %slice.34), channel_id=1, source_target_pairs={{0,16},{8,24},{16,0},{24,8},{1,17},{9,25},{17,1},{25,9},{2,18},{10... | collective-permute-start | bytes 786440 | tf_op jit(solution)/shard_map/ppermute | solution.py:19
  53.7 10.1 %collective-permute-start.13 = (f32[1,256,256]{2,1,0:T(8,128)S(1)}, f32[1,256,256]{2,1,0:T(8,128)S(1)}, u32[]{:S(2)}, u32[]{:S(2)}) collective-permute-start(f32[1,256,256]{2,1,0:T(8,128)S(1)} %slice.35), channel_id=1, source_target_pairs={{0,8},{8,0},{16,24},{24,16},{1,9},{9,1},{17,25},{25,17},{2,10},{10... | collective-permute-start | bytes 786440 | tf_op jit(solution)/shard_map/ppermute | solution.py:19
  58.2 6.4 %collective-permute-start.14 = (f32[1,256,256]{2,1,0:T(8,128)S(1)}, f32[1,256,256]{2,1,0:T(8,128)S(1)}, u32[]{:S(2)}, u32[]{:S(2)}) collective-permute-start(f32[1,256,256]{2,1,0:T(8,128)S(1)} %copy-done.6), channel_id=1, source_target_pairs={{0,1},{1,0},{2,3},{3,2},{4,5},{5,4},{6,7},{7,6},{8,9},{9,8},{10,11... | collective-permute-start | bytes 786440 | tf_op jit(solution)/shard_map/ppermute | solution.py:19
  64.6 14.9 %slice-start = ((s8[8388608]{0:T(1024)(128)(4,1)}), s8[4194304]{0:T(1024)(128)(4,1)S(1)}, s32[]{:S(2)}) async-start(s8[8388608]{0:T(1024)(128)(4,1)} %bitcast.4), calls=%async_computation.1 | async-start | bytes 8388608
  65.6 13.9 %slice-start.1 = ((s8[8388608]{0:T(1024)(128)(4,1)}), s8[4194304]{0:T(1024)(128)(4,1)S(1)}, s32[]{:S(2)}) async-start(s8[8388608]{0:T(1024)(128)(4,1)} %bitcast.4), calls=%async_computation.2 | async-start | bytes 8388608
  81.8 4.4 %collective-permute-start.15 = (f32[8,256]{1,0:T(8,128)S(1)}, f32[8,256]{1,0:T(8,128)S(1)}, u32[]{:S(2)}, u32[]{:S(2)}) collective-permute-start(f32[8,256]{1,0:T(8,128)S(1)} %get-tuple-element.55), channel_id=1, source_target_pairs={{0,1},{1,0},{2,3},{3,2},{4,5},{5,4},{6,7},{7,6},{8,9},{9,8},{10,11... | collective-permute-start | bytes 24584 | tf_op jit(solution)/shard_map/ppermute | solution.py:358
  82.9 4.5 %collective-permute-start.16 = (f32[8,256]{1,0:T(8,128)S(1)}, f32[8,256]{1,0:T(8,128)S(1)}, u32[]{:S(2)}, u32[]{:S(2)}) collective-permute-start(f32[8,256]{1,0:T(8,128)S(1)} %get-tuple-element.56), channel_id=1, source_target_pairs={{0,2},{1,3},{2,0},{3,1},{4,6},{5,7},{6,4},{7,5},{8,10},{9,11},{10,... | collective-permute-start | bytes 24584 | tf_op jit(solution)/shard_map/ppermute | solution.py:358
  84.1 5.4 %collective-permute-start.17 = (f32[8,256]{1,0:T(8,128)S(1)}, f32[8,256]{1,0:T(8,128)S(1)}, u32[]{:S(2)}, u32[]{:S(2)}) collective-permute-start(f32[8,256]{1,0:T(8,128)S(1)} %get-tuple-element.56), channel_id=1, source_target_pairs={{0,3},{1,2},{2,1},{3,0},{4,7},{5,6},{6,5},{7,4},{8,11},{9,10},{10,... | collective-permute-start | bytes 24584 | tf_op jit(solution)/shard_map/ppermute | solution.py:358
  89.6 5.7 %collective-permute-start.18 = (f32[8,256]{1,0:T(8,128)S(1)}, f32[8,256]{1,0:T(8,128)S(1)}, u32[]{:S(2)}, u32[]{:S(2)}) collective-permute-start(f32[8,256]{1,0:T(8,128)S(1)} %add_add_fusion.refs_0_), channel_id=1, source_target_pairs={{0,8},{8,0},{16,24},{24,16},{1,9},{9,1},{17,25},{25,17},{2,10},{10... | collective-permute-start | bytes 24584 | tf_op jit(solution)/shard_map/ppermute | solution.py:19
  90.8 4.5 %collective-permute-start.19 = (f32[8,256]{1,0:T(8,128)S(1)}, f32[8,256]{1,0:T(8,128)S(1)}, u32[]{:S(2)}, u32[]{:S(2)}) collective-permute-start(f32[8,256]{1,0:T(8,128)S(1)} %add_add_fusion.refs_0_), channel_id=1, source_target_pairs={{0,16},{8,24},{16,0},{24,8},{1,17},{9,25},{17,1},{25,9},{2,18},{10... | collective-permute-start | bytes 24584 | tf_op jit(solution)/shard_map/ppermute | solution.py:19
  91.2 4.5 %collective-permute-start.20 = (f32[8,256]{1,0:T(8,128)S(1)}, f32[8,256]{1,0:T(8,128)S(1)}, u32[]{:S(2)}, u32[]{:S(2)}) collective-permute-start(f32[8,256]{1,0:T(8,128)S(1)} %add_add_fusion.refs_0_), channel_id=1, source_target_pairs={{0,24},{8,16},{16,8},{24,0},{1,25},{9,17},{17,9},{25,1},{2,26},{10... | collective-permute-start | bytes 24584 | tf_op jit(solution)/shard_map/ppermute | solution.py:19
  95.8 1.9 %copy-start.7 = (f32[256]{0:T(256)S(1)}, f32[256]{0:T(256)}, u32[]{:S(2)}) copy-start(f32[256]{0:T(256)} %param.8) | copy-start | bytes 3076
  95.8 1.9 %copy-start.8 = (f32[128]{0:T(128)S(1)}, f32[128]{0:T(128)}, u32[]{:S(2)}) copy-start(f32[128]{0:T(128)} %param.7) | copy-start | bytes 1540
  97.6 2.0 %collective-permute-start.21 = (f32[4,128,256]{2,1,0:T(8,128)S(1)}, f32[4,128,256]{2,1,0:T(8,128)S(1)}, u32[]{:S(2)}, u32[]{:S(2)}) collective-permute-start(f32[4,128,256]{2,1,0:T(8,128)S(1)} %shard_map.74), channel_id=1, source_target_pairs={{0,4},{4,0},{1,5},{5,1},{2,6},{6,2},{3,7},{7,3},{8,12},{12,8},{9,1... | collective-permute-start | bytes 1572872 | tf_op jit(solution)/shard_map/ppermute | solution.py:19
  99.6 25.9 %collective-permute-start.26 = (f32[4,128,256]{2,1,0:T(8,128)S(1)}, f32[4,128,256]{2,1,0:T(8,128)S(1)}, u32[]{:S(2)}, u32[]{:S(2)}) collective-permute-start(f32[4,128,256]{2,1,0:T(8,128)S(1)} %add.24), channel_id=1, source_target_pairs={{0,2},{2,0},{1,3},{3,1},{4,6},{6,4},{5,7},{7,5},{8,10},{10,8},{9,1... | collective-permute-start | bytes 1572872 | tf_op jit(solution)/shard_map/ppermute | solution.py:19
  101.5 2.9 %collective-permute-start.22 = (f32[1,128,256]{2,1,0:T(8,128)S(1)}, f32[1,128,256]{2,1,0:T(8,128)S(1)}, u32[]{:S(2)}, u32[]{:S(2)}) collective-permute-start(f32[1,128,256]{2,1,0:T(8,128)S(1)} %get-tuple-element.81), channel_id=1, source_target_pairs={{0,4},{4,0},{1,5},{5,1},{2,6},{6,2},{3,7},{7,3},{8,12},{12,8},{9,1... | collective-permute-start | bytes 393224 | tf_op jit(solution)/shard_map/ppermute | solution.py:19
  102.1 2.4 %collective-permute-start.23 = (f32[1,128,256]{2,1,0:T(8,128)S(1)}, f32[1,128,256]{2,1,0:T(8,128)S(1)}, u32[]{:S(2)}, u32[]{:S(2)}) collective-permute-start(f32[1,128,256]{2,1,0:T(8,128)S(1)} %get-tuple-element.84), channel_id=1, source_target_pairs={{0,4},{4,0},{1,5},{5,1},{2,6},{6,2},{3,7},{7,3},{8,12},{12,8},{9,1... | collective-permute-start | bytes 393224 | tf_op jit(solution)/shard_map/ppermute | solution.py:19
  102.2 2.3 %collective-permute-start.24 = (f32[1,128,256]{2,1,0:T(8,128)S(1)}, f32[1,128,256]{2,1,0:T(8,128)S(1)}, u32[]{:S(2)}, u32[]{:S(2)}) collective-permute-start(f32[1,128,256]{2,1,0:T(8,128)S(1)} %get-tuple-element.83), channel_id=1, source_target_pairs={{0,4},{4,0},{1,5},{5,1},{2,6},{6,2},{3,7},{7,3},{8,12},{12,8},{9,1... | collective-permute-start | bytes 393224 | tf_op jit(solution)/shard_map/ppermute | solution.py:19
  102.6 1.9 %collective-permute-start.25 = (f32[1,128,256]{2,1,0:T(8,128)S(1)}, f32[1,128,256]{2,1,0:T(8,128)S(1)}, u32[]{:S(2)}, u32[]{:S(2)}) collective-permute-start(f32[1,128,256]{2,1,0:T(8,128)S(1)} %get-tuple-element.82), channel_id=1, source_target_pairs={{0,4},{4,0},{1,5},{5,1},{2,6},{6,2},{3,7},{7,3},{8,12},{12,8},{9,1... | collective-permute-start | bytes 393224 | tf_op jit(solution)/shard_map/ppermute | solution.py:19

commit v5 on v4

--- a/solution.py
+++ b/solution.py
@@ -299,19 +299,20 @@
     return after, vals, [jnp.stack(tiles[a * nblk:(a + 1) * nblk]) for a in range(ntop)]
 
 
-def apply_kernel(nchip, pair_ref, *refs):
+def apply_kernel(nchip, start, pair_ref, *refs):
     pots, (val_ref, right, out_ref, left) = refs[:nchip], refs[nchip:]
     nb, nv, nc = out_ref.shape
     pts = val_ref.shape[2]
     pair = pair_ref[0]
+    vecs = pots[0].shape[0] // 2
     for j in range(nchip):
         both = pots[j][...]
         for e in range(2):
             g = e * nchip + j
-            pot = jnp.where((pair ^ e) == 0, both[:nb], both[nb:])
+            pot = jnp.where((pair ^ e) == 0, both[:vecs], both[vecs:])
             rows = val_ref[g]
             for b in range(nb):
-                high, low = split(rows * pot[b:b + 1])
+                high, low = split(rows * pot[start + b:start + b + 1])
                 at = pl.ds(b * nv, nv)
                 left[at, pl.ds(3 * g * pts, pts)] = high
                 left[at, pl.ds((3 * g + 1) * pts, pts)] = high
@@ -320,14 +321,14 @@
     out_ref[...] = total.reshape(nb, nv, nc)
 
 
-def applied(aligned, pair, pots, val, con, shape):
+def applied(aligned, pair, pots, val, con, start, shape):
     nb, nv, nc = shape
     nblk = val.shape[0]
     nchip = nblk // 2
     pts = pots[0].shape[1]
     if aligned:
         return pl.pallas_call(
-            functools.partial(apply_kernel, nchip),
+            functools.partial(apply_kernel, nchip, start),
             out_shape=jax.ShapeDtypeStruct(shape, jnp.float32),
             in_specs=[SMEM] + [VMEM] * (nchip + 2),
             out_specs=VMEM,
@@ -335,7 +336,7 @@
             compiler_params=PARAMS,
             cost_estimate=COST,
         )(pair.astype(jnp.int32)[None], *pots, val, con)
-    pot = relative(jnp.stack(pots).reshape(nchip, 2, nb, pts), 1, pair)
+    pot = relative(jnp.stack(pots).reshape(nchip, 2, -1, pts), 1, pair)[:, :, start:start + nb]
     pot = jnp.transpose(pot, (1, 0, 2, 3)).reshape(nblk, nb, pts)
     return jnp.einsum("gvp,gbp,gpc->bvc", val.reshape(nblk, nv, pts), pot, con.reshape(nblk, pts, nc), precision=HIGH)
 
@@ -400,10 +401,13 @@
         for j in singles:
             got = rc_swap(from_pair, j)
             con[1][j] = [(got, a) for a in range(ntop)]
+        x = [[t, core_swap(t)] for t in x_tops]
+        held = [con[0][j][0][0] for j in singles]
+        x, held = lax.optimization_barrier((x, held))
+        late = {j: [(held[i], index) for _, index in con[0][j]] for i, j in enumerate(singles)}
         for j in others:
-            con[0][j] = relay(con[0], j)
-
-        x = [[t, core_swap(t)] for t in x_tops]
+            late[j] = relay(late, j)
+            con[0][j] = late[j]
         if aligned:
             x = halves(x)
         else:
@@ -425,13 +429,15 @@
             for j in others:
                 con[1][j] = relay(con[1], j)
             pair_val(others)
-        groups += [
-            [(0, j) for j in others],
-            [(1, 0)] + [(1, j) for j in singles],
-            [(1, j) for j in others],
-        ]
-        groups = [group for group in groups if group]
-        dens += [density(group) for group in groups[1:]]
+        groups.append([(1, 0)] + [(1, j) for j in singles])
+        dens.append(density(groups[1]))
+        if others:
+            across = [con[0][j][a][0] for j in others for a in range(ntop)]
+            dens[1], across = ordered(dens[1], across)
+            for i, j in enumerate(others):
+                con[0][j] = [(across[i * ntop + a], con[0][j][a][1]) for a in range(ntop)]
+            groups += [[(0, j) for j in others], [(1, j) for j in others]]
+            dens += [density(group) for group in groups[2:]]
         order = [e * nchip + j for group in groups for e, j in group]
         part = route(aligned, nchip, rc, pair, order, dens)
         got = lax.all_to_all(part, ("rc", "core", "top", "pair"), 0, 0, tiled=True)
@@ -445,22 +451,25 @@
             row = row + col_swap(rows[d // 2], d)
         pots = [row] + [rc_swap(row, j) for j in range(1, nchip)]
 
-        def apply(a, k):
-            return applied(aligned, pair, pots, vals[k], cons[a], x_pairs.shape)
+        def apply(a, k, start, count):
+            return applied(aligned, pair, pots, vals[k], cons[a], start, (count, nv, nc))
+
+        def from_core(away):
+            return jnp.concatenate([core_swap(away[i:i + 1]) for i in range(away.shape[0])], axis=0)
 
         base = (eps_con[None, None, :] - eps_val[None, :, None]) * x_pairs
-        sent = None
-        for a in list(range(1, ntop)) + [0]:
-            away, step = apply(a, 1), apply(a, 0)
-            if a:
-                step, pots[0] = lax.optimization_barrier((step + core_swap(away), pots[0]))
-                piece = top_swap(step, a)
-                sent = piece if sent is None else sent + piece
-            else:
-                size = nb // 4
-                parts = [core_swap(away[i * size:(i + 1) * size]) for i in range(4)]
-                base = lax.optimization_barrier(base + step + jnp.concatenate(parts, axis=0))
-        return base if sent is None else base + sent
+        half = nb // 2
+        sent = []
+        for a in range(1, ntop):
+            pieces = []
+            for start in (0, half):
+                away, step = apply(a, 1, start, half), apply(a, 0, start, half)
+                step, pots[0] = lax.optimization_barrier((step + from_core(away), pots[0]))
+                pieces.append(top_swap(step, a))
+            sent = [s + p for s, p in zip(sent, pieces)] if sent else pieces
+        away, step = apply(0, 1, 0, nb), apply(0, 0, 0, nb)
+        base = lax.optimization_barrier(base + step + from_core(away))
+        return base + jnp.concatenate(sent, axis=0) if sent else base
 
     return per_device
 

time: 127 us -> 125 us (0.984)
  waiting for transfers between devices: 56.4 us -> 51.4 us
  starting transfers between devices: 26.5 us -> 29.7 us
  local copies, waits for them, and re-layouts: 4.05 us -> 2.68 us
    ppermute x24 -> x28, waiting for transfers between devices: 53 us -> 47.9 us  [swap(): return lax.ppermute(x, axis, [(i, i ^ mask) for i in range(size)])]
    ppermute x24 -> x28, starting transfers between devices: 22.1 us -> 26.2 us  [swap(): return lax.ppermute(x, axis, [(i, i ^ mask) for i in range(size)])]
    slice x2, local copies, waits for them, and re-layouts: 1.49 us -> 0.04 us  [pair_val(): got = pair_swap(jnp.stack([val[0][j][0][val[0][j][1]] for j in part]))]
    pallas_call x4 -> x6, Pallas kernels: 7.16 us -> 7.93 us  [applied(): pl.pallas_call(functools.partial(apply_kernel, nchip, start), out_shape=j...]
  transfers between devices with their start and end apart: 27 -> 31, of which waited for: 11 -> 12; matrix products, arithmetic and copies ran while one was open for 2% -> 1% of each run, Pallas kernels for 14% -> 14%
where the time goes in v5:
time: 125 us
  waiting for transfers between devices  51.4 us (41%)
  starting transfers between devices  29.7 us (24%)
  Pallas kernels  24.4 us (20%)
  blocking collectives  13.9 us (11%)
  local copies, waits for them, and re-layouts  2.68 us (2%)
  other arithmetic  2.23 us (2%)
    ppermute x28, waiting for transfers between devices, swap(): return lax.ppermute(x, axis, [(i, i ^ mask) for i in range(size)])  47.9 us
    ppermute x28, starting transfers between devices, swap(): return lax.ppermute(x, axis, [(i, i ^ mask) for i in range(size)])  26.2 us
    all_to_all x1, blocking collectives, per_device(): got = lax.all_to_all(part, ('rc', 'core', 'top', 'pair'), 0, 0, tiled=True)  13.9 us
    pallas_call x4, Pallas kernels, densities(): pl.pallas_call(functools.partial(density_kernel, nblk, ntop, shape, at[:n...  8.77 us
    pallas_call x6, Pallas kernels, applied(): pl.pallas_call(functools.partial(apply_kernel, nchip, start), out_shape=j...  7.93 us
    ppermute x3, waiting for transfers between devices, col_swap(): return lax.ppermute(x, ('top', 'pair'), [(i, i ^ mask) for i in range(n)])  3.54 us
    ppermute x3, starting transfers between devices, col_swap(): return lax.ppermute(x, ('top', 'pair'), [(i, i ^ mask) for i in range(n)])  3.51 us
  transfers between devices with their start and end apart: 31, of which 12 were waited for; matrix products, arithmetic and copies ran while one was open for 1% of the time, Pallas kernels for 14%

profile of v5, /device:TPU:0, one launch (start us, length us, event | category | flops | bytes accessed | tf_op | source)
XLA Modules:
  0.0 124.8 jit_solution(7234350619813238780)
XLA Ops:
  0.0 0.1 pad_add_fusion.1.where
  0.1 1.2 copy-done.1
  1.3 1.2 copy-done.2
  2.5 0.9 shard_map.64
  3.5 3.0 %collective-permute-start.4 = (f32[3,256,256]{2,1,0:T(8,128)S(1)}, f32[3,256,256]{2,1,0:T(8,128)S(1)}, u32[]{:S(2)}, u32[]{:S(2)}) collective-permute-start(f32[3,256,256]{2,1,0:T(8,128)S(1)} %get-tuple-element.77.refs_0_), channel_id=1, source_target_pairs={{0,8},{8,0},{16,24},{24,16},{1,9},{9,1},{17,25},{25,17},{2,10},{10... | collective-permute-start | bytes 2359304 | tf_op jit(solution)/shard_map/ppermute | solution.py:19
  6.5 1.5 %collective-permute-start.5 = (f32[3,256,256]{2,1,0:T(8,128)S(1)}, f32[3,256,256]{2,1,0:T(8,128)S(1)}, u32[]{:S(2)}, u32[]{:S(2)}) collective-permute-start(f32[3,256,256]{2,1,0:T(8,128)S(1)} %get-tuple-element.54), channel_id=1, source_target_pairs={{0,16},{8,24},{16,0},{24,8},{1,17},{9,25},{17,1},{25,9},{2,18},{10... | collective-permute-start | bytes 2359304 | tf_op jit(solution)/shard_map/ppermute | solution.py:19
  8.0 2.6 %collective-permute-start.1 = (f32[4,128,256]{2,1,0:T(8,128)S(1)}, f32[4,128,256]{2,1,0:T(8,128)}, u32[]{:S(2)}, u32[]{:S(2)}) collective-permute-start(f32[4,128,256]{2,1,0:T(8,128)S(1)} %copy-done), channel_id=1, source_target_pairs={{0,2},{2,0},{1,3},{3,1},{4,6},{6,4},{5,7},{7,5},{8,10},{10,8},{9,1... | collective-permute-start | bytes 1572872 | tf_op jit(solution)/shard_map/ppermute | solution.py:19
  10.6 1.6 %collective-permute-start.3 = (f32[2,256,256]{2,1,0:T(8,128)S(1)}, f32[2,256,256]{2,1,0:T(8,128)}, u32[]{:S(2)}, u32[]{:S(2)}) collective-permute-start(f32[2,256,256]{2,1,0:T(8,128)S(1)} %get-tuple-element.52), channel_id=1, source_target_pairs={{0,1},{1,0},{2,3},{3,2},{4,5},{5,4},{6,7},{7,6},{8,9},{9,8},{10,11... | collective-permute-start | bytes 1572872 | tf_op jit(solution)/shard_map/ppermute | solution.py:19
  12.2 0.5 collective-permute-start.6
  12.6 18.3 %collective-permute-done.6.refs_2_.refs_11_ = f32[1,256,256]{2,1,0:T(8,128)S(1)} collective-permute-done((f32[1,256,256]{2,1,0:T(8,128)S(1)}, f32[1,256,256]{2,1,0:T(8,128)S(1)}, u32[]{:S(2)}, u32[]{:S(2)}) %collective-permute-start.6) | collective-permute-done | bytes 262176 | tf_op jit(solution)/shard_map/ppermute | solution.py:19
  30.9 2.5 %collective-permute-done.1.refs_2_ = f32[4,128,256]{2,1,0:T(8,128)} collective-permute-done((f32[4,128,256]{2,1,0:T(8,128)S(1)}, f32[4,128,256]{2,1,0:T(8,128)}, u32[]{:S(2)}, u32[]{:S(2)}) %collective-permute-start.1) | collective-permute-done | bytes 524320 | tf_op jit(solution)/shard_map/ppermute | solution.py:19
  33.4 0.2 collective-permute-done.3.refs_0_.refs_4_
  33.7 0.9 pad_maximum_fusion
  34.6 1.4 %collective-permute-start.9 = (f32[3,256,256]{2,1,0:T(8,128)}, f32[3,256,256]{2,1,0:T(8,128)}, u32[]{:S(2)}, u32[]{:S(2)}) collective-permute-start(f32[3,256,256]{2,1,0:T(8,128)} %pad_maximum_fusion), channel_id=1, source_target_pairs={{0,1},{1,0},{2,3},{3,2},{4,5},{5,4},{6,7},{7,6},{8,9},{9,8},{10,11... | collective-permute-start | bytes 2359304 | tf_op jit(solution)/shard_map/ppermute | solution.py:19
  36.1 0.5 collective-permute-start.7
  36.6 0.5 collective-permute-start.8
  37.1 0.1 pad_add_fusion.where
  37.2 1.6 %collective-permute-start.10 = (f32[1,256,256]{2,1,0:T(8,128)S(1)}, f32[1,256,256]{2,1,0:T(8,128)S(1)}, u32[]{:S(2)}, u32[]{:S(2)}) collective-permute-start(f32[1,256,256]{2,1,0:T(8,128)S(1)} %slice.44), channel_id=1, source_target_pairs={{0,16},{8,24},{16,0},{24,8},{1,17},{9,25},{17,1},{25,9},{2,18},{10... | collective-permute-start | bytes 786440 | tf_op jit(solution)/shard_map/ppermute | solution.py:19
  38.8 1.6 %collective-permute-start.11 = (f32[1,256,256]{2,1,0:T(8,128)S(1)}, f32[1,256,256]{2,1,0:T(8,128)S(1)}, u32[]{:S(2)}, u32[]{:S(2)}) collective-permute-start(f32[1,256,256]{2,1,0:T(8,128)S(1)} %slice.45), channel_id=1, source_target_pairs={{0,8},{8,0},{16,24},{24,16},{1,9},{9,1},{17,25},{25,17},{2,10},{10... | collective-permute-start | bytes 786440 | tf_op jit(solution)/shard_map/ppermute | solution.py:19
  40.4 1.8 %shard_map.65.x_ref = bf16[1024,1024]{1,0:T(8,128)(2,1)S(1)} custom-call(f32[4,128,256]{2,1,0:T(8,128)S(1)} %copy-done, f32[4,128,256]{2,1,0:T(8,128)} %collective-permute-done.refs_1_, f32[4,128,256]{2,1,0:T(8,128)} %collective-permute-done.1.refs_2_, f32[4,128,256]{2,1,0:T(8,128)} %collective-permute-done.2.refs_3_), custom_call_target="tpu_custom_call" | custom-call | flops 2000000000 | bytes 4194304 | tf_op jit(solution)/shard_map/pallas_call | solution.py:118
  42.2 2.7 %shard_map.66.refs_0_ = f32[3,4,256]{2,1,0:T(4,128)S(1)} custom-call(s32[1]{0:T(128)} %bitcast.3.core_ref, bf16[1024,1024]{1,0:T(8,128)(2,1)S(1)} %shard_map.65.x_ref, f32[3,256,256]{2,1,0:T(8,128)S(1)} %copy-done.4, f32[3,256,256]{2,1,0:T(8,128)S(1)} %collective-permute-done.4.refs_1_, f32[3,256,256]{2,1,0:T(8,128)S(1)} %collective-permute-done.5.refs_2_, ...), custom_call_target="tpu_custom_call" | custom-call | flops 2000000000 | bytes 4194304 | tf_op jit(solution)/shard_map/pallas_call | solution.py:160
  44.9 6.2 %collective-permute-done.7.refs_1_.refs_5_ = f32[2,256,256]{2,1,0:T(8,128)S(1)} collective-permute-done((f32[2,256,256]{2,1,0:T(8,128)}, f32[2,256,256]{2,1,0:T(8,128)S(1)}, u32[]{:S(2)}, u32[]{:S(2)}) %collective-permute-start.7) | collective-permute-done | bytes 524320 | tf_op jit(solution)/shard_map/ppermute | solution.py:19
  51.1 0.5 collective-permute-done.8.refs_2_.refs_6_
  51.7 0.6 collective-permute-start.12
  52.3 1.6 %collective-permute-start.13 = (f32[1,256,256]{2,1,0:T(8,128)S(1)}, f32[1,256,256]{2,1,0:T(8,128)S(1)}, u32[]{:S(2)}, u32[]{:S(2)}) collective-permute-start(f32[1,256,256]{2,1,0:T(8,128)S(1)} %slice.47), channel_id=1, source_target_pairs={{0,8},{8,0},{16,24},{24,16},{1,9},{9,1},{17,25},{25,17},{2,10},{10... | collective-permute-start | bytes 786440 | tf_op jit(solution)/shard_map/ppermute | solution.py:19
  53.8 0.9 collective-permute-done.9.refs_3_.refs_12_
  54.7 0.5 collective-permute-start.14
  55.2 4.0 %shard_map.67.refs_1_ = f32[3,4,256]{2,1,0:T(4,128)S(1)} custom-call(s32[1]{0:T(128)} %bitcast.3.core_ref, bf16[1024,1024]{1,0:T(8,128)(2,1)S(1)} %shard_map.65.x_ref, f32[2,256,256]{2,1,0:T(8,128)} %collective-permute-done.3.refs_0_.refs_4_, f32[2,256,256]{2,1,0:T(8,128)S(1)} %collective-permute-done.7.refs_1_.refs_5_, ...), custom_call_target="tpu_custom_call" | custom-call | flops 2000000000 | bytes 4194304 | tf_op jit(solution)/shard_map/pallas_call | solution.py:160
  59.2 1.0 shard_map.68.refs_2_
  60.3 0.4 collective-permute-done.12.refs_0_.refs_7_
  60.7 1.8 %collective-permute-done.14.refs_2_.refs_13_ = f32[1,256,256]{2,1,0:T(8,128)S(1)} collective-permute-done((f32[1,256,256]{2,1,0:T(8,128)S(1)}, f32[1,256,256]{2,1,0:T(8,128)S(1)}, u32[]{:S(2)}, u32[]{:S(2)}) %collective-permute-start.14) | collective-permute-done | bytes 262176 | tf_op jit(solution)/shard_map/ppermute | solution.py:19
  62.5 1.0 shard_map.69.refs_3_
  63.5 0.6 shard_map.70
  64.1 13.9 %all_to_all.5.got_ref = f32[32,8,256]{2,1,0:T(8,128)S(1)} all-to-all(f32[32,8,256]{2,1,0:T(8,128)S(1)} %shard_map.70), channel_id=1, replica_groups=mesh['rc'=4,'core'=2,'top'=2,'pair'=2] {'rc','core','top','pair'}, dimensions={0} | all-to-all | bytes 524288 | tf_op jit(solution)/shard_map/all_to_all | solution.py:443
  78.1 2.3 %shard_map.71 = (f32[8,256]{1,0:T(8,128)S(1)}, f32[8,256]{1,0:T(8,128)S(1)}) custom-call(s32[1]{0:T(128)} %bitcast.1.top_ref, f32[32,8,256]{2,1,0:T(8,128)S(1)} %all_to_all.5.got_ref, f32[1024,2048]{1,0:T(8,128)S(1)} %bitcast.5), custom_call_target="tpu_custom_call" | custom-call | flops 2000000000 | bytes 4194304 | tf_op jit(solution)/shard_map/pallas_call | solution.py:246
  80.4 0.8 collective-permute-start.16
  81.2 2.7 %collective-permute-start.17 = (f32[8,256]{1,0:T(8,128)S(1)}, f32[8,256]{1,0:T(8,128)S(1)}, u32[]{:S(2)}, u32[]{:S(2)}) collective-permute-start(f32[8,256]{1,0:T(8,128)S(1)} %get-tuple-element.76), channel_id=1, source_target_pairs={{0,3},{1,2},{2,1},{3,0},{4,7},{5,6},{6,5},{7,4},{8,11},{9,10},{10,... | collective-permute-start | bytes 24584 | tf_op jit(solution)/shard_map/ppermute | solution.py:359
  83.9 0.1 broadcast_subtract_fusion
  84.0 3.5 %collective-permute-done.15 = f32[8,256]{1,0:T(8,128)S(1)} collective-permute-done((f32[8,256]{1,0:T(8,128)S(1)}, f32[8,256]{1,0:T(8,128)S(1)}, u32[]{:S(2)}, u32[]{:S(2)}) %collective-permute-start.15) | collective-permute-done | bytes 8224 | tf_op jit(solution)/shard_map/ppermute | solution.py:359
  87.5 0.7 collective-permute-start.18
  88.3 0.8 collective-permute-start.19
  89.0 2.1 %collective-permute-start.20 = (f32[8,256]{1,0:T(8,128)S(1)}, f32[8,256]{1,0:T(8,128)S(1)}, u32[]{:S(2)}, u32[]{:S(2)}) collective-permute-start(f32[8,256]{1,0:T(8,128)S(1)} %add_add_fusion.refs_0_), channel_id=1, source_target_pairs={{0,24},{8,16},{16,8},{24,0},{1,25},{9,17},{17,9},{25,1},{2,26},{10... | collective-permute-start | bytes 24584 | tf_op jit(solution)/shard_map/ppermute | solution.py:19
  91.1 2.2 %shard_map.72 = (bf16[6144,256]{1,0:T(8,128)(2,1)S(1)}, bf16[6144,256]{1,0:T(8,128)(2,1)S(1)}, f32[8,128,256]{2,1,0:T(8,128)S(1)}, f32[8,128,256]{2,1,0:T(8,128)S(1)}) custom-call(s32[1]{0:T(128)} %bitcast.3.core_ref, f32[3,256,256]{2,1,0:T(8,128)S(1)} %copy-done.4, f32[3,256,256]{2,1,0:T(8,128)S(1)} %collective-permute-done.4.refs_1_, ...), custom_call_target="tpu_custom_call" | custom-call | flops 2000000000 | bytes 4194304 | tf_op jit(solution)/shard_map/pallas_call | solution.py:286
  93.3 0.3 collective-permute-done.20.refs_3_
  93.6 1.1 shard_map.74
  94.7 0.1 collective-permute-start.21
  94.8 0.5 collective-permute-start.22
  95.3 1.0 shard_map.73
  96.4 1.1 shard_map.76
  97.5 0.4 collective-permute-start.23
  97.8 0.2 collective-permute-start.24
  98.0 0.5 collective-permute-start.29
  98.5 1.0 shard_map.75
  99.6 1.9 %shard_map.78 = f32[4,128,256]{2,1,0:T(8,128)S(1)} custom-call(s32[1]{0:T(128)} %bitcast.pair_ref, f32[8,256]{1,0:T(8,128)S(1)} %add_add_fusion.refs_0_, f32[8,256]{1,0:T(8,128)S(1)} %collective-permute-done.18.refs_1_, f32[8,256]{1,0:T(8,128)S(1)} %collective-permute-done.19.refs_2_, f32[8,256]{1,0:T(8,128)S(1)} %collective-permute-done.20.refs_3_, ...), custom_call_target="tpu_custom_call" | custom-call | flops 2000000000 | bytes 4194304 | tf_op jit(solution)/shard_map/pallas_call | solution.py:330
  101.6 0.1 collective-permute-start.25
  101.7 0.5 collective-permute-start.26
  102.2 0.1 collective-permute-start.27
  102.2 0.4 collective-permute-start.28
  102.7 1.8 %shard_map.77 = f32[4,128,256]{2,1,0:T(8,128)S(1)} custom-call(s32[1]{0:T(128)} %bitcast.pair_ref, f32[8,256]{1,0:T(8,128)S(1)} %add_add_fusion.refs_0_, f32[8,256]{1,0:T(8,128)S(1)} %collective-permute-done.18.refs_1_, f32[8,256]{1,0:T(8,128)S(1)} %collective-permute-done.19.refs_2_, f32[8,256]{1,0:T(8,128)S(1)} %collective-permute-done.20.refs_3_, ...), custom_call_target="tpu_custom_call" | custom-call | flops 2000000000 | bytes 4194304 | tf_op jit(solution)/shard_map/pallas_call | solution.py:330
  104.5 2.5 %collective-permute-start.30 = (f32[2,128,256]{2,1,0:T(8,128)S(1)}, f32[2,128,256]{2,1,0:T(8,128)S(1)}, u32[]{:S(2)}, u32[]{:S(2)}) collective-permute-start(f32[2,128,256]{2,1,0:T(8,128)S(1)} %maximum_add_fusion.3), channel_id=1, source_target_pairs={{0,2},{2,0},{1,3},{3,1},{4,6},{6,4},{5,7},{7,5},{8,10},{10,8},{9,1... | collective-permute-start | bytes 786440 | tf_op jit(solution)/shard_map/ppermute | solution.py:19
  107.0 0.1 maximum_add_fusion
  107.2 11.2 %collective-permute-done.29 = f32[2,128,256]{2,1,0:T(8,128)S(1)} collective-permute-done((f32[2,128,256]{2,1,0:T(8,128)S(1)}, f32[2,128,256]{2,1,0:T(8,128)S(1)}, u32[]{:S(2)}, u32[]{:S(2)}) %collective-permute-start.29) | collective-permute-done | bytes 262176 | tf_op jit(solution)/shard_map/ppermute | solution.py:19
  118.3 5.6 %collective-permute-done.30 = f32[2,128,256]{2,1,0:T(8,128)S(1)} collective-permute-done((f32[2,128,256]{2,1,0:T(8,128)S(1)}, f32[2,128,256]{2,1,0:T(8,128)S(1)}, u32[]{:S(2)}, u32[]{:S(2)}) %collective-permute-start.30) | collective-permute-done | bytes 262176 | tf_op jit(solution)/shard_map/ppermute | solution.py:19
  123.9 0.9 maximum_add_fusion.1
  (55 shorter events, 0.4 us)
Async XLA Ops:
  0.1 1.2 copy-start.1
  1.3 1.2 copy-start.2
  2.5 5.5 %copy-start = (f32[4,128,256]{2,1,0:T(8,128)S(1)}, f32[4,128,256]{2,1,0:T(8,128)}, u32[]{:S(2)}) copy-start(f32[4,128,256]{2,1,0:T(8,128)} %refs_0_) | copy-start | bytes 1572868
  3.4 32.6 %copy-start.3 = (f32[3,256,256]{2,1,0:T(8,128)}, f32[3,256,256]{2,1,0:T(8,128)S(1)}, u32[]{:S(2)}) copy-start(f32[3,256,256]{2,1,0:T(8,128)S(1)} %get-tuple-element.77.refs_0_) | copy-start | bytes 2359300
  3.5 30.2 %collective-permute-start.4 = (f32[3,256,256]{2,1,0:T(8,128)S(1)}, f32[3,256,256]{2,1,0:T(8,128)S(1)}, u32[]{:S(2)}, u32[]{:S(2)}) collective-permute-start(f32[3,256,256]{2,1,0:T(8,128)S(1)} %get-tuple-element.77.refs_0_), channel_id=1, source_target_pairs={{0,8},{8,0},{16,24},{24,16},{1,9},{9,1},{17,25},{25,17},{2,10},{10... | collective-permute-start | bytes 2359304 | tf_op jit(solution)/shard_map/ppermute | solution.py:19
  6.5 27.2 %collective-permute-start.5 = (f32[3,256,256]{2,1,0:T(8,128)S(1)}, f32[3,256,256]{2,1,0:T(8,128)S(1)}, u32[]{:S(2)}, u32[]{:S(2)}) collective-permute-start(f32[3,256,256]{2,1,0:T(8,128)S(1)} %get-tuple-element.54), channel_id=1, source_target_pairs={{0,16},{8,24},{16,0},{24,8},{1,17},{9,25},{17,1},{25,9},{2,18},{10... | collective-permute-start | bytes 2359304 | tf_op jit(solution)/shard_map/ppermute | solution.py:19
  8.0 25.4 %collective-permute-start.1 = (f32[4,128,256]{2,1,0:T(8,128)S(1)}, f32[4,128,256]{2,1,0:T(8,128)}, u32[]{:S(2)}, u32[]{:S(2)}) collective-permute-start(f32[4,128,256]{2,1,0:T(8,128)S(1)} %copy-done), channel_id=1, source_target_pairs={{0,2},{2,0},{1,3},{3,1},{4,6},{6,4},{5,7},{7,5},{8,10},{10,8},{9,1... | collective-permute-start | bytes 1572872 | tf_op jit(solution)/shard_map/ppermute | solution.py:19
  10.6 23.0 %collective-permute-start.3 = (f32[2,256,256]{2,1,0:T(8,128)S(1)}, f32[2,256,256]{2,1,0:T(8,128)}, u32[]{:S(2)}, u32[]{:S(2)}) collective-permute-start(f32[2,256,256]{2,1,0:T(8,128)S(1)} %get-tuple-element.52), channel_id=1, source_target_pairs={{0,1},{1,0},{2,3},{3,2},{4,5},{5,4},{6,7},{7,6},{8,9},{9,8},{10,11... | collective-permute-start | bytes 1572872 | tf_op jit(solution)/shard_map/ppermute | solution.py:19
  12.2 18.8 %collective-permute-start.6 = (f32[1,256,256]{2,1,0:T(8,128)S(1)}, f32[1,256,256]{2,1,0:T(8,128)S(1)}, u32[]{:S(2)}, u32[]{:S(2)}) collective-permute-start(f32[1,256,256]{2,1,0:T(8,128)S(1)} %get-tuple-element.55), channel_id=1, source_target_pairs={{0,24},{8,16},{16,8},{24,0},{1,25},{9,17},{17,9},{25,1},{2,26},{10... | collective-permute-start | bytes 786440 | tf_op jit(solution)/shard_map/ppermute | solution.py:19
  30.9 2.7 %copy-start.5 = (f32[1,256,256]{2,1,0:T(8,128)}, f32[1,256,256]{2,1,0:T(8,128)S(1)}, u32[]{:S(2)}) copy-start(f32[1,256,256]{2,1,0:T(8,128)S(1)} %collective-permute-done.6.refs_2_.refs_11_) | copy-start | bytes 786436
  30.9 6.3 %collective-permute-start = (f32[4,128,256]{2,1,0:T(8,128)S(1)}, f32[4,128,256]{2,1,0:T(8,128)}, u32[]{:S(2)}, u32[]{:S(2)}) collective-permute-start(f32[4,128,256]{2,1,0:T(8,128)S(1)} %copy-done), channel_id=1, source_target_pairs={{0,4},{4,0},{1,5},{5,1},{2,6},{6,2},{3,7},{7,3},{8,12},{12,8},{9,1... | collective-permute-start | bytes 1572872 | tf_op jit(solution)/shard_map/ppermute | solution.py:19
  33.4 3.8 %collective-permute-start.2 = (f32[4,128,256]{2,1,0:T(8,128)}, f32[4,128,256]{2,1,0:T(8,128)}, u32[]{:S(2)}, u32[]{:S(2)}) collective-permute-start(f32[4,128,256]{2,1,0:T(8,128)} %collective-permute-done.1.refs_2_), channel_id=1, source_target_pairs={{0,4},{4,0},{1,5},{5,1},{2,6},{6,2},{3,7},{7,3},{8,12},{12,8},{9,1... | collective-permute-start | bytes 1572872 | tf_op jit(solution)/shard_map/ppermute | solution.py:19
  34.6 20.1 %collective-permute-start.9 = (f32[3,256,256]{2,1,0:T(8,128)}, f32[3,256,256]{2,1,0:T(8,128)}, u32[]{:S(2)}, u32[]{:S(2)}) collective-permute-start(f32[3,256,256]{2,1,0:T(8,128)} %pad_maximum_fusion), channel_id=1, source_target_pairs={{0,1},{1,0},{2,3},{3,2},{4,5},{5,4},{6,7},{7,6},{8,9},{9,8},{10,11... | collective-permute-start | bytes 2359304 | tf_op jit(solution)/shard_map/ppermute | solution.py:19
  36.1 15.1 %collective-permute-start.7 = (f32[2,256,256]{2,1,0:T(8,128)}, f32[2,256,256]{2,1,0:T(8,128)S(1)}, u32[]{:S(2)}, u32[]{:S(2)}) collective-permute-start(f32[2,256,256]{2,1,0:T(8,128)} %collective-permute-done.3.refs_0_.refs_4_), channel_id=1, source_target_pairs={{0,8},{8,0},{16,24},{24,16},{1,9},{9,1},{17,25},{25,17},{2,10},{10... | collective-permute-start | bytes 1572872 | tf_op jit(solution)/shard_map/ppermute | solution.py:19
  36.6 15.1 %collective-permute-start.8 = (f32[2,256,256]{2,1,0:T(8,128)}, f32[2,256,256]{2,1,0:T(8,128)S(1)}, u32[]{:S(2)}, u32[]{:S(2)}) collective-permute-start(f32[2,256,256]{2,1,0:T(8,128)} %collective-permute-done.3.refs_0_.refs_4_), channel_id=1, source_target_pairs={{0,16},{8,24},{16,0},{24,8},{1,17},{9,25},{17,1},{25,9},{2,18},{10... | collective-permute-start | bytes 1572872 | tf_op jit(solution)/shard_map/ppermute | solution.py:19
  37.2 22.0 %collective-permute-start.10 = (f32[1,256,256]{2,1,0:T(8,128)S(1)}, f32[1,256,256]{2,1,0:T(8,128)S(1)}, u32[]{:S(2)}, u32[]{:S(2)}) collective-permute-start(f32[1,256,256]{2,1,0:T(8,128)S(1)} %slice.44), channel_id=1, source_target_pairs={{0,16},{8,24},{16,0},{24,8},{1,17},{9,25},{17,1},{25,9},{2,18},{10... | collective-permute-start | bytes 786440 | tf_op jit(solution)/shard_map/ppermute | solution.py:19
  38.8 3.3 %copy-start.4 = (f32[3,256,256]{2,1,0:T(8,128)S(1)}, f32[3,256,256]{2,1,0:T(8,128)}, u32[]{:S(2)}) copy-start(f32[3,256,256]{2,1,0:T(8,128)} %copy-done.3) | copy-start | bytes 2359300
  38.8 20.4 %collective-permute-start.11 = (f32[1,256,256]{2,1,0:T(8,128)S(1)}, f32[1,256,256]{2,1,0:T(8,128)S(1)}, u32[]{:S(2)}, u32[]{:S(2)}) collective-permute-start(f32[1,256,256]{2,1,0:T(8,128)S(1)} %slice.45), channel_id=1, source_target_pairs={{0,8},{8,0},{16,24},{24,16},{1,9},{9,1},{17,25},{25,17},{2,10},{10... | collective-permute-start | bytes 786440 | tf_op jit(solution)/shard_map/ppermute | solution.py:19
  42.2 12.6 %copy-start.6 = (f32[1,256,256]{2,1,0:T(8,128)S(1)}, f32[1,256,256]{2,1,0:T(8,128)}, u32[]{:S(2)}) copy-start(f32[1,256,256]{2,1,0:T(8,128)} %copy-done.5) | copy-start | bytes 786436
  51.7 9.0 %collective-permute-start.12 = (f32[1,256,256]{2,1,0:T(8,128)S(1)}, f32[1,256,256]{2,1,0:T(8,128)S(1)}, u32[]{:S(2)}, u32[]{:S(2)}) collective-permute-start(f32[1,256,256]{2,1,0:T(8,128)S(1)} %slice.46), channel_id=1, source_target_pairs={{0,16},{8,24},{16,0},{24,8},{1,17},{9,25},{17,1},{25,9},{2,18},{10... | collective-permute-start | bytes 786440 | tf_op jit(solution)/shard_map/ppermute | solution.py:19
  52.3 8.4 %collective-permute-start.13 = (f32[1,256,256]{2,1,0:T(8,128)S(1)}, f32[1,256,256]{2,1,0:T(8,128)S(1)}, u32[]{:S(2)}, u32[]{:S(2)}) collective-permute-start(f32[1,256,256]{2,1,0:T(8,128)S(1)} %slice.47), channel_id=1, source_target_pairs={{0,8},{8,0},{16,24},{24,16},{1,9},{9,1},{17,25},{25,17},{2,10},{10... | collective-permute-start | bytes 786440 | tf_op jit(solution)/shard_map/ppermute | solution.py:19
  54.7 7.7 %collective-permute-start.14 = (f32[1,256,256]{2,1,0:T(8,128)S(1)}, f32[1,256,256]{2,1,0:T(8,128)S(1)}, u32[]{:S(2)}, u32[]{:S(2)}) collective-permute-start(f32[1,256,256]{2,1,0:T(8,128)S(1)} %copy-done.6), channel_id=1, source_target_pairs={{0,1},{1,0},{2,3},{3,2},{4,5},{5,4},{6,7},{7,6},{8,9},{9,8},{10,11... | collective-permute-start | bytes 786440 | tf_op jit(solution)/shard_map/ppermute | solution.py:19
  62.5 15.6 %slice-start = ((s8[8388608]{0:T(1024)(128)(4,1)}), s8[4194304]{0:T(1024)(128)(4,1)S(1)}, s32[]{:S(2)}) async-start(s8[8388608]{0:T(1024)(128)(4,1)} %bitcast.4), calls=%async_computation.1 | async-start | bytes 8388608
  63.5 14.6 %slice-start.1 = ((s8[8388608]{0:T(1024)(128)(4,1)}), s8[4194304]{0:T(1024)(128)(4,1)S(1)}, s32[]{:S(2)}) async-start(s8[8388608]{0:T(1024)(128)(4,1)} %bitcast.4), calls=%async_computation.2 | async-start | bytes 8388608
  78.1 5.8 %copy-start.7 = (f32[256]{0:T(256)S(1)}, f32[256]{0:T(256)}, u32[]{:S(2)}) copy-start(f32[256]{0:T(256)} %param.8) | copy-start | bytes 3076
  78.1 5.8 %copy-start.8 = (f32[128]{0:T(128)S(1)}, f32[128]{0:T(128)}, u32[]{:S(2)}) copy-start(f32[128]{0:T(128)} %param.7) | copy-start | bytes 1540
  80.4 7.1 %collective-permute-start.16 = (f32[8,256]{1,0:T(8,128)S(1)}, f32[8,256]{1,0:T(8,128)S(1)}, u32[]{:S(2)}, u32[]{:S(2)}) collective-permute-start(f32[8,256]{1,0:T(8,128)S(1)} %get-tuple-element.76), channel_id=1, source_target_pairs={{0,2},{1,3},{2,0},{3,1},{4,6},{5,7},{6,4},{7,5},{8,10},{9,11},{10,... | collective-permute-start | bytes 24584 | tf_op jit(solution)/shard_map/ppermute | solution.py:359
  81.2 6.4 %collective-permute-start.17 = (f32[8,256]{1,0:T(8,128)S(1)}, f32[8,256]{1,0:T(8,128)S(1)}, u32[]{:S(2)}, u32[]{:S(2)}) collective-permute-start(f32[8,256]{1,0:T(8,128)S(1)} %get-tuple-element.76), channel_id=1, source_target_pairs={{0,3},{1,2},{2,1},{3,0},{4,7},{5,6},{6,5},{7,4},{8,11},{9,10},{10,... | collective-permute-start | bytes 24584 | tf_op jit(solution)/shard_map/ppermute | solution.py:359
  83.9 3.7 %collective-permute-start.15 = (f32[8,256]{1,0:T(8,128)S(1)}, f32[8,256]{1,0:T(8,128)S(1)}, u32[]{:S(2)}, u32[]{:S(2)}) collective-permute-start(f32[8,256]{1,0:T(8,128)S(1)} %get-tuple-element.75), channel_id=1, source_target_pairs={{0,1},{1,0},{2,3},{3,2},{4,5},{5,4},{6,7},{7,6},{8,9},{9,8},{10,11... | collective-permute-start | bytes 24584 | tf_op jit(solution)/shard_map/ppermute | solution.py:359
  87.5 5.7 %collective-permute-start.18 = (f32[8,256]{1,0:T(8,128)S(1)}, f32[8,256]{1,0:T(8,128)S(1)}, u32[]{:S(2)}, u32[]{:S(2)}) collective-permute-start(f32[8,256]{1,0:T(8,128)S(1)} %add_add_fusion.refs_0_), channel_id=1, source_target_pairs={{0,8},{8,0},{16,24},{24,16},{1,9},{9,1},{17,25},{25,17},{2,10},{10... | collective-permute-start | bytes 24584 | tf_op jit(solution)/shard_map/ppermute | solution.py:19
  88.3 5.0 %collective-permute-start.19 = (f32[8,256]{1,0:T(8,128)S(1)}, f32[8,256]{1,0:T(8,128)S(1)}, u32[]{:S(2)}, u32[]{:S(2)}) collective-permute-start(f32[8,256]{1,0:T(8,128)S(1)} %add_add_fusion.refs_0_), channel_id=1, source_target_pairs={{0,16},{8,24},{16,0},{24,8},{1,17},{9,25},{17,1},{25,9},{2,18},{10... | collective-permute-start | bytes 24584 | tf_op jit(solution)/shard_map/ppermute | solution.py:19
  89.0 4.5 %collective-permute-start.20 = (f32[8,256]{1,0:T(8,128)S(1)}, f32[8,256]{1,0:T(8,128)S(1)}, u32[]{:S(2)}, u32[]{:S(2)}) collective-permute-start(f32[8,256]{1,0:T(8,128)S(1)} %add_add_fusion.refs_0_), channel_id=1, source_target_pairs={{0,24},{8,16},{16,8},{24,0},{1,25},{9,17},{17,9},{25,1},{2,26},{10... | collective-permute-start | bytes 24584 | tf_op jit(solution)/shard_map/ppermute | solution.py:19
  94.7 1.6 %collective-permute-start.21 = (f32[1,128,256]{2,1,0:T(8,128)S(1)}, f32[1,128,256]{2,1,0:T(8,128)S(1)}, u32[]{:S(2)}, u32[]{:S(2)}) collective-permute-start(f32[1,128,256]{2,1,0:T(8,128)S(1)} %get-tuple-element.105), channel_id=1, source_target_pairs={{0,4},{4,0},{1,5},{5,1},{2,6},{6,2},{3,7},{7,3},{8,12},{12,8},{9,1... | collective-permute-start | bytes 393224 | tf_op jit(solution)/shard_map/ppermute | solution.py:19
  94.8 1.5 %collective-permute-start.22 = (f32[1,128,256]{2,1,0:T(8,128)S(1)}, f32[1,128,256]{2,1,0:T(8,128)S(1)}, u32[]{:S(2)}, u32[]{:S(2)}) collective-permute-start(f32[1,128,256]{2,1,0:T(8,128)S(1)} %get-tuple-element.106), channel_id=1, source_target_pairs={{0,4},{4,0},{1,5},{5,1},{2,6},{6,2},{3,7},{7,3},{8,12},{12,8},{9,1... | collective-permute-start | bytes 393224 | tf_op jit(solution)/shard_map/ppermute | solution.py:19
  97.5 2.1 %collective-permute-start.23 = (f32[1,128,256]{2,1,0:T(8,128)S(1)}, f32[1,128,256]{2,1,0:T(8,128)S(1)}, u32[]{:S(2)}, u32[]{:S(2)}) collective-permute-start(f32[1,128,256]{2,1,0:T(8,128)S(1)} %get-tuple-element.103), channel_id=1, source_target_pairs={{0,4},{4,0},{1,5},{5,1},{2,6},{6,2},{3,7},{7,3},{8,12},{12,8},{9,1... | collective-permute-start | bytes 393224 | tf_op jit(solution)/shard_map/ppermute | solution.py:19
  97.8 1.8 %collective-permute-start.24 = (f32[1,128,256]{2,1,0:T(8,128)S(1)}, f32[1,128,256]{2,1,0:T(8,128)S(1)}, u32[]{:S(2)}, u32[]{:S(2)}) collective-permute-start(f32[1,128,256]{2,1,0:T(8,128)S(1)} %get-tuple-element.104), channel_id=1, source_target_pairs={{0,4},{4,0},{1,5},{5,1},{2,6},{6,2},{3,7},{7,3},{8,12},{12,8},{9,1... | collective-permute-start | bytes 393224 | tf_op jit(solution)/shard_map/ppermute | solution.py:19
  98.0 20.3 %collective-permute-start.29 = (f32[2,128,256]{2,1,0:T(8,128)S(1)}, f32[2,128,256]{2,1,0:T(8,128)S(1)}, u32[]{:S(2)}, u32[]{:S(2)}) collective-permute-start(f32[2,128,256]{2,1,0:T(8,128)S(1)} %maximum_add_fusion.2), channel_id=1, source_target_pairs={{0,2},{2,0},{1,3},{3,1},{4,6},{6,4},{5,7},{7,5},{8,10},{10,8},{9,1... | collective-permute-start | bytes 786440 | tf_op jit(solution)/shard_map/ppermute | solution.py:19
  101.6 2.9 %collective-permute-start.25 = (f32[1,128,256]{2,1,0:T(8,128)S(1)}, f32[1,128,256]{2,1,0:T(8,128)S(1)}, u32[]{:S(2)}, u32[]{:S(2)}) collective-permute-start(f32[1,128,256]{2,1,0:T(8,128)S(1)} %get-tuple-element.99), channel_id=1, source_target_pairs={{0,4},{4,0},{1,5},{5,1},{2,6},{6,2},{3,7},{7,3},{8,12},{12,8},{9,1... | collective-permute-start | bytes 393224 | tf_op jit(solution)/shard_map/ppermute | solution.py:19
  101.7 5.4 %collective-permute-start.26 = (f32[1,128,256]{2,1,0:T(8,128)S(1)}, f32[1,128,256]{2,1,0:T(8,128)S(1)}, u32[]{:S(2)}, u32[]{:S(2)}) collective-permute-start(f32[1,128,256]{2,1,0:T(8,128)S(1)} %get-tuple-element.102), channel_id=1, source_target_pairs={{0,4},{4,0},{1,5},{5,1},{2,6},{6,2},{3,7},{7,3},{8,12},{12,8},{9,1... | collective-permute-start | bytes 393224 | tf_op jit(solution)/shard_map/ppermute | solution.py:19
  102.2 4.9 %collective-permute-start.27 = (f32[1,128,256]{2,1,0:T(8,128)S(1)}, f32[1,128,256]{2,1,0:T(8,128)S(1)}, u32[]{:S(2)}, u32[]{:S(2)}) collective-permute-start(f32[1,128,256]{2,1,0:T(8,128)S(1)} %get-tuple-element.101), channel_id=1, source_target_pairs={{0,4},{4,0},{1,5},{5,1},{2,6},{6,2},{3,7},{7,3},{8,12},{12,8},{9,1... | collective-permute-start | bytes 393224 | tf_op jit(solution)/shard_map/ppermute | solution.py:19
  102.2 4.8 %collective-permute-start.28 = (f32[1,128,256]{2,1,0:T(8,128)S(1)}, f32[1,128,256]{2,1,0:T(8,128)S(1)}, u32[]{:S(2)}, u32[]{:S(2)}) collective-permute-start(f32[1,128,256]{2,1,0:T(8,128)S(1)} %get-tuple-element.100), channel_id=1, source_target_pairs={{0,4},{4,0},{1,5},{5,1},{2,6},{6,2},{3,7},{7,3},{8,12},{12,8},{9,1... | collective-permute-start | bytes 393224 | tf_op jit(solution)/shard_map/ppermute | solution.py:19
  104.5 19.4 %collective-permute-start.30 = (f32[2,128,256]{2,1,0:T(8,128)S(1)}, f32[2,128,256]{2,1,0:T(8,128)S(1)}, u32[]{:S(2)}, u32[]{:S(2)}) collective-permute-start(f32[2,128,256]{2,1,0:T(8,128)S(1)} %maximum_add_fusion.3), channel_id=1, source_target_pairs={{0,2},{2,0},{1,3},{3,1},{4,6},{6,4},{5,7},{7,5},{8,10},{10,8},{9,1... | collective-permute-start | bytes 786440 | tf_op jit(solution)/shard_map/ppermute | solution.py:19

commit v6 on v5

--- a/solution.py
+++ b/solution.py
@@ -300,7 +300,7 @@
 
 
 def apply_kernel(nchip, start, pair_ref, *refs):
-    pots, (val_ref, right, out_ref, left) = refs[:nchip], refs[nchip:]
+    pots, (val_ref, right), (out_ref, left) = refs[:nchip], refs[nchip:nchip + 2], refs[-2:]
     nb, nv, nc = out_ref.shape
     pts = val_ref.shape[2]
     pair = pair_ref[0]
@@ -321,7 +321,7 @@
     out_ref[...] = total.reshape(nb, nv, nc)
 
 
-def applied(aligned, pair, pots, val, con, start, shape):
+def applied(aligned, pair, pots, val, con, start, shape, after=()):
     nb, nv, nc = shape
     nblk = val.shape[0]
     nchip = nblk // 2
@@ -330,12 +330,12 @@
         return pl.pallas_call(
             functools.partial(apply_kernel, nchip, start),
             out_shape=jax.ShapeDtypeStruct(shape, jnp.float32),
-            in_specs=[SMEM] + [VMEM] * (nchip + 2),
+            in_specs=[SMEM] + [VMEM] * (nchip + 2) + [ANY] * len(after),
             out_specs=VMEM,
             scratch_shapes=[pltpu.VMEM((nb * nv, 3 * nblk * pts), jnp.bfloat16)],
             compiler_params=PARAMS,
             cost_estimate=COST,
-        )(pair.astype(jnp.int32)[None], *pots, val, con)
+        )(pair.astype(jnp.int32)[None], *pots, val, con, *after)
     pot = relative(jnp.stack(pots).reshape(nchip, 2, -1, pts), 1, pair)[:, :, start:start + nb]
     pot = jnp.transpose(pot, (1, 0, 2, 3)).reshape(nblk, nb, pts)
     return jnp.einsum("gvp,gbp,gpc->bvc", val.reshape(nblk, nv, pts), pot, con.reshape(nblk, pts, nc), precision=HIGH)
@@ -451,8 +451,8 @@
             row = row + col_swap(rows[d // 2], d)
         pots = [row] + [rc_swap(row, j) for j in range(1, nchip)]
 
-        def apply(a, k, start, count):
-            return applied(aligned, pair, pots, vals[k], cons[a], start, (count, nv, nc))
+        def apply(a, k, start, count, after=()):
+            return applied(aligned, pair, pots, vals[k], cons[a], start, (count, nv, nc), after)
 
         def from_core(away):
             return jnp.concatenate([core_swap(away[i:i + 1]) for i in range(away.shape[0])], axis=0)
@@ -462,10 +462,12 @@
         sent = []
         for a in range(1, ntop):
             pieces = []
+            after = ()
             for start in (0, half):
-                away, step = apply(a, 1, start, half), apply(a, 0, start, half)
+                away, step = apply(a, 1, start, half, after), apply(a, 0, start, half, after)
                 step, pots[0] = lax.optimization_barrier((step + from_core(away), pots[0]))
                 pieces.append(top_swap(step, a))
+                after = (core_swap(step[0, :8, :128]),)
             sent = [s + p for s, p in zip(sent, pieces)] if sent else pieces
         away, step = apply(0, 1, 0, nb), apply(0, 0, 0, nb)
         base = lax.optimization_barrier(base + step + from_core(away))

time: 125 us -> 124 us (level)
    ppermute x28 -> x29, waiting for transfers between devices: 47.9 us -> 46.9 us  [swap(): return lax.ppermute(x, axis, [(i, i ^ mask) for i in range(size)])]
    ppermute x28 -> x29, starting transfers between devices: 26.2 us -> 25.7 us  [swap(): return lax.ppermute(x, axis, [(i, i ^ mask) for i in range(size)])]
  transfers between devices with their start and end apart: 31 -> 32, of which waited for: 12 -> 15; matrix products, arithmetic and copies ran while one was open for 1% -> 1% of each run, Pallas kernels for 14% -> 15%
where the time goes in v6:
time: 124 us
  waiting for transfers between devices  50.3 us (41%)
  starting transfers between devices  30.1 us (24%)
  Pallas kernels  24.4 us (20%)
  blocking collectives  13.9 us (11%)
  local copies, waits for them, and re-layouts  2.68 us (2%)
  other arithmetic  2.23 us (2%)
    ppermute x29, waiting for transfers between devices, swap(): return lax.ppermute(x, axis, [(i, i ^ mask) for i in range(size)])  46.9 us
    ppermute x29, starting transfers between devices, swap(): return lax.ppermute(x, axis, [(i, i ^ mask) for i in range(size)])  25.7 us
    all_to_all x1, blocking collectives, per_device(): got = lax.all_to_all(part, ('rc', 'core', 'top', 'pair'), 0, 0, tiled=True)  13.9 us
    pallas_call x4, Pallas kernels, densities(): pl.pallas_call(functools.partial(density_kernel, nblk, ntop, shape, at[:n...  8.77 us
    pallas_call x6, Pallas kernels, applied(): pl.pallas_call(functools.partial(apply_kernel, nchip, start), out_shape=j...  7.93 us
    ppermute x3, starting transfers between devices, col_swap(): return lax.ppermute(x, ('top', 'pair'), [(i, i ^ mask) for i in range(n)])  4.4 us
    ppermute x3, waiting for transfers between devices, col_swap(): return lax.ppermute(x, ('top', 'pair'), [(i, i ^ mask) for i in range(n)])  3.38 us
    unnamed x22, local copies, waits for them, and re-layouts  2.49 us
  transfers between devices with their start and end apart: 32, of which 15 were waited for; matrix products, arithmetic and copies ran while one was open for 1% of the time, Pallas kernels for 15%

profile of v6, /device:TPU:0, one launch (start us, length us, event | category | flops | bytes accessed | tf_op | source)
XLA Modules:
  0.0 124.1 jit_solution(5000256469754923243)
XLA Ops:
  0.1 1.2 copy-done.1
  1.3 1.2 copy-done.2
  2.5 0.9 shard_map.64
  3.5 3.0 %collective-permute-start.4 = (f32[3,256,256]{2,1,0:T(8,128)S(1)}, f32[3,256,256]{2,1,0:T(8,128)S(1)}, u32[]{:S(2)}, u32[]{:S(2)}) collective-permute-start(f32[3,256,256]{2,1,0:T(8,128)S(1)} %get-tuple-element.77.refs_0_), channel_id=1, source_target_pairs={{0,8},{8,0},{16,24},{24,16},{1,9},{9,1},{17,25},{25,17},{2,10},{10... | collective-permute-start | bytes 2359304 | tf_op jit(solution)/shard_map/ppermute | solution.py:19
  6.5 1.5 %collective-permute-start.5 = (f32[3,256,256]{2,1,0:T(8,128)S(1)}, f32[3,256,256]{2,1,0:T(8,128)S(1)}, u32[]{:S(2)}, u32[]{:S(2)}) collective-permute-start(f32[3,256,256]{2,1,0:T(8,128)S(1)} %get-tuple-element.54), channel_id=1, source_target_pairs={{0,16},{8,24},{16,0},{24,8},{1,17},{9,25},{17,1},{25,9},{2,18},{10... | collective-permute-start | bytes 2359304 | tf_op jit(solution)/shard_map/ppermute | solution.py:19
  8.0 2.6 %collective-permute-start.1 = (f32[4,128,256]{2,1,0:T(8,128)S(1)}, f32[4,128,256]{2,1,0:T(8,128)}, u32[]{:S(2)}, u32[]{:S(2)}) collective-permute-start(f32[4,128,256]{2,1,0:T(8,128)S(1)} %copy-done), channel_id=1, source_target_pairs={{0,2},{2,0},{1,3},{3,1},{4,6},{6,4},{5,7},{7,5},{8,10},{10,8},{9,1... | collective-permute-start | bytes 1572872 | tf_op jit(solution)/shard_map/ppermute | solution.py:19
  10.6 1.6 %collective-permute-start.3 = (f32[2,256,256]{2,1,0:T(8,128)S(1)}, f32[2,256,256]{2,1,0:T(8,128)}, u32[]{:S(2)}, u32[]{:S(2)}) collective-permute-start(f32[2,256,256]{2,1,0:T(8,128)S(1)} %get-tuple-element.52), channel_id=1, source_target_pairs={{0,1},{1,0},{2,3},{3,2},{4,5},{5,4},{6,7},{7,6},{8,9},{9,8},{10,11... | collective-permute-start | bytes 1572872 | tf_op jit(solution)/shard_map/ppermute | solution.py:19
  12.2 0.5 collective-permute-start.6
  12.6 18.3 %collective-permute-done.6.refs_2_.refs_11_ = f32[1,256,256]{2,1,0:T(8,128)S(1)} collective-permute-done((f32[1,256,256]{2,1,0:T(8,128)S(1)}, f32[1,256,256]{2,1,0:T(8,128)S(1)}, u32[]{:S(2)}, u32[]{:S(2)}) %collective-permute-start.6) | collective-permute-done | bytes 262176 | tf_op jit(solution)/shard_map/ppermute | solution.py:19
  30.9 2.5 %collective-permute-done.1.refs_2_ = f32[4,128,256]{2,1,0:T(8,128)} collective-permute-done((f32[4,128,256]{2,1,0:T(8,128)S(1)}, f32[4,128,256]{2,1,0:T(8,128)}, u32[]{:S(2)}, u32[]{:S(2)}) %collective-permute-start.1) | collective-permute-done | bytes 524320 | tf_op jit(solution)/shard_map/ppermute | solution.py:19
  33.4 0.2 collective-permute-done.3.refs_0_.refs_4_
  33.7 0.9 pad_maximum_fusion
  34.6 1.4 %collective-permute-start.9 = (f32[3,256,256]{2,1,0:T(8,128)}, f32[3,256,256]{2,1,0:T(8,128)}, u32[]{:S(2)}, u32[]{:S(2)}) collective-permute-start(f32[3,256,256]{2,1,0:T(8,128)} %pad_maximum_fusion), channel_id=1, source_target_pairs={{0,1},{1,0},{2,3},{3,2},{4,5},{5,4},{6,7},{7,6},{8,9},{9,8},{10,11... | collective-permute-start | bytes 2359304 | tf_op jit(solution)/shard_map/ppermute | solution.py:19
  36.1 0.5 collective-permute-start.7
  36.6 0.5 collective-permute-start.8
  37.2 1.6 %collective-permute-start.10 = (f32[1,256,256]{2,1,0:T(8,128)S(1)}, f32[1,256,256]{2,1,0:T(8,128)S(1)}, u32[]{:S(2)}, u32[]{:S(2)}) collective-permute-start(f32[1,256,256]{2,1,0:T(8,128)S(1)} %slice.47), channel_id=1, source_target_pairs={{0,16},{8,24},{16,0},{24,8},{1,17},{9,25},{17,1},{25,9},{2,18},{10... | collective-permute-start | bytes 786440 | tf_op jit(solution)/shard_map/ppermute | solution.py:19
  38.8 1.6 %collective-permute-start.11 = (f32[1,256,256]{2,1,0:T(8,128)S(1)}, f32[1,256,256]{2,1,0:T(8,128)S(1)}, u32[]{:S(2)}, u32[]{:S(2)}) collective-permute-start(f32[1,256,256]{2,1,0:T(8,128)S(1)} %slice.48), channel_id=1, source_target_pairs={{0,8},{8,0},{16,24},{24,16},{1,9},{9,1},{17,25},{25,17},{2,10},{10... | collective-permute-start | bytes 786440 | tf_op jit(solution)/shard_map/ppermute | solution.py:19
  40.4 1.8 %shard_map.65.x_ref = bf16[1024,1024]{1,0:T(8,128)(2,1)S(1)} custom-call(f32[4,128,256]{2,1,0:T(8,128)S(1)} %copy-done, f32[4,128,256]{2,1,0:T(8,128)} %collective-permute-done.refs_1_, f32[4,128,256]{2,1,0:T(8,128)} %collective-permute-done.1.refs_2_, f32[4,128,256]{2,1,0:T(8,128)} %collective-permute-done.2.refs_3_), custom_call_target="tpu_custom_call" | custom-call | flops 2000000000 | bytes 4194304 | tf_op jit(solution)/shard_map/pallas_call | solution.py:118
  42.2 2.7 %shard_map.66.refs_0_ = f32[3,4,256]{2,1,0:T(4,128)S(1)} custom-call(s32[1]{0:T(128)} %bitcast.3.core_ref, bf16[1024,1024]{1,0:T(8,128)(2,1)S(1)} %shard_map.65.x_ref, f32[3,256,256]{2,1,0:T(8,128)S(1)} %copy-done.4, f32[3,256,256]{2,1,0:T(8,128)S(1)} %collective-permute-done.4.refs_1_, f32[3,256,256]{2,1,0:T(8,128)S(1)} %collective-permute-done.5.refs_2_, ...), custom_call_target="tpu_custom_call" | custom-call | flops 2000000000 | bytes 4194304 | tf_op jit(solution)/shard_map/pallas_call | solution.py:160
  44.9 6.2 %collective-permute-done.7.refs_1_.refs_5_ = f32[2,256,256]{2,1,0:T(8,128)S(1)} collective-permute-done((f32[2,256,256]{2,1,0:T(8,128)}, f32[2,256,256]{2,1,0:T(8,128)S(1)}, u32[]{:S(2)}, u32[]{:S(2)}) %collective-permute-start.7) | collective-permute-done | bytes 524320 | tf_op jit(solution)/shard_map/ppermute | solution.py:19
  51.1 0.5 collective-permute-done.8.refs_2_.refs_6_
  51.7 0.6 collective-permute-start.12
  52.3 1.6 %collective-permute-start.13 = (f32[1,256,256]{2,1,0:T(8,128)S(1)}, f32[1,256,256]{2,1,0:T(8,128)S(1)}, u32[]{:S(2)}, u32[]{:S(2)}) collective-permute-start(f32[1,256,256]{2,1,0:T(8,128)S(1)} %slice.50), channel_id=1, source_target_pairs={{0,8},{8,0},{16,24},{24,16},{1,9},{9,1},{17,25},{25,17},{2,10},{10... | collective-permute-start | bytes 786440 | tf_op jit(solution)/shard_map/ppermute | solution.py:19
  53.9 0.9 collective-permute-done.9.refs_3_.refs_12_
  54.7 0.5 collective-permute-start.14
  55.2 4.0 %shard_map.67.refs_1_ = f32[3,4,256]{2,1,0:T(4,128)S(1)} custom-call(s32[1]{0:T(128)} %bitcast.3.core_ref, bf16[1024,1024]{1,0:T(8,128)(2,1)S(1)} %shard_map.65.x_ref, f32[2,256,256]{2,1,0:T(8,128)} %collective-permute-done.3.refs_0_.refs_4_, f32[2,256,256]{2,1,0:T(8,128)S(1)} %collective-permute-done.7.refs_1_.refs_5_, ...), custom_call_target="tpu_custom_call" | custom-call | flops 2000000000 | bytes 4194304 | tf_op jit(solution)/shard_map/pallas_call | solution.py:160
  59.2 1.0 shard_map.68.refs_2_
  60.3 0.4 collective-permute-done.12.refs_0_.refs_7_
  60.7 1.8 %collective-permute-done.14.refs_2_.refs_13_ = f32[1,256,256]{2,1,0:T(8,128)S(1)} collective-permute-done((f32[1,256,256]{2,1,0:T(8,128)S(1)}, f32[1,256,256]{2,1,0:T(8,128)S(1)}, u32[]{:S(2)}, u32[]{:S(2)}) %collective-permute-start.14) | collective-permute-done | bytes 262176 | tf_op jit(solution)/shard_map/ppermute | solution.py:19
  62.5 1.0 shard_map.69.refs_3_
  63.5 0.6 shard_map.70
  64.1 13.9 %all_to_all.5.got_ref = f32[32,8,256]{2,1,0:T(8,128)S(1)} all-to-all(f32[32,8,256]{2,1,0:T(8,128)S(1)} %shard_map.70), channel_id=1, replica_groups=mesh['rc'=4,'core'=2,'top'=2,'pair'=2] {'rc','core','top','pair'}, dimensions={0} | all-to-all | bytes 524288 | tf_op jit(solution)/shard_map/all_to_all | solution.py:443
  78.1 2.3 %shard_map.71 = (f32[8,256]{1,0:T(8,128)S(1)}, f32[8,256]{1,0:T(8,128)S(1)}) custom-call(s32[1]{0:T(128)} %bitcast.1.top_ref, f32[32,8,256]{2,1,0:T(8,128)S(1)} %all_to_all.5.got_ref, f32[1024,2048]{1,0:T(8,128)S(1)} %bitcast.7), custom_call_target="tpu_custom_call" | custom-call | flops 2000000000 | bytes 4194304 | tf_op jit(solution)/shard_map/pallas_call | solution.py:246
  80.4 1.1 collective-permute-start.15
  81.5 1.2 collective-permute-start.16
  82.7 2.1 %collective-permute-start.17 = (f32[8,256]{1,0:T(8,128)S(1)}, f32[8,256]{1,0:T(8,128)S(1)}, u32[]{:S(2)}, u32[]{:S(2)}) collective-permute-start(f32[8,256]{1,0:T(8,128)S(1)} %get-tuple-element.76), channel_id=1, source_target_pairs={{0,3},{1,2},{2,1},{3,0},{4,7},{5,6},{6,5},{7,4},{8,11},{9,10},{10,... | collective-permute-start | bytes 24584 | tf_op jit(solution)/shard_map/ppermute | solution.py:359
  84.8 1.3 %collective-permute-done.16 = f32[8,256]{1,0:T(8,128)S(1)} collective-permute-done((f32[8,256]{1,0:T(8,128)S(1)}, f32[8,256]{1,0:T(8,128)S(1)}, u32[]{:S(2)}, u32[]{:S(2)}) %collective-permute-start.16) | collective-permute-done | bytes 8224 | tf_op jit(solution)/shard_map/ppermute | solution.py:359
  86.0 2.1 %collective-permute-done.17 = f32[8,256]{1,0:T(8,128)S(1)} collective-permute-done((f32[8,256]{1,0:T(8,128)S(1)}, f32[8,256]{1,0:T(8,128)S(1)}, u32[]{:S(2)}, u32[]{:S(2)}) %collective-permute-start.17) | collective-permute-done | bytes 8224 | tf_op jit(solution)/shard_map/ppermute | solution.py:359
  88.2 1.2 collective-permute-start.18
  89.3 0.4 collective-permute-start.19
  89.8 1.9 %collective-permute-start.20 = (f32[8,256]{1,0:T(8,128)S(1)}, f32[8,256]{1,0:T(8,128)S(1)}, u32[]{:S(2)}, u32[]{:S(2)}) collective-permute-start(f32[8,256]{1,0:T(8,128)S(1)} %add_add_fusion.refs_0_), channel_id=1, source_target_pairs={{0,24},{8,16},{16,8},{24,0},{1,25},{9,17},{17,9},{25,1},{2,26},{10... | collective-permute-start | bytes 24584 | tf_op jit(solution)/shard_map/ppermute | solution.py:19
  91.6 2.2 %shard_map.72 = (bf16[6144,256]{1,0:T(8,128)(2,1)S(1)}, bf16[6144,256]{1,0:T(8,128)(2,1)S(1)}, f32[8,128,256]{2,1,0:T(8,128)S(1)}, f32[8,128,256]{2,1,0:T(8,128)S(1)}) custom-call(s32[1]{0:T(128)} %bitcast.3.core_ref, f32[3,256,256]{2,1,0:T(8,128)S(1)} %copy-done.4, f32[3,256,256]{2,1,0:T(8,128)S(1)} %collective-permute-done.4.refs_1_, ...), custom_call_target="tpu_custom_call" | custom-call | flops 2000000000 | bytes 4194304 | tf_op jit(solution)/shard_map/pallas_call | solution.py:286
  93.9 0.5 collective-permute-done.20.refs_3_
  94.3 1.1 shard_map.74
  95.5 0.5 collective-permute-start.22
  96.0 1.0 shard_map.73
  97.1 0.3 collective-permute-start.23
  97.6 0.7 collective-permute-done.23.refs_6_
  98.3 1.1 shard_map.76
  99.4 0.4 collective-permute-start.24
  99.8 0.2 collective-permute-start.25
  100.0 1.0 shard_map.75
  101.1 0.1 collective-permute-done.25
  101.2 1.9 %shard_map.78 = f32[4,128,256]{2,1,0:T(8,128)S(1)} custom-call(s32[1]{0:T(128)} %bitcast.pair_ref, f32[8,256]{1,0:T(8,128)S(1)} %add_add_fusion.refs_0_, f32[8,256]{1,0:T(8,128)S(1)} %collective-permute-done.18.refs_1_, f32[8,256]{1,0:T(8,128)S(1)} %collective-permute-done.19.refs_2_, f32[8,256]{1,0:T(8,128)S(1)} %collective-permute-done.20.refs_3_, ...), custom_call_target="tpu_custom_call" | custom-call | flops 2000000000 | bytes 4194304 | tf_op jit(solution)/shard_map/pallas_call | solution.py:330
  103.1 0.3 collective-permute-start.26
  103.4 0.3 collective-permute-start.27
  103.7 0.2 collective-permute-start.28
  103.9 0.3 collective-permute-start.29
  104.2 1.8 %shard_map.77 = f32[4,128,256]{2,1,0:T(8,128)S(1)} custom-call(s32[1]{0:T(128)} %bitcast.pair_ref, f32[8,256]{1,0:T(8,128)S(1)} %add_add_fusion.refs_0_, f32[8,256]{1,0:T(8,128)S(1)} %collective-permute-done.18.refs_1_, f32[8,256]{1,0:T(8,128)S(1)} %collective-permute-done.19.refs_2_, f32[8,256]{1,0:T(8,128)S(1)} %collective-permute-done.20.refs_3_, ...), custom_call_target="tpu_custom_call" | custom-call | flops 2000000000 | bytes 4194304 | tf_op jit(solution)/shard_map/pallas_call | solution.py:330
  106.1 2.2 %collective-permute-start.31 = (f32[2,128,256]{2,1,0:T(8,128)S(1)}, f32[2,128,256]{2,1,0:T(8,128)S(1)}, u32[]{:S(2)}, u32[]{:S(2)}) collective-permute-start(f32[2,128,256]{2,1,0:T(8,128)S(1)} %maximum_add_fusion.3), channel_id=1, source_target_pairs={{0,2},{2,0},{1,3},{3,1},{4,6},{6,4},{5,7},{7,5},{8,10},{10,8},{9,1... | collective-permute-start | bytes 786440 | tf_op jit(solution)/shard_map/ppermute | solution.py:19
  108.3 0.1 maximum_add_fusion
  108.4 9.2 %collective-permute-done.30 = f32[2,128,256]{2,1,0:T(8,128)S(1)} collective-permute-done((f32[2,128,256]{2,1,0:T(8,128)S(1)}, f32[2,128,256]{2,1,0:T(8,128)S(1)}, u32[]{:S(2)}, u32[]{:S(2)}) %collective-permute-start.30) | collective-permute-done | bytes 262176 | tf_op jit(solution)/shard_map/ppermute | solution.py:19
  117.6 5.6 %collective-permute-done.31 = f32[2,128,256]{2,1,0:T(8,128)S(1)} collective-permute-done((f32[2,128,256]{2,1,0:T(8,128)S(1)}, f32[2,128,256]{2,1,0:T(8,128)S(1)}, u32[]{:S(2)}, u32[]{:S(2)}) %collective-permute-start.31) | collective-permute-done | bytes 262176 | tf_op jit(solution)/shard_map/ppermute | solution.py:19
  123.2 0.9 maximum_add_fusion.1
  (58 shorter events, 0.7 us)
Async XLA Ops:
  0.1 1.2 copy-start.1
  1.3 1.2 copy-start.2
  2.5 5.5 %copy-start = (f32[4,128,256]{2,1,0:T(8,128)S(1)}, f32[4,128,256]{2,1,0:T(8,128)}, u32[]{:S(2)}) copy-start(f32[4,128,256]{2,1,0:T(8,128)} %refs_0_) | copy-start | bytes 1572868
  3.4 32.6 %copy-start.3 = (f32[3,256,256]{2,1,0:T(8,128)}, f32[3,256,256]{2,1,0:T(8,128)S(1)}, u32[]{:S(2)}) copy-start(f32[3,256,256]{2,1,0:T(8,128)S(1)} %get-tuple-element.77.refs_0_) | copy-start | bytes 2359300
  3.5 30.2 %collective-permute-start.4 = (f32[3,256,256]{2,1,0:T(8,128)S(1)}, f32[3,256,256]{2,1,0:T(8,128)S(1)}, u32[]{:S(2)}, u32[]{:S(2)}) collective-permute-start(f32[3,256,256]{2,1,0:T(8,128)S(1)} %get-tuple-element.77.refs_0_), channel_id=1, source_target_pairs={{0,8},{8,0},{16,24},{24,16},{1,9},{9,1},{17,25},{25,17},{2,10},{10... | collective-permute-start | bytes 2359304 | tf_op jit(solution)/shard_map/ppermute | solution.py:19
  6.5 27.2 %collective-permute-start.5 = (f32[3,256,256]{2,1,0:T(8,128)S(1)}, f32[3,256,256]{2,1,0:T(8,128)S(1)}, u32[]{:S(2)}, u32[]{:S(2)}) collective-permute-start(f32[3,256,256]{2,1,0:T(8,128)S(1)} %get-tuple-element.54), channel_id=1, source_target_pairs={{0,16},{8,24},{16,0},{24,8},{1,17},{9,25},{17,1},{25,9},{2,18},{10... | collective-permute-start | bytes 2359304 | tf_op jit(solution)/shard_map/ppermute | solution.py:19
  8.0 25.4 %collective-permute-start.1 = (f32[4,128,256]{2,1,0:T(8,128)S(1)}, f32[4,128,256]{2,1,0:T(8,128)}, u32[]{:S(2)}, u32[]{:S(2)}) collective-permute-start(f32[4,128,256]{2,1,0:T(8,128)S(1)} %copy-done), channel_id=1, source_target_pairs={{0,2},{2,0},{1,3},{3,1},{4,6},{6,4},{5,7},{7,5},{8,10},{10,8},{9,1... | collective-permute-start | bytes 1572872 | tf_op jit(solution)/shard_map/ppermute | solution.py:19
  10.6 23.0 %collective-permute-start.3 = (f32[2,256,256]{2,1,0:T(8,128)S(1)}, f32[2,256,256]{2,1,0:T(8,128)}, u32[]{:S(2)}, u32[]{:S(2)}) collective-permute-start(f32[2,256,256]{2,1,0:T(8,128)S(1)} %get-tuple-element.52), channel_id=1, source_target_pairs={{0,1},{1,0},{2,3},{3,2},{4,5},{5,4},{6,7},{7,6},{8,9},{9,8},{10,11... | collective-permute-start | bytes 1572872 | tf_op jit(solution)/shard_map/ppermute | solution.py:19
  12.2 18.8 %collective-permute-start.6 = (f32[1,256,256]{2,1,0:T(8,128)S(1)}, f32[1,256,256]{2,1,0:T(8,128)S(1)}, u32[]{:S(2)}, u32[]{:S(2)}) collective-permute-start(f32[1,256,256]{2,1,0:T(8,128)S(1)} %get-tuple-element.55), channel_id=1, source_target_pairs={{0,24},{8,16},{16,8},{24,0},{1,25},{9,17},{17,9},{25,1},{2,26},{10... | collective-permute-start | bytes 786440 | tf_op jit(solution)/shard_map/ppermute | solution.py:19
  30.9 2.7 %copy-start.5 = (f32[1,256,256]{2,1,0:T(8,128)}, f32[1,256,256]{2,1,0:T(8,128)S(1)}, u32[]{:S(2)}) copy-start(f32[1,256,256]{2,1,0:T(8,128)S(1)} %collective-permute-done.6.refs_2_.refs_11_) | copy-start | bytes 786436
  30.9 6.3 %collective-permute-start = (f32[4,128,256]{2,1,0:T(8,128)S(1)}, f32[4,128,256]{2,1,0:T(8,128)}, u32[]{:S(2)}, u32[]{:S(2)}) collective-permute-start(f32[4,128,256]{2,1,0:T(8,128)S(1)} %copy-done), channel_id=1, source_target_pairs={{0,4},{4,0},{1,5},{5,1},{2,6},{6,2},{3,7},{7,3},{8,12},{12,8},{9,1... | collective-permute-start | bytes 1572872 | tf_op jit(solution)/shard_map/ppermute | solution.py:19
  33.4 3.8 %collective-permute-start.2 = (f32[4,128,256]{2,1,0:T(8,128)}, f32[4,128,256]{2,1,0:T(8,128)}, u32[]{:S(2)}, u32[]{:S(2)}) collective-permute-start(f32[4,128,256]{2,1,0:T(8,128)} %collective-permute-done.1.refs_2_), channel_id=1, source_target_pairs={{0,4},{4,0},{1,5},{5,1},{2,6},{6,2},{3,7},{7,3},{8,12},{12,8},{9,1... | collective-permute-start | bytes 1572872 | tf_op jit(solution)/shard_map/ppermute | solution.py:19
  34.6 20.1 %collective-permute-start.9 = (f32[3,256,256]{2,1,0:T(8,128)}, f32[3,256,256]{2,1,0:T(8,128)}, u32[]{:S(2)}, u32[]{:S(2)}) collective-permute-start(f32[3,256,256]{2,1,0:T(8,128)} %pad_maximum_fusion), channel_id=1, source_target_pairs={{0,1},{1,0},{2,3},{3,2},{4,5},{5,4},{6,7},{7,6},{8,9},{9,8},{10,11... | collective-permute-start | bytes 2359304 | tf_op jit(solution)/shard_map/ppermute | solution.py:19
  36.1 15.1 %collective-permute-start.7 = (f32[2,256,256]{2,1,0:T(8,128)}, f32[2,256,256]{2,1,0:T(8,128)S(1)}, u32[]{:S(2)}, u32[]{:S(2)}) collective-permute-start(f32[2,256,256]{2,1,0:T(8,128)} %collective-permute-done.3.refs_0_.refs_4_), channel_id=1, source_target_pairs={{0,8},{8,0},{16,24},{24,16},{1,9},{9,1},{17,25},{25,17},{2,10},{10... | collective-permute-start | bytes 1572872 | tf_op jit(solution)/shard_map/ppermute | solution.py:19
  36.6 15.1 %collective-permute-start.8 = (f32[2,256,256]{2,1,0:T(8,128)}, f32[2,256,256]{2,1,0:T(8,128)S(1)}, u32[]{:S(2)}, u32[]{:S(2)}) collective-permute-start(f32[2,256,256]{2,1,0:T(8,128)} %collective-permute-done.3.refs_0_.refs_4_), channel_id=1, source_target_pairs={{0,16},{8,24},{16,0},{24,8},{1,17},{9,25},{17,1},{25,9},{2,18},{10... | collective-permute-start | bytes 1572872 | tf_op jit(solution)/shard_map/ppermute | solution.py:19
  37.2 22.0 %collective-permute-start.10 = (f32[1,256,256]{2,1,0:T(8,128)S(1)}, f32[1,256,256]{2,1,0:T(8,128)S(1)}, u32[]{:S(2)}, u32[]{:S(2)}) collective-permute-start(f32[1,256,256]{2,1,0:T(8,128)S(1)} %slice.47), channel_id=1, source_target_pairs={{0,16},{8,24},{16,0},{24,8},{1,17},{9,25},{17,1},{25,9},{2,18},{10... | collective-permute-start | bytes 786440 | tf_op jit(solution)/shard_map/ppermute | solution.py:19
  38.8 3.3 %copy-start.4 = (f32[3,256,256]{2,1,0:T(8,128)S(1)}, f32[3,256,256]{2,1,0:T(8,128)}, u32[]{:S(2)}) copy-start(f32[3,256,256]{2,1,0:T(8,128)} %copy-done.3) | copy-start | bytes 2359300
  38.8 20.4 %collective-permute-start.11 = (f32[1,256,256]{2,1,0:T(8,128)S(1)}, f32[1,256,256]{2,1,0:T(8,128)S(1)}, u32[]{:S(2)}, u32[]{:S(2)}) collective-permute-start(f32[1,256,256]{2,1,0:T(8,128)S(1)} %slice.48), channel_id=1, source_target_pairs={{0,8},{8,0},{16,24},{24,16},{1,9},{9,1},{17,25},{25,17},{2,10},{10... | collective-permute-start | bytes 786440 | tf_op jit(solution)/shard_map/ppermute | solution.py:19
  42.2 12.6 %copy-start.6 = (f32[1,256,256]{2,1,0:T(8,128)S(1)}, f32[1,256,256]{2,1,0:T(8,128)}, u32[]{:S(2)}) copy-start(f32[1,256,256]{2,1,0:T(8,128)} %copy-done.5) | copy-start | bytes 786436
  51.7 9.0 %collective-permute-start.12 = (f32[1,256,256]{2,1,0:T(8,128)S(1)}, f32[1,256,256]{2,1,0:T(8,128)S(1)}, u32[]{:S(2)}, u32[]{:S(2)}) collective-permute-start(f32[1,256,256]{2,1,0:T(8,128)S(1)} %slice.49), channel_id=1, source_target_pairs={{0,16},{8,24},{16,0},{24,8},{1,17},{9,25},{17,1},{25,9},{2,18},{10... | collective-permute-start | bytes 786440 | tf_op jit(solution)/shard_map/ppermute | solution.py:19
  52.3 8.4 %collective-permute-start.13 = (f32[1,256,256]{2,1,0:T(8,128)S(1)}, f32[1,256,256]{2,1,0:T(8,128)S(1)}, u32[]{:S(2)}, u32[]{:S(2)}) collective-permute-start(f32[1,256,256]{2,1,0:T(8,128)S(1)} %slice.50), channel_id=1, source_target_pairs={{0,8},{8,0},{16,24},{24,16},{1,9},{9,1},{17,25},{25,17},{2,10},{10... | collective-permute-start | bytes 786440 | tf_op jit(solution)/shard_map/ppermute | solution.py:19
  54.7 7.7 %collective-permute-start.14 = (f32[1,256,256]{2,1,0:T(8,128)S(1)}, f32[1,256,256]{2,1,0:T(8,128)S(1)}, u32[]{:S(2)}, u32[]{:S(2)}) collective-permute-start(f32[1,256,256]{2,1,0:T(8,128)S(1)} %copy-done.6), channel_id=1, source_target_pairs={{0,1},{1,0},{2,3},{3,2},{4,5},{5,4},{6,7},{7,6},{8,9},{9,8},{10,11... | collective-permute-start | bytes 786440 | tf_op jit(solution)/shard_map/ppermute | solution.py:19
  62.5 15.6 %slice-start = ((s8[8388608]{0:T(1024)(128)(4,1)}), s8[4194304]{0:T(1024)(128)(4,1)S(1)}, s32[]{:S(2)}) async-start(s8[8388608]{0:T(1024)(128)(4,1)} %bitcast.6), calls=%async_computation.1 | async-start | bytes 8388608
  63.5 14.5 %slice-start.1 = ((s8[8388608]{0:T(1024)(128)(4,1)}), s8[4194304]{0:T(1024)(128)(4,1)S(1)}, s32[]{:S(2)}) async-start(s8[8388608]{0:T(1024)(128)(4,1)} %bitcast.6), calls=%async_computation.2 | async-start | bytes 8388608
  80.4 4.4 %collective-permute-start.15 = (f32[8,256]{1,0:T(8,128)S(1)}, f32[8,256]{1,0:T(8,128)S(1)}, u32[]{:S(2)}, u32[]{:S(2)}) collective-permute-start(f32[8,256]{1,0:T(8,128)S(1)} %get-tuple-element.75), channel_id=1, source_target_pairs={{0,1},{1,0},{2,3},{3,2},{4,5},{5,4},{6,7},{7,6},{8,9},{9,8},{10,11... | collective-permute-start | bytes 24584 | tf_op jit(solution)/shard_map/ppermute | solution.py:359
  81.5 4.5 %collective-permute-start.16 = (f32[8,256]{1,0:T(8,128)S(1)}, f32[8,256]{1,0:T(8,128)S(1)}, u32[]{:S(2)}, u32[]{:S(2)}) collective-permute-start(f32[8,256]{1,0:T(8,128)S(1)} %get-tuple-element.76), channel_id=1, source_target_pairs={{0,2},{1,3},{2,0},{3,1},{4,6},{5,7},{6,4},{7,5},{8,10},{9,11},{10,... | collective-permute-start | bytes 24584 | tf_op jit(solution)/shard_map/ppermute | solution.py:359
  82.7 5.4 %collective-permute-start.17 = (f32[8,256]{1,0:T(8,128)S(1)}, f32[8,256]{1,0:T(8,128)S(1)}, u32[]{:S(2)}, u32[]{:S(2)}) collective-permute-start(f32[8,256]{1,0:T(8,128)S(1)} %get-tuple-element.76), channel_id=1, source_target_pairs={{0,3},{1,2},{2,1},{3,0},{4,7},{5,6},{6,5},{7,4},{8,11},{9,10},{10,... | collective-permute-start | bytes 24584 | tf_op jit(solution)/shard_map/ppermute | solution.py:359
  88.2 5.7 %collective-permute-start.18 = (f32[8,256]{1,0:T(8,128)S(1)}, f32[8,256]{1,0:T(8,128)S(1)}, u32[]{:S(2)}, u32[]{:S(2)}) collective-permute-start(f32[8,256]{1,0:T(8,128)S(1)} %add_add_fusion.refs_0_), channel_id=1, source_target_pairs={{0,8},{8,0},{16,24},{24,16},{1,9},{9,1},{17,25},{25,17},{2,10},{10... | collective-permute-start | bytes 24584 | tf_op jit(solution)/shard_map/ppermute | solution.py:19
  89.3 4.5 %collective-permute-start.19 = (f32[8,256]{1,0:T(8,128)S(1)}, f32[8,256]{1,0:T(8,128)S(1)}, u32[]{:S(2)}, u32[]{:S(2)}) collective-permute-start(f32[8,256]{1,0:T(8,128)S(1)} %add_add_fusion.refs_0_), channel_id=1, source_target_pairs={{0,16},{8,24},{16,0},{24,8},{1,17},{9,25},{17,1},{25,9},{2,18},{10... | collective-permute-start | bytes 24584 | tf_op jit(solution)/shard_map/ppermute | solution.py:19
  89.8 4.5 %collective-permute-start.20 = (f32[8,256]{1,0:T(8,128)S(1)}, f32[8,256]{1,0:T(8,128)S(1)}, u32[]{:S(2)}, u32[]{:S(2)}) collective-permute-start(f32[8,256]{1,0:T(8,128)S(1)} %add_add_fusion.refs_0_), channel_id=1, source_target_pairs={{0,24},{8,16},{16,8},{24,0},{1,25},{9,17},{17,9},{25,1},{2,26},{10... | collective-permute-start | bytes 24584 | tf_op jit(solution)/shard_map/ppermute | solution.py:19
  95.4 1.6 %collective-permute-start.21 = (f32[1,128,256]{2,1,0:T(8,128)S(1)}, f32[1,128,256]{2,1,0:T(8,128)S(1)}, u32[]{:S(2)}, u32[]{:S(2)}) collective-permute-start(f32[1,128,256]{2,1,0:T(8,128)S(1)} %get-tuple-element.105), channel_id=1, source_target_pairs={{0,4},{4,0},{1,5},{5,1},{2,6},{6,2},{3,7},{7,3},{8,12},{12,8},{9,1... | collective-permute-start | bytes 393224 | tf_op jit(solution)/shard_map/ppermute | solution.py:19
  95.5 1.5 %collective-permute-start.22 = (f32[1,128,256]{2,1,0:T(8,128)S(1)}, f32[1,128,256]{2,1,0:T(8,128)S(1)}, u32[]{:S(2)}, u32[]{:S(2)}) collective-permute-start(f32[1,128,256]{2,1,0:T(8,128)S(1)} %get-tuple-element.106), channel_id=1, source_target_pairs={{0,4},{4,0},{1,5},{5,1},{2,6},{6,2},{3,7},{7,3},{8,12},{12,8},{9,1... | collective-permute-start | bytes 393224 | tf_op jit(solution)/shard_map/ppermute | solution.py:19
  96.0 1.5 %copy-start.7 = (f32[256]{0:T(256)S(1)}, f32[256]{0:T(256)}, u32[]{:S(2)}) copy-start(f32[256]{0:T(256)} %param.8) | copy-start | bytes 3076
  96.0 1.5 %copy-start.8 = (f32[128]{0:T(128)S(1)}, f32[128]{0:T(128)}, u32[]{:S(2)}) copy-start(f32[128]{0:T(128)} %param.7) | copy-start | bytes 1540
  97.1 1.2 collective-permute-start.23
  97.5 20.1 %collective-permute-start.30 = (f32[2,128,256]{2,1,0:T(8,128)S(1)}, f32[2,128,256]{2,1,0:T(8,128)S(1)}, u32[]{:S(2)}, u32[]{:S(2)}) collective-permute-start(f32[2,128,256]{2,1,0:T(8,128)S(1)} %maximum_add_fusion.2), channel_id=1, source_target_pairs={{0,2},{2,0},{1,3},{3,1},{4,6},{6,4},{5,7},{7,5},{8,10},{10,8},{9,1... | collective-permute-start | bytes 786440 | tf_op jit(solution)/shard_map/ppermute | solution.py:19
  99.4 1.6 %collective-permute-start.24 = (f32[1,128,256]{2,1,0:T(8,128)S(1)}, f32[1,128,256]{2,1,0:T(8,128)S(1)}, u32[]{:S(2)}, u32[]{:S(2)}) collective-permute-start(f32[1,128,256]{2,1,0:T(8,128)S(1)} %get-tuple-element.103), channel_id=1, source_target_pairs={{0,4},{4,0},{1,5},{5,1},{2,6},{6,2},{3,7},{7,3},{8,12},{12,8},{9,1... | collective-permute-start | bytes 393224 | tf_op jit(solution)/shard_map/ppermute | solution.py:19
  99.8 1.3 %collective-permute-start.25 = (f32[1,128,256]{2,1,0:T(8,128)S(1)}, f32[1,128,256]{2,1,0:T(8,128)S(1)}, u32[]{:S(2)}, u32[]{:S(2)}) collective-permute-start(f32[1,128,256]{2,1,0:T(8,128)S(1)} %get-tuple-element.104), channel_id=1, source_target_pairs={{0,4},{4,0},{1,5},{5,1},{2,6},{6,2},{3,7},{7,3},{8,12},{12,8},{9,1... | collective-permute-start | bytes 393224 | tf_op jit(solution)/shard_map/ppermute | solution.py:19
  103.1 2.9 %collective-permute-start.26 = (f32[1,128,256]{2,1,0:T(8,128)S(1)}, f32[1,128,256]{2,1,0:T(8,128)S(1)}, u32[]{:S(2)}, u32[]{:S(2)}) collective-permute-start(f32[1,128,256]{2,1,0:T(8,128)S(1)} %get-tuple-element.99), channel_id=1, source_target_pairs={{0,4},{4,0},{1,5},{5,1},{2,6},{6,2},{3,7},{7,3},{8,12},{12,8},{9,1... | collective-permute-start | bytes 393224 | tf_op jit(solution)/shard_map/ppermute | solution.py:19
  103.4 4.9 %collective-permute-start.27 = (f32[1,128,256]{2,1,0:T(8,128)S(1)}, f32[1,128,256]{2,1,0:T(8,128)S(1)}, u32[]{:S(2)}, u32[]{:S(2)}) collective-permute-start(f32[1,128,256]{2,1,0:T(8,128)S(1)} %get-tuple-element.102), channel_id=1, source_target_pairs={{0,4},{4,0},{1,5},{5,1},{2,6},{6,2},{3,7},{7,3},{8,12},{12,8},{9,1... | collective-permute-start | bytes 393224 | tf_op jit(solution)/shard_map/ppermute | solution.py:19
  103.7 4.6 %collective-permute-start.28 = (f32[1,128,256]{2,1,0:T(8,128)S(1)}, f32[1,128,256]{2,1,0:T(8,128)S(1)}, u32[]{:S(2)}, u32[]{:S(2)}) collective-permute-start(f32[1,128,256]{2,1,0:T(8,128)S(1)} %get-tuple-element.101), channel_id=1, source_target_pairs={{0,4},{4,0},{1,5},{5,1},{2,6},{6,2},{3,7},{7,3},{8,12},{12,8},{9,1... | collective-permute-start | bytes 393224 | tf_op jit(solution)/shard_map/ppermute | solution.py:19
  103.9 4.4 %collective-permute-start.29 = (f32[1,128,256]{2,1,0:T(8,128)S(1)}, f32[1,128,256]{2,1,0:T(8,128)S(1)}, u32[]{:S(2)}, u32[]{:S(2)}) collective-permute-start(f32[1,128,256]{2,1,0:T(8,128)S(1)} %get-tuple-element.100), channel_id=1, source_target_pairs={{0,4},{4,0},{1,5},{5,1},{2,6},{6,2},{3,7},{7,3},{8,12},{12,8},{9,1... | collective-permute-start | bytes 393224 | tf_op jit(solution)/shard_map/ppermute | solution.py:19
  106.1 17.1 %collective-permute-start.31 = (f32[2,128,256]{2,1,0:T(8,128)S(1)}, f32[2,128,256]{2,1,0:T(8,128)S(1)}, u32[]{:S(2)}, u32[]{:S(2)}) collective-permute-start(f32[2,128,256]{2,1,0:T(8,128)S(1)} %maximum_add_fusion.3), channel_id=1, source_target_pairs={{0,2},{2,0},{1,3},{3,1},{4,6},{6,4},{5,7},{7,5},{8,10},{10,8},{9,1... | collective-permute-start | bytes 786440 | tf_op jit(solution)/shard_map/ppermute | solution.py:19

commit v7 on v6

--- a/solution.py
+++ b/solution.py
@@ -421,8 +421,11 @@
         groups = [[(0, 0)] + [(0, j) for j in singles]]
         dens = [density(groups[0])]
         if others:
-            arrays = [con[1][j][0][0] for j in singles] + [val[0][j][0] for j in others]
+            arrays = [con[1][j][0][0] for j in singles]
+            last = [val[0][j][0] for j in others]
+            dens[0], last = ordered(dens[0], last)
             dens[0], arrays = ordered(dens[0], arrays)
+            arrays = arrays + last
             con[1].update({j: [(arrays[i], index) for _, index in con[1][j]] for i, j in enumerate(singles)})
             for i, j in enumerate(others):
                 val[0][j] = (arrays[len(singles) + i], val[0][j][1])

time: 124 us -> 124 us (level)
  transfers between devices with their start and end apart: 32 -> 32, of which waited for: 15 -> 13; matrix products, arithmetic and copies ran while one was open for 1% -> 1% of each run, Pallas kernels for 15% -> 15%
where the time goes in v7:
time: 124 us
  waiting for transfers between devices  51.2 us (41%)
  starting transfers between devices  29.2 us (24%)
  Pallas kernels  24.5 us (20%)
  blocking collectives  13.9 us (11%)
  local copies, waits for them, and re-layouts  2.68 us (2%)
  other arithmetic  2.23 us (2%)
    ppermute x29, waiting for transfers between devices, swap(): return lax.ppermute(x, axis, [(i, i ^ mask) for i in range(size)])  47.9 us
    ppermute x29, starting transfers between devices, swap(): return lax.ppermute(x, axis, [(i, i ^ mask) for i in range(size)])  24.8 us
    all_to_all x1, blocking collectives, per_device(): got = lax.all_to_all(part, ('rc', 'core', 'top', 'pair'), 0, 0, tiled=True)  13.9 us
    pallas_call x4, Pallas kernels, densities(): pl.pallas_call(functools.partial(density_kernel, nblk, ntop, shape, at[:n...  8.78 us
    pallas_call x6, Pallas kernels, applied(): pl.pallas_call(functools.partial(apply_kernel, nchip, start), out_shape=j...  7.93 us
    ppermute x3, starting transfers between devices, col_swap(): return lax.ppermute(x, ('top', 'pair'), [(i, i ^ mask) for i in range(n)])  4.4 us
    ppermute x3, waiting for transfers between devices, col_swap(): return lax.ppermute(x, ('top', 'pair'), [(i, i ^ mask) for i in range(n)])  3.38 us
    unnamed x22, local copies, waits for them, and re-layouts  2.49 us
  transfers between devices with their start and end apart: 32, of which 13 were waited for; matrix products, arithmetic and copies ran while one was open for 1% of the time, Pallas kernels for 15%

profile of v7, /device:TPU:0, one launch (start us, length us, event | category | flops | bytes accessed | tf_op | source)
XLA Modules:
  0.0 124.1 jit_solution(11088652775209636248)
XLA Ops:
  0.0 0.1 pad_add_fusion.1.where
  0.1 1.2 copy-done.1
  1.3 1.2 copy-done.2
  2.5 0.9 shard_map.64
  3.5 3.0 %collective-permute-start.4 = (f32[3,256,256]{2,1,0:T(8,128)S(1)}, f32[3,256,256]{2,1,0:T(8,128)S(1)}, u32[]{:S(2)}, u32[]{:S(2)}) collective-permute-start(f32[3,256,256]{2,1,0:T(8,128)S(1)} %get-tuple-element.79.refs_0_), channel_id=1, source_target_pairs={{0,8},{8,0},{16,24},{24,16},{1,9},{9,1},{17,25},{25,17},{2,10},{10... | collective-permute-start | bytes 2359304 | tf_op jit(solution)/shard_map/ppermute | solution.py:19
  6.5 1.5 %collective-permute-start.5 = (f32[3,256,256]{2,1,0:T(8,128)S(1)}, f32[3,256,256]{2,1,0:T(8,128)S(1)}, u32[]{:S(2)}, u32[]{:S(2)}) collective-permute-start(f32[3,256,256]{2,1,0:T(8,128)S(1)} %get-tuple-element.55), channel_id=1, source_target_pairs={{0,16},{8,24},{16,0},{24,8},{1,17},{9,25},{17,1},{25,9},{2,18},{10... | collective-permute-start | bytes 2359304 | tf_op jit(solution)/shard_map/ppermute | solution.py:19
  8.0 2.6 %collective-permute-start.1 = (f32[4,128,256]{2,1,0:T(8,128)S(1)}, f32[4,128,256]{2,1,0:T(8,128)}, u32[]{:S(2)}, u32[]{:S(2)}) collective-permute-start(f32[4,128,256]{2,1,0:T(8,128)S(1)} %copy-done), channel_id=1, source_target_pairs={{0,2},{2,0},{1,3},{3,1},{4,6},{6,4},{5,7},{7,5},{8,10},{10,8},{9,1... | collective-permute-start | bytes 1572872 | tf_op jit(solution)/shard_map/ppermute | solution.py:19
  10.6 1.6 %collective-permute-start.3 = (f32[2,256,256]{2,1,0:T(8,128)S(1)}, f32[2,256,256]{2,1,0:T(8,128)}, u32[]{:S(2)}, u32[]{:S(2)}) collective-permute-start(f32[2,256,256]{2,1,0:T(8,128)S(1)} %get-tuple-element.53), channel_id=1, source_target_pairs={{0,1},{1,0},{2,3},{3,2},{4,5},{5,4},{6,7},{7,6},{8,9},{9,8},{10,11... | collective-permute-start | bytes 1572872 | tf_op jit(solution)/shard_map/ppermute | solution.py:19
  12.2 0.5 collective-permute-start.6
  12.6 18.3 %collective-permute-done.6.refs_2_.refs_11_ = f32[1,256,256]{2,1,0:T(8,128)S(1)} collective-permute-done((f32[1,256,256]{2,1,0:T(8,128)S(1)}, f32[1,256,256]{2,1,0:T(8,128)S(1)}, u32[]{:S(2)}, u32[]{:S(2)}) %collective-permute-start.6) | collective-permute-done | bytes 262176 | tf_op jit(solution)/shard_map/ppermute | solution.py:19
  30.9 2.5 %collective-permute-done.1.refs_2_ = f32[4,128,256]{2,1,0:T(8,128)} collective-permute-done((f32[4,128,256]{2,1,0:T(8,128)S(1)}, f32[4,128,256]{2,1,0:T(8,128)}, u32[]{:S(2)}, u32[]{:S(2)}) %collective-permute-start.1) | collective-permute-done | bytes 524320 | tf_op jit(solution)/shard_map/ppermute | solution.py:19
  33.4 0.2 collective-permute-done.3.refs_0_.refs_4_
  33.7 0.9 pad_maximum_fusion
  34.6 1.4 %collective-permute-start.9 = (f32[3,256,256]{2,1,0:T(8,128)}, f32[3,256,256]{2,1,0:T(8,128)}, u32[]{:S(2)}, u32[]{:S(2)}) collective-permute-start(f32[3,256,256]{2,1,0:T(8,128)} %pad_maximum_fusion), channel_id=1, source_target_pairs={{0,1},{1,0},{2,3},{3,2},{4,5},{5,4},{6,7},{7,6},{8,9},{9,8},{10,11... | collective-permute-start | bytes 2359304 | tf_op jit(solution)/shard_map/ppermute | solution.py:19
  36.1 0.5 collective-permute-start.7
  36.6 0.5 collective-permute-start.8
  37.1 0.1 pad_add_fusion.where
  37.2 1.6 %collective-permute-start.10 = (f32[1,256,256]{2,1,0:T(8,128)S(1)}, f32[1,256,256]{2,1,0:T(8,128)S(1)}, u32[]{:S(2)}, u32[]{:S(2)}) collective-permute-start(f32[1,256,256]{2,1,0:T(8,128)S(1)} %slice.47), channel_id=1, source_target_pairs={{0,16},{8,24},{16,0},{24,8},{1,17},{9,25},{17,1},{25,9},{2,18},{10... | collective-permute-start | bytes 786440 | tf_op jit(solution)/shard_map/ppermute | solution.py:19
  38.8 1.6 %collective-permute-start.11 = (f32[1,256,256]{2,1,0:T(8,128)S(1)}, f32[1,256,256]{2,1,0:T(8,128)S(1)}, u32[]{:S(2)}, u32[]{:S(2)}) collective-permute-start(f32[1,256,256]{2,1,0:T(8,128)S(1)} %slice.48), channel_id=1, source_target_pairs={{0,8},{8,0},{16,24},{24,16},{1,9},{9,1},{17,25},{25,17},{2,10},{10... | collective-permute-start | bytes 786440 | tf_op jit(solution)/shard_map/ppermute | solution.py:19
  40.4 1.8 %shard_map.65.x_ref = bf16[1024,1024]{1,0:T(8,128)(2,1)S(1)} custom-call(f32[4,128,256]{2,1,0:T(8,128)S(1)} %copy-done, f32[4,128,256]{2,1,0:T(8,128)} %collective-permute-done.refs_1_, f32[4,128,256]{2,1,0:T(8,128)} %collective-permute-done.1.refs_2_, f32[4,128,256]{2,1,0:T(8,128)} %collective-permute-done.2.refs_3_), custom_call_target="tpu_custom_call" | custom-call | flops 2000000000 | bytes 4194304 | tf_op jit(solution)/shard_map/pallas_call | solution.py:118
  42.2 2.7 %shard_map.66.refs_0_ = f32[3,4,256]{2,1,0:T(4,128)S(1)} custom-call(s32[1]{0:T(128)} %bitcast.3.core_ref, bf16[1024,1024]{1,0:T(8,128)(2,1)S(1)} %shard_map.65.x_ref, f32[3,256,256]{2,1,0:T(8,128)S(1)} %copy-done.4, f32[3,256,256]{2,1,0:T(8,128)S(1)} %collective-permute-done.4.refs_1_, f32[3,256,256]{2,1,0:T(8,128)S(1)} %collective-permute-done.5.refs_2_, ...), custom_call_target="tpu_custom_call" | custom-call | flops 2000000000 | bytes 4194304 | tf_op jit(solution)/shard_map/pallas_call | solution.py:160
  44.9 6.2 %collective-permute-done.7.refs_1_.refs_5_ = f32[2,256,256]{2,1,0:T(8,128)S(1)} collective-permute-done((f32[2,256,256]{2,1,0:T(8,128)}, f32[2,256,256]{2,1,0:T(8,128)S(1)}, u32[]{:S(2)}, u32[]{:S(2)}) %collective-permute-start.7) | collective-permute-done | bytes 524320 | tf_op jit(solution)/shard_map/ppermute | solution.py:19
  51.1 0.5 collective-permute-start.14
  51.7 0.6 collective-permute-start.12
  52.3 3.0 %collective-permute-done.9.refs_3_.refs_12_ = f32[3,256,256]{2,1,0:T(8,128)} collective-permute-done((f32[3,256,256]{2,1,0:T(8,128)}, f32[3,256,256]{2,1,0:T(8,128)}, u32[]{:S(2)}, u32[]{:S(2)}) %collective-permute-start.9) | collective-permute-done | bytes 786464 | tf_op jit(solution)/shard_map/ppermute | solution.py:19
  55.3 0.5 collective-permute-start.13
  55.8 4.0 %shard_map.67.refs_1_ = f32[3,4,256]{2,1,0:T(4,128)S(1)} custom-call(s32[1]{0:T(128)} %bitcast.3.core_ref, bf16[1024,1024]{1,0:T(8,128)(2,1)S(1)} %shard_map.65.x_ref, f32[2,256,256]{2,1,0:T(8,128)} %collective-permute-done.3.refs_0_.refs_4_, f32[2,256,256]{2,1,0:T(8,128)S(1)} %collective-permute-done.7.refs_1_.refs_5_, ...), custom_call_target="tpu_custom_call" | custom-call | flops 2000000000 | bytes 4194304 | tf_op jit(solution)/shard_map/pallas_call | solution.py:160
  59.9 1.0 shard_map.68.refs_2_
  60.9 1.5 %collective-permute-done.13.refs_1_.refs_9_ = f32[1,256,256]{2,1,0:T(8,128)S(1)} collective-permute-done((f32[1,256,256]{2,1,0:T(8,128)S(1)}, f32[1,256,256]{2,1,0:T(8,128)S(1)}, u32[]{:S(2)}, u32[]{:S(2)}) %collective-permute-start.13) | collective-permute-done | bytes 262176 | tf_op jit(solution)/shard_map/ppermute | solution.py:19
  62.5 1.0 shard_map.69.refs_3_
  63.5 0.6 shard_map.70
  64.1 13.9 %all_to_all.5.got_ref = f32[32,8,256]{2,1,0:T(8,128)S(1)} all-to-all(f32[32,8,256]{2,1,0:T(8,128)S(1)} %shard_map.70), channel_id=1, replica_groups=mesh['rc'=4,'core'=2,'top'=2,'pair'=2] {'rc','core','top','pair'}, dimensions={0} | all-to-all | bytes 524288 | tf_op jit(solution)/shard_map/all_to_all | solution.py:446
  78.1 2.3 %shard_map.71 = (f32[8,256]{1,0:T(8,128)S(1)}, f32[8,256]{1,0:T(8,128)S(1)}) custom-call(s32[1]{0:T(128)} %bitcast.1.top_ref, f32[32,8,256]{2,1,0:T(8,128)S(1)} %all_to_all.5.got_ref, f32[1024,2048]{1,0:T(8,128)S(1)} %bitcast.7), custom_call_target="tpu_custom_call" | custom-call | flops 2000000000 | bytes 4194304 | tf_op jit(solution)/shard_map/pallas_call | solution.py:246
  80.4 1.1 collective-permute-start.15
  81.5 1.2 collective-permute-start.16
  82.7 2.1 %collective-permute-start.17 = (f32[8,256]{1,0:T(8,128)S(1)}, f32[8,256]{1,0:T(8,128)S(1)}, u32[]{:S(2)}, u32[]{:S(2)}) collective-permute-start(f32[8,256]{1,0:T(8,128)S(1)} %get-tuple-element.78), channel_id=1, source_target_pairs={{0,3},{1,2},{2,1},{3,0},{4,7},{5,6},{6,5},{7,4},{8,11},{9,10},{10,... | collective-permute-start | bytes 24584 | tf_op jit(solution)/shard_map/ppermute | solution.py:359
  84.8 1.3 %collective-permute-done.16 = f32[8,256]{1,0:T(8,128)S(1)} collective-permute-done((f32[8,256]{1,0:T(8,128)S(1)}, f32[8,256]{1,0:T(8,128)S(1)}, u32[]{:S(2)}, u32[]{:S(2)}) %collective-permute-start.16) | collective-permute-done | bytes 8224 | tf_op jit(solution)/shard_map/ppermute | solution.py:359
  86.0 2.1 %collective-permute-done.17 = f32[8,256]{1,0:T(8,128)S(1)} collective-permute-done((f32[8,256]{1,0:T(8,128)S(1)}, f32[8,256]{1,0:T(8,128)S(1)}, u32[]{:S(2)}, u32[]{:S(2)}) %collective-permute-start.17) | collective-permute-done | bytes 8224 | tf_op jit(solution)/shard_map/ppermute | solution.py:359
  88.2 1.2 collective-permute-start.18
  89.3 0.4 collective-permute-start.19
  89.8 1.9 %collective-permute-start.20 = (f32[8,256]{1,0:T(8,128)S(1)}, f32[8,256]{1,0:T(8,128)S(1)}, u32[]{:S(2)}, u32[]{:S(2)}) collective-permute-start(f32[8,256]{1,0:T(8,128)S(1)} %add_add_fusion.refs_0_), channel_id=1, source_target_pairs={{0,24},{8,16},{16,8},{24,0},{1,25},{9,17},{17,9},{25,1},{2,26},{10... | collective-permute-start | bytes 24584 | tf_op jit(solution)/shard_map/ppermute | solution.py:19
  91.6 2.2 %shard_map.72 = (bf16[6144,256]{1,0:T(8,128)(2,1)S(1)}, bf16[6144,256]{1,0:T(8,128)(2,1)S(1)}, f32[8,128,256]{2,1,0:T(8,128)S(1)}, f32[8,128,256]{2,1,0:T(8,128)S(1)}) custom-call(s32[1]{0:T(128)} %bitcast.3.core_ref, f32[3,256,256]{2,1,0:T(8,128)S(1)} %copy-done.4, f32[3,256,256]{2,1,0:T(8,128)S(1)} %collective-permute-done.4.refs_1_, ...), custom_call_target="tpu_custom_call" | custom-call | flops 2000000000 | bytes 4194304 | tf_op jit(solution)/shard_map/pallas_call | solution.py:286
  93.9 0.5 collective-permute-done.20.refs_3_
  94.3 1.1 shard_map.74
  95.5 0.5 collective-permute-start.22
  96.0 1.0 shard_map.73
  97.1 0.3 collective-permute-start.23
  97.5 0.1 broadcast_subtract_fusion
  97.6 0.7 collective-permute-done.23.refs_6_
  98.3 1.1 shard_map.76
  99.5 0.3 collective-permute-start.24
  99.8 0.2 collective-permute-start.25
  100.0 1.0 shard_map.75
  101.2 1.9 %shard_map.78 = f32[4,128,256]{2,1,0:T(8,128)S(1)} custom-call(s32[1]{0:T(128)} %bitcast.pair_ref, f32[8,256]{1,0:T(8,128)S(1)} %add_add_fusion.refs_0_, f32[8,256]{1,0:T(8,128)S(1)} %collective-permute-done.18.refs_1_, f32[8,256]{1,0:T(8,128)S(1)} %collective-permute-done.19.refs_2_, f32[8,256]{1,0:T(8,128)S(1)} %collective-permute-done.20.refs_3_, ...), custom_call_target="tpu_custom_call" | custom-call | flops 2000000000 | bytes 4194304 | tf_op jit(solution)/shard_map/pallas_call | solution.py:330
  103.1 0.3 collective-permute-start.26
  103.4 0.3 collective-permute-start.27
  103.7 0.2 collective-permute-start.28
  103.9 0.3 collective-permute-start.29
  104.2 1.8 %shard_map.77 = f32[4,128,256]{2,1,0:T(8,128)S(1)} custom-call(s32[1]{0:T(128)} %bitcast.pair_ref, f32[8,256]{1,0:T(8,128)S(1)} %add_add_fusion.refs_0_, f32[8,256]{1,0:T(8,128)S(1)} %collective-permute-done.18.refs_1_, f32[8,256]{1,0:T(8,128)S(1)} %collective-permute-done.19.refs_2_, f32[8,256]{1,0:T(8,128)S(1)} %collective-permute-done.20.refs_3_, ...), custom_call_target="tpu_custom_call" | custom-call | flops 2000000000 | bytes 4194304 | tf_op jit(solution)/shard_map/pallas_call | solution.py:330
  106.1 2.2 %collective-permute-start.31 = (f32[2,128,256]{2,1,0:T(8,128)S(1)}, f32[2,128,256]{2,1,0:T(8,128)S(1)}, u32[]{:S(2)}, u32[]{:S(2)}) collective-permute-start(f32[2,128,256]{2,1,0:T(8,128)S(1)} %maximum_add_fusion.3), channel_id=1, source_target_pairs={{0,2},{2,0},{1,3},{3,1},{4,6},{6,4},{5,7},{7,5},{8,10},{10,8},{9,1... | collective-permute-start | bytes 786440 | tf_op jit(solution)/shard_map/ppermute | solution.py:19
  108.3 0.1 maximum_add_fusion
  108.4 9.2 %collective-permute-done.30 = f32[2,128,256]{2,1,0:T(8,128)S(1)} collective-permute-done((f32[2,128,256]{2,1,0:T(8,128)S(1)}, f32[2,128,256]{2,1,0:T(8,128)S(1)}, u32[]{:S(2)}, u32[]{:S(2)}) %collective-permute-start.30) | collective-permute-done | bytes 262176 | tf_op jit(solution)/shard_map/ppermute | solution.py:19
  117.6 5.6 %collective-permute-done.31 = f32[2,128,256]{2,1,0:T(8,128)S(1)} collective-permute-done((f32[2,128,256]{2,1,0:T(8,128)S(1)}, f32[2,128,256]{2,1,0:T(8,128)S(1)}, u32[]{:S(2)}, u32[]{:S(2)}) %collective-permute-start.31) | collective-permute-done | bytes 262176 | tf_op jit(solution)/shard_map/ppermute | solution.py:19
  123.2 0.9 maximum_add_fusion.1
  (58 shorter events, 0.6 us)
Async XLA Ops:
  0.1 1.2 copy-start.1
  1.3 1.2 copy-start.2
  2.5 5.5 %copy-start = (f32[4,128,256]{2,1,0:T(8,128)S(1)}, f32[4,128,256]{2,1,0:T(8,128)}, u32[]{:S(2)}) copy-start(f32[4,128,256]{2,1,0:T(8,128)} %refs_0_) | copy-start | bytes 1572868
  3.4 32.6 %copy-start.3 = (f32[3,256,256]{2,1,0:T(8,128)}, f32[3,256,256]{2,1,0:T(8,128)S(1)}, u32[]{:S(2)}) copy-start(f32[3,256,256]{2,1,0:T(8,128)S(1)} %get-tuple-element.79.refs_0_) | copy-start | bytes 2359300
  3.5 30.2 %collective-permute-start.4 = (f32[3,256,256]{2,1,0:T(8,128)S(1)}, f32[3,256,256]{2,1,0:T(8,128)S(1)}, u32[]{:S(2)}, u32[]{:S(2)}) collective-permute-start(f32[3,256,256]{2,1,0:T(8,128)S(1)} %get-tuple-element.79.refs_0_), channel_id=1, source_target_pairs={{0,8},{8,0},{16,24},{24,16},{1,9},{9,1},{17,25},{25,17},{2,10},{10... | collective-permute-start | bytes 2359304 | tf_op jit(solution)/shard_map/ppermute | solution.py:19
  6.5 27.2 %collective-permute-start.5 = (f32[3,256,256]{2,1,0:T(8,128)S(1)}, f32[3,256,256]{2,1,0:T(8,128)S(1)}, u32[]{:S(2)}, u32[]{:S(2)}) collective-permute-start(f32[3,256,256]{2,1,0:T(8,128)S(1)} %get-tuple-element.55), channel_id=1, source_target_pairs={{0,16},{8,24},{16,0},{24,8},{1,17},{9,25},{17,1},{25,9},{2,18},{10... | collective-permute-start | bytes 2359304 | tf_op jit(solution)/shard_map/ppermute | solution.py:19
  8.0 25.4 %collective-permute-start.1 = (f32[4,128,256]{2,1,0:T(8,128)S(1)}, f32[4,128,256]{2,1,0:T(8,128)}, u32[]{:S(2)}, u32[]{:S(2)}) collective-permute-start(f32[4,128,256]{2,1,0:T(8,128)S(1)} %copy-done), channel_id=1, source_target_pairs={{0,2},{2,0},{1,3},{3,1},{4,6},{6,4},{5,7},{7,5},{8,10},{10,8},{9,1... | collective-permute-start | bytes 1572872 | tf_op jit(solution)/shard_map/ppermute | solution.py:19
  10.6 23.0 %collective-permute-start.3 = (f32[2,256,256]{2,1,0:T(8,128)S(1)}, f32[2,256,256]{2,1,0:T(8,128)}, u32[]{:S(2)}, u32[]{:S(2)}) collective-permute-start(f32[2,256,256]{2,1,0:T(8,128)S(1)} %get-tuple-element.53), channel_id=1, source_target_pairs={{0,1},{1,0},{2,3},{3,2},{4,5},{5,4},{6,7},{7,6},{8,9},{9,8},{10,11... | collective-permute-start | bytes 1572872 | tf_op jit(solution)/shard_map/ppermute | solution.py:19
  12.2 18.8 %collective-permute-start.6 = (f32[1,256,256]{2,1,0:T(8,128)S(1)}, f32[1,256,256]{2,1,0:T(8,128)S(1)}, u32[]{:S(2)}, u32[]{:S(2)}) collective-permute-start(f32[1,256,256]{2,1,0:T(8,128)S(1)} %get-tuple-element.56), channel_id=1, source_target_pairs={{0,24},{8,16},{16,8},{24,0},{1,25},{9,17},{17,9},{25,1},{2,26},{10... | collective-permute-start | bytes 786440 | tf_op jit(solution)/shard_map/ppermute | solution.py:19
  30.9 2.7 %copy-start.5 = (f32[1,256,256]{2,1,0:T(8,128)}, f32[1,256,256]{2,1,0:T(8,128)S(1)}, u32[]{:S(2)}) copy-start(f32[1,256,256]{2,1,0:T(8,128)S(1)} %collective-permute-done.6.refs_2_.refs_11_) | copy-start | bytes 786436
  30.9 6.3 %collective-permute-start = (f32[4,128,256]{2,1,0:T(8,128)S(1)}, f32[4,128,256]{2,1,0:T(8,128)}, u32[]{:S(2)}, u32[]{:S(2)}) collective-permute-start(f32[4,128,256]{2,1,0:T(8,128)S(1)} %copy-done), channel_id=1, source_target_pairs={{0,4},{4,0},{1,5},{5,1},{2,6},{6,2},{3,7},{7,3},{8,12},{12,8},{9,1... | collective-permute-start | bytes 1572872 | tf_op jit(solution)/shard_map/ppermute | solution.py:19
  33.4 3.8 %collective-permute-start.2 = (f32[4,128,256]{2,1,0:T(8,128)}, f32[4,128,256]{2,1,0:T(8,128)}, u32[]{:S(2)}, u32[]{:S(2)}) collective-permute-start(f32[4,128,256]{2,1,0:T(8,128)} %collective-permute-done.1.refs_2_), channel_id=1, source_target_pairs={{0,4},{4,0},{1,5},{5,1},{2,6},{6,2},{3,7},{7,3},{8,12},{12,8},{9,1... | collective-permute-start | bytes 1572872 | tf_op jit(solution)/shard_map/ppermute | solution.py:19
  34.6 20.7 %collective-permute-start.9 = (f32[3,256,256]{2,1,0:T(8,128)}, f32[3,256,256]{2,1,0:T(8,128)}, u32[]{:S(2)}, u32[]{:S(2)}) collective-permute-start(f32[3,256,256]{2,1,0:T(8,128)} %pad_maximum_fusion), channel_id=1, source_target_pairs={{0,1},{1,0},{2,3},{3,2},{4,5},{5,4},{6,7},{7,6},{8,9},{9,8},{10,11... | collective-permute-start | bytes 2359304 | tf_op jit(solution)/shard_map/ppermute | solution.py:19
  36.1 15.1 %collective-permute-start.7 = (f32[2,256,256]{2,1,0:T(8,128)}, f32[2,256,256]{2,1,0:T(8,128)S(1)}, u32[]{:S(2)}, u32[]{:S(2)}) collective-permute-start(f32[2,256,256]{2,1,0:T(8,128)} %collective-permute-done.3.refs_0_.refs_4_), channel_id=1, source_target_pairs={{0,8},{8,0},{16,24},{24,16},{1,9},{9,1},{17,25},{25,17},{2,10},{10... | collective-permute-start | bytes 1572872 | tf_op jit(solution)/shard_map/ppermute | solution.py:19
  36.6 15.1 %collective-permute-start.8 = (f32[2,256,256]{2,1,0:T(8,128)}, f32[2,256,256]{2,1,0:T(8,128)S(1)}, u32[]{:S(2)}, u32[]{:S(2)}) collective-permute-start(f32[2,256,256]{2,1,0:T(8,128)} %collective-permute-done.3.refs_0_.refs_4_), channel_id=1, source_target_pairs={{0,16},{8,24},{16,0},{24,8},{1,17},{9,25},{17,1},{25,9},{2,18},{10... | collective-permute-start | bytes 1572872 | tf_op jit(solution)/shard_map/ppermute | solution.py:19
  37.2 22.6 %collective-permute-start.10 = (f32[1,256,256]{2,1,0:T(8,128)S(1)}, f32[1,256,256]{2,1,0:T(8,128)S(1)}, u32[]{:S(2)}, u32[]{:S(2)}) collective-permute-start(f32[1,256,256]{2,1,0:T(8,128)S(1)} %slice.47), channel_id=1, source_target_pairs={{0,16},{8,24},{16,0},{24,8},{1,17},{9,25},{17,1},{25,9},{2,18},{10... | collective-permute-start | bytes 786440 | tf_op jit(solution)/shard_map/ppermute | solution.py:19
  38.8 3.3 %copy-start.4 = (f32[3,256,256]{2,1,0:T(8,128)S(1)}, f32[3,256,256]{2,1,0:T(8,128)}, u32[]{:S(2)}) copy-start(f32[3,256,256]{2,1,0:T(8,128)} %copy-done.3) | copy-start | bytes 2359300
  38.8 21.0 %collective-permute-start.11 = (f32[1,256,256]{2,1,0:T(8,128)S(1)}, f32[1,256,256]{2,1,0:T(8,128)S(1)}, u32[]{:S(2)}, u32[]{:S(2)}) collective-permute-start(f32[1,256,256]{2,1,0:T(8,128)S(1)} %slice.48), channel_id=1, source_target_pairs={{0,8},{8,0},{16,24},{24,16},{1,9},{9,1},{17,25},{25,17},{2,10},{10... | collective-permute-start | bytes 786440 | tf_op jit(solution)/shard_map/ppermute | solution.py:19
  42.2 9.0 %copy-start.6 = (f32[1,256,256]{2,1,0:T(8,128)S(1)}, f32[1,256,256]{2,1,0:T(8,128)}, u32[]{:S(2)}) copy-start(f32[1,256,256]{2,1,0:T(8,128)} %copy-done.5) | copy-start | bytes 786436
  51.1 9.8 %collective-permute-start.14 = (f32[1,256,256]{2,1,0:T(8,128)S(1)}, f32[1,256,256]{2,1,0:T(8,128)S(1)}, u32[]{:S(2)}, u32[]{:S(2)}) collective-permute-start(f32[1,256,256]{2,1,0:T(8,128)S(1)} %copy-done.6), channel_id=1, source_target_pairs={{0,1},{1,0},{2,3},{3,2},{4,5},{5,4},{6,7},{7,6},{8,9},{9,8},{10,11... | collective-permute-start | bytes 786440 | tf_op jit(solution)/shard_map/ppermute | solution.py:19
  51.7 9.2 %collective-permute-start.12 = (f32[1,256,256]{2,1,0:T(8,128)S(1)}, f32[1,256,256]{2,1,0:T(8,128)S(1)}, u32[]{:S(2)}, u32[]{:S(2)}) collective-permute-start(f32[1,256,256]{2,1,0:T(8,128)S(1)} %slice.49), channel_id=1, source_target_pairs={{0,16},{8,24},{16,0},{24,8},{1,17},{9,25},{17,1},{25,9},{2,18},{10... | collective-permute-start | bytes 786440 | tf_op jit(solution)/shard_map/ppermute | solution.py:19
  55.3 7.2 %collective-permute-start.13 = (f32[1,256,256]{2,1,0:T(8,128)S(1)}, f32[1,256,256]{2,1,0:T(8,128)S(1)}, u32[]{:S(2)}, u32[]{:S(2)}) collective-permute-start(f32[1,256,256]{2,1,0:T(8,128)S(1)} %slice.50), channel_id=1, source_target_pairs={{0,8},{8,0},{16,24},{24,16},{1,9},{9,1},{17,25},{25,17},{2,10},{10... | collective-permute-start | bytes 786440 | tf_op jit(solution)/shard_map/ppermute | solution.py:19
  62.5 15.6 %slice-start = ((s8[8388608]{0:T(1024)(128)(4,1)}), s8[4194304]{0:T(1024)(128)(4,1)S(1)}, s32[]{:S(2)}) async-start(s8[8388608]{0:T(1024)(128)(4,1)} %bitcast.6), calls=%async_computation.1 | async-start | bytes 8388608
  63.5 14.5 %slice-start.1 = ((s8[8388608]{0:T(1024)(128)(4,1)}), s8[4194304]{0:T(1024)(128)(4,1)S(1)}, s32[]{:S(2)}) async-start(s8[8388608]{0:T(1024)(128)(4,1)} %bitcast.6), calls=%async_computation.2 | async-start | bytes 8388608
  80.4 4.4 %collective-permute-start.15 = (f32[8,256]{1,0:T(8,128)S(1)}, f32[8,256]{1,0:T(8,128)S(1)}, u32[]{:S(2)}, u32[]{:S(2)}) collective-permute-start(f32[8,256]{1,0:T(8,128)S(1)} %get-tuple-element.77), channel_id=1, source_target_pairs={{0,1},{1,0},{2,3},{3,2},{4,5},{5,4},{6,7},{7,6},{8,9},{9,8},{10,11... | collective-permute-start | bytes 24584 | tf_op jit(solution)/shard_map/ppermute | solution.py:359
  81.5 4.5 %collective-permute-start.16 = (f32[8,256]{1,0:T(8,128)S(1)}, f32[8,256]{1,0:T(8,128)S(1)}, u32[]{:S(2)}, u32[]{:S(2)}) collective-permute-start(f32[8,256]{1,0:T(8,128)S(1)} %get-tuple-element.78), channel_id=1, source_target_pairs={{0,2},{1,3},{2,0},{3,1},{4,6},{5,7},{6,4},{7,5},{8,10},{9,11},{10,... | collective-permute-start | bytes 24584 | tf_op jit(solution)/shard_map/ppermute | solution.py:359
  82.7 5.4 %collective-permute-start.17 = (f32[8,256]{1,0:T(8,128)S(1)}, f32[8,256]{1,0:T(8,128)S(1)}, u32[]{:S(2)}, u32[]{:S(2)}) collective-permute-start(f32[8,256]{1,0:T(8,128)S(1)} %get-tuple-element.78), channel_id=1, source_target_pairs={{0,3},{1,2},{2,1},{3,0},{4,7},{5,6},{6,5},{7,4},{8,11},{9,10},{10,... | collective-permute-start | bytes 24584 | tf_op jit(solution)/shard_map/ppermute | solution.py:359
  88.2 5.7 %collective-permute-start.18 = (f32[8,256]{1,0:T(8,128)S(1)}, f32[8,256]{1,0:T(8,128)S(1)}, u32[]{:S(2)}, u32[]{:S(2)}) collective-permute-start(f32[8,256]{1,0:T(8,128)S(1)} %add_add_fusion.refs_0_), channel_id=1, source_target_pairs={{0,8},{8,0},{16,24},{24,16},{1,9},{9,1},{17,25},{25,17},{2,10},{10... | collective-permute-start | bytes 24584 | tf_op jit(solution)/shard_map/ppermute | solution.py:19
  89.3 4.5 %collective-permute-start.19 = (f32[8,256]{1,0:T(8,128)S(1)}, f32[8,256]{1,0:T(8,128)S(1)}, u32[]{:S(2)}, u32[]{:S(2)}) collective-permute-start(f32[8,256]{1,0:T(8,128)S(1)} %add_add_fusion.refs_0_), channel_id=1, source_target_pairs={{0,16},{8,24},{16,0},{24,8},{1,17},{9,25},{17,1},{25,9},{2,18},{10... | collective-permute-start | bytes 24584 | tf_op jit(solution)/shard_map/ppermute | solution.py:19
  89.8 4.5 %collective-permute-start.20 = (f32[8,256]{1,0:T(8,128)S(1)}, f32[8,256]{1,0:T(8,128)S(1)}, u32[]{:S(2)}, u32[]{:S(2)}) collective-permute-start(f32[8,256]{1,0:T(8,128)S(1)} %add_add_fusion.refs_0_), channel_id=1, source_target_pairs={{0,24},{8,16},{16,8},{24,0},{1,25},{9,17},{17,9},{25,1},{2,26},{10... | collective-permute-start | bytes 24584 | tf_op jit(solution)/shard_map/ppermute | solution.py:19
  95.4 1.6 %collective-permute-start.21 = (f32[1,128,256]{2,1,0:T(8,128)S(1)}, f32[1,128,256]{2,1,0:T(8,128)S(1)}, u32[]{:S(2)}, u32[]{:S(2)}) collective-permute-start(f32[1,128,256]{2,1,0:T(8,128)S(1)} %get-tuple-element.107), channel_id=1, source_target_pairs={{0,4},{4,0},{1,5},{5,1},{2,6},{6,2},{3,7},{7,3},{8,12},{12,8},{9,1... | collective-permute-start | bytes 393224 | tf_op jit(solution)/shard_map/ppermute | solution.py:19
  95.5 1.6 %collective-permute-start.22 = (f32[1,128,256]{2,1,0:T(8,128)S(1)}, f32[1,128,256]{2,1,0:T(8,128)S(1)}, u32[]{:S(2)}, u32[]{:S(2)}) collective-permute-start(f32[1,128,256]{2,1,0:T(8,128)S(1)} %get-tuple-element.108), channel_id=1, source_target_pairs={{0,4},{4,0},{1,5},{5,1},{2,6},{6,2},{3,7},{7,3},{8,12},{12,8},{9,1... | collective-permute-start | bytes 393224 | tf_op jit(solution)/shard_map/ppermute | solution.py:19
  96.0 1.5 %copy-start.7 = (f32[256]{0:T(256)S(1)}, f32[256]{0:T(256)}, u32[]{:S(2)}) copy-start(f32[256]{0:T(256)} %param.8) | copy-start | bytes 3076
  96.0 1.5 %copy-start.8 = (f32[128]{0:T(128)S(1)}, f32[128]{0:T(128)}, u32[]{:S(2)}) copy-start(f32[128]{0:T(128)} %param.7) | copy-start | bytes 1540
  97.1 1.2 collective-permute-start.23
  97.6 20.1 %collective-permute-start.30 = (f32[2,128,256]{2,1,0:T(8,128)S(1)}, f32[2,128,256]{2,1,0:T(8,128)S(1)}, u32[]{:S(2)}, u32[]{:S(2)}) collective-permute-start(f32[2,128,256]{2,1,0:T(8,128)S(1)} %maximum_add_fusion.2), channel_id=1, source_target_pairs={{0,2},{2,0},{1,3},{3,1},{4,6},{6,4},{5,7},{7,5},{8,10},{10,8},{9,1... | collective-permute-start | bytes 786440 | tf_op jit(solution)/shard_map/ppermute | solution.py:19
  99.5 1.6 %collective-permute-start.24 = (f32[1,128,256]{2,1,0:T(8,128)S(1)}, f32[1,128,256]{2,1,0:T(8,128)S(1)}, u32[]{:S(2)}, u32[]{:S(2)}) collective-permute-start(f32[1,128,256]{2,1,0:T(8,128)S(1)} %get-tuple-element.105), channel_id=1, source_target_pairs={{0,4},{4,0},{1,5},{5,1},{2,6},{6,2},{3,7},{7,3},{8,12},{12,8},{9,1... | collective-permute-start | bytes 393224 | tf_op jit(solution)/shard_map/ppermute | solution.py:19
  99.8 1.3 %collective-permute-start.25 = (f32[1,128,256]{2,1,0:T(8,128)S(1)}, f32[1,128,256]{2,1,0:T(8,128)S(1)}, u32[]{:S(2)}, u32[]{:S(2)}) collective-permute-start(f32[1,128,256]{2,1,0:T(8,128)S(1)} %get-tuple-element.106), channel_id=1, source_target_pairs={{0,4},{4,0},{1,5},{5,1},{2,6},{6,2},{3,7},{7,3},{8,12},{12,8},{9,1... | collective-permute-start | bytes 393224 | tf_op jit(solution)/shard_map/ppermute | solution.py:19
  103.1 2.9 %collective-permute-start.26 = (f32[1,128,256]{2,1,0:T(8,128)S(1)}, f32[1,128,256]{2,1,0:T(8,128)S(1)}, u32[]{:S(2)}, u32[]{:S(2)}) collective-permute-start(f32[1,128,256]{2,1,0:T(8,128)S(1)} %get-tuple-element.101), channel_id=1, source_target_pairs={{0,4},{4,0},{1,5},{5,1},{2,6},{6,2},{3,7},{7,3},{8,12},{12,8},{9,1... | collective-permute-start | bytes 393224 | tf_op jit(solution)/shard_map/ppermute | solution.py:19
  103.4 4.9 %collective-permute-start.27 = (f32[1,128,256]{2,1,0:T(8,128)S(1)}, f32[1,128,256]{2,1,0:T(8,128)S(1)}, u32[]{:S(2)}, u32[]{:S(2)}) collective-permute-start(f32[1,128,256]{2,1,0:T(8,128)S(1)} %get-tuple-element.104), channel_id=1, source_target_pairs={{0,4},{4,0},{1,5},{5,1},{2,6},{6,2},{3,7},{7,3},{8,12},{12,8},{9,1... | collective-permute-start | bytes 393224 | tf_op jit(solution)/shard_map/ppermute | solution.py:19
  103.7 4.6 %collective-permute-start.28 = (f32[1,128,256]{2,1,0:T(8,128)S(1)}, f32[1,128,256]{2,1,0:T(8,128)S(1)}, u32[]{:S(2)}, u32[]{:S(2)}) collective-permute-start(f32[1,128,256]{2,1,0:T(8,128)S(1)} %get-tuple-element.103), channel_id=1, source_target_pairs={{0,4},{4,0},{1,5},{5,1},{2,6},{6,2},{3,7},{7,3},{8,12},{12,8},{9,1... | collective-permute-start | bytes 393224 | tf_op jit(solution)/shard_map/ppermute | solution.py:19
  103.9 4.4 %collective-permute-start.29 = (f32[1,128,256]{2,1,0:T(8,128)S(1)}, f32[1,128,256]{2,1,0:T(8,128)S(1)}, u32[]{:S(2)}, u32[]{:S(2)}) collective-permute-start(f32[1,128,256]{2,1,0:T(8,128)S(1)} %get-tuple-element.102), channel_id=1, source_target_pairs={{0,4},{4,0},{1,5},{5,1},{2,6},{6,2},{3,7},{7,3},{8,12},{12,8},{9,1... | collective-permute-start | bytes 393224 | tf_op jit(solution)/shard_map/ppermute | solution.py:19
  106.1 17.1 %collective-permute-start.31 = (f32[2,128,256]{2,1,0:T(8,128)S(1)}, f32[2,128,256]{2,1,0:T(8,128)S(1)}, u32[]{:S(2)}, u32[]{:S(2)}) collective-permute-start(f32[2,128,256]{2,1,0:T(8,128)S(1)} %maximum_add_fusion.3), channel_id=1, source_target_pairs={{0,2},{2,0},{1,3},{3,1},{4,6},{6,4},{5,7},{7,5},{8,10},{10,8},{9,1... | collective-permute-start | bytes 786440 | tf_op jit(solution)/shard_map/ppermute | solution.py:19
